TPU v7x, 32 devices: a whole 2x2x4 slice. The times are simulated.
32 devices in a mesh: leaf: 16 (over z, y, x), sec: 2 (over core).
Axes of the slice: x: 2, y: 2, z: 4, core: 2. Of those that a mesh axis runs over, the one named last changes fastest.
Arguments:
- leaf_inv: bfloat16 [32768, 1024], P(('leaf', 'sec')), may hold values from -0.1875 to 0.1875
- subtree_blocks: int32 [16, 2], P('leaf', 'sec'), may hold values from 1 to 8
- subtree_shift_rhs: bfloat16 [32768, 128], P(('leaf', 'sec')), may hold values from -6 to 6
- leaf_noise: bfloat16 [32768, 128], P(('leaf', 'sec')), may hold values from -6 to 6
- leaf_dev: bfloat16 [32768], P(('leaf', 'sec')), may hold values from 0.29882812 to 3
- sep_inv: bfloat16 [1024, 896], P(('leaf', 'sec')), may hold values from -0.375 to 0.375
- sep_panel: bfloat16 [1024, 896], P(('leaf', 'sec')), may hold values from -0.375 to 0.375
- sep_rhs: bfloat16 [3, 1024, 128], P(None, ('leaf', 'sec')), may hold values from -6 to 6
- sep_noise: bfloat16 [3, 1024, 128], P(None, ('leaf', 'sec')), may hold values from -6 to 6
- sep_dev: bfloat16 [3, 1024], P(None, ('leaf', 'sec')), may hold values from 0.29882812 to 3
Outputs:
- subtree_scaled_samples: bfloat16 [32768, 128], P(('leaf', 'sec'))
- sep_sample: bfloat16 [3, 1024, 128], P(None, ('leaf', 'sec'))
All inputs are finite; a program needn't handle non-finite values.
Results may differ from a plain program's by a relative error of at most 0.019.
Values may be sent and summed in bfloat16 or wider, within the bound.
No kernel may reach another device: no remote copies, remote signals or barrier semaphores. Data moves between devices by JAX's collectives and lax.ppermute only.
A program may use at most 64 MiB of HBM per device.

v0:
```python
import jax
import jax.numpy as jnp
from jax import lax
from jax.sharding import PartitionSpec as P

BLOCK = 128


def from_partner(block, axis, apart):
    count = lax.axis_size(axis)
    route = []
    for low in range(count):
        high = low | 1 << apart
        if high != low and high < count:
            route += [(low, high), (high, low)]
    return lax.ppermute(block, axis, route)


def pair_gather(block, height):
    leaf_place = lax.axis_index("leaf")
    for bit_index in range(height):
        partner = from_partner(block, "leaf", bit_index)
        upper_half = leaf_place >> bit_index & 1 == 1
        block = jnp.where(
            upper_half, jnp.concatenate([partner, block], 0), jnp.concatenate([block, partner], 0)
        )
    return block


def group_gather(piece, height):
    block = lax.all_gather(piece, "sec", axis=0, tiled=True)
    return pair_gather(block, height)


def halve_pairs(partial_sum, height):
    leaf_place = lax.axis_index("leaf")
    for bit_index in reversed(range(height)):
        half_rows = partial_sum.shape[0] // 2
        lower_rows = partial_sum[:half_rows]
        upper_rows = partial_sum[half_rows:]
        upper_half = leaf_place >> bit_index & 1 == 1
        kept = jnp.where(upper_half, upper_rows, lower_rows)
        outgoing = jnp.where(upper_half, lower_rows, upper_rows)
        partial_sum = kept + from_partner(outgoing, "leaf", bit_index)
    return partial_sum


def group_reduce(partial_sum, height):
    reduced = halve_pairs(partial_sum, height)
    return lax.psum_scatter(reduced, "sec", scatter_dimension=0, tiled=True)


def transposed_product(matrix, vector):
    return lax.dot_general(
        matrix, vector, (((0,), (0,)), ((), ())), preferred_element_type=jnp.float32
    )


def on_device(
    leaf_inv,
    subtree_blocks,
    subtree_shift_rhs,
    leaf_noise,
    leaf_dev,
    sep_inv,
    sep_panel,
    sep_rhs,
    sep_noise,
    sep_dev,
):
    subtree_row_count = leaf_inv.shape[0]
    row_count = sep_inv.shape[0]
    levels = sep_rhs.shape[0]
    sections = lax.axis_size("sec")
    active_rows = subtree_blocks[0, 0] * BLOCK
    row_positions = jnp.arange(subtree_row_count, dtype=jnp.int32)
    row_activity = (row_positions >= subtree_row_count - active_rows)[:, None]
    subtree_shifted = jnp.where(
        row_activity, subtree_shift_rhs, jnp.zeros((), subtree_shift_rhs.dtype)
    )
    forward_subtree = jnp.dot(leaf_inv, subtree_shifted, preferred_element_type=jnp.float32)
    subtree_forward_solution = jnp.where(row_activity, forward_subtree, jnp.float32(0.0)).astype(
        jnp.bfloat16
    )
    top = subtree_forward_solution[subtree_row_count - row_count :]
    solved = []
    for height in range(1, levels + 1):
        span = 2**height * sections * row_count
        offset = (2**height - 2) * sections * row_count
        children = group_gather(top, height)
        panel = sep_panel[:, offset : offset + span]
        inverse_block = sep_inv[:, offset : offset + span]
        reduced = (
            sep_rhs[height - 1].astype(jnp.float32)
            - jnp.dot(panel, children, preferred_element_type=jnp.float32)
        ).astype(jnp.bfloat16)
        whole_reduced = group_gather(reduced, height)
        result = jnp.dot(inverse_block, whole_reduced, preferred_element_type=jnp.float32).astype(
            jnp.bfloat16
        )
        solved.append(result)
        top = result
    samples = [None] * levels
    correction = None
    for height in range(levels, 0, -1):
        span = 2**height * sections * row_count
        offset = (2**height - 2) * sections * row_count
        panel = sep_panel[:, offset : offset + span]
        inverse_block = sep_inv[:, offset : offset + span]
        summed = solved[height - 1].astype(jnp.float32) + sep_noise[height - 1].astype(jnp.float32)
        if correction is not None:
            summed = summed - correction
        vector = summed.astype(jnp.bfloat16)
        backed = group_reduce(transposed_product(inverse_block, vector), height).astype(
            jnp.bfloat16
        )
        samples[height - 1] = (
            sep_dev[height - 1][:, None].astype(jnp.float32) * backed.astype(jnp.float32)
        ).astype(jnp.bfloat16)
        correction = group_reduce(transposed_product(panel, backed), height)
    leading = jnp.zeros((subtree_row_count - row_count, correction.shape[1]), jnp.float32)
    placed = jnp.concatenate([leading, correction], axis=0)
    subtree_summed = (
        subtree_forward_solution.astype(jnp.float32) + leaf_noise.astype(jnp.float32) - placed
    )
    subtree_weight = jnp.where(row_activity, subtree_summed, jnp.float32(0.0)).astype(jnp.bfloat16)
    subtree_solution = transposed_product(leaf_inv, subtree_weight)
    sample_scales = leaf_dev[:, None].astype(jnp.float32)
    subtree_scaled_samples = jnp.where(
        row_activity, sample_scales * subtree_solution, jnp.float32(0.0)
    ).astype(jnp.bfloat16)
    return (subtree_scaled_samples, jnp.stack(samples))


def solution(mesh):
    in_specs = (
        P(("leaf", "sec"), None),
        P("leaf", "sec"),
        P(("leaf", "sec"), None),
        P(("leaf", "sec"), None),
        P(("leaf", "sec")),
        P(("leaf", "sec"), None),
        P(("leaf", "sec"), None),
        P(None, ("leaf", "sec"), None),
        P(None, ("leaf", "sec"), None),
        P(None, ("leaf", "sec")),
    )
    out_specs = (P(("leaf", "sec"), None), P(None, ("leaf", "sec"), None))
    return jax.shard_map(
        on_device, mesh=mesh, in_specs=in_specs, out_specs=out_specs, check_vma=False
    )
```

profile of v0, /device:TPU:0, one launch (start us, length us, event | category | flops | bytes accessed | tf_op | source)
XLA Modules:
  0.0 197.3 jit_solution(12825677317004949414)
XLA Ops:
  10.2 2.0 all_gather.18
  12.1 2.8 %collective-permute-start = (bf16[64,128]{1,0:T(8,128)(2,1)S(1)}, bf16[64,128]{1,0:T(8,128)(2,1)S(1)}, u32[]{:S(2)}, u32[]{:S(2)}) collective-permute-start(bf16[64,128]{1,0:T(8,128)(2,1)S(1)} %all_gather.18), channel_id=1, source_target_pairs={{0,2},{2,0},{4,6},{6,4},{8,10},{10,8},{12,14},{14,12},{16,18},{18,... | collective-permute-start | bytes 49160 | tf_op jit(solution)/shard_map/ppermute | solution.py:16
  16.8 1.8 all_gather.19
  18.6 2.1 %collective-permute-start.1 = (bf16[64,128]{1,0:T(8,128)(2,1)S(1)}, bf16[64,128]{1,0:T(8,128)(2,1)S(1)}, u32[]{:S(2)}, u32[]{:S(2)}) collective-permute-start(bf16[64,128]{1,0:T(8,128)(2,1)S(1)} %all_gather.19), channel_id=1, source_target_pairs={{0,2},{2,0},{4,6},{6,4},{8,10},{10,8},{12,14},{14,12},{16,18},{18,... | collective-permute-start | bytes 49160 | tf_op jit(solution)/shard_map/ppermute | solution.py:16
  22.5 1.8 all_gather.20
  24.3 2.1 %collective-permute-start.2 = (bf16[64,128]{1,0:T(8,128)(2,1)S(1)}, bf16[64,128]{1,0:T(8,128)(2,1)S(1)}, u32[]{:S(2)}, u32[]{:S(2)}) collective-permute-start(bf16[64,128]{1,0:T(8,128)(2,1)S(1)} %all_gather.20), channel_id=1, source_target_pairs={{0,2},{2,0},{4,6},{6,4},{8,10},{10,8},{12,14},{14,12},{16,18},{18,... | collective-permute-start | bytes 49160 | tf_op jit(solution)/shard_map/ppermute | solution.py:16
  28.1 2.1 %collective-permute-start.3 = (bf16[128,128]{1,0:T(8,128)(2,1)S(1)}, bf16[128,128]{1,0:T(8,128)(2,1)S(1)}, u32[]{:S(2)}, u32[]{:S(2)}) collective-permute-start(bf16[128,128]{1,0:T(8,128)(2,1)S(1)} %maximum_select_fusion.15), channel_id=1, source_target_pairs={{0,4},{4,0},{2,6},{6,2},{8,12},{12,8},{10,14},{14,10},{16,20},{20,... | collective-permute-start | bytes 98312 | tf_op jit(solution)/shard_map/ppermute | solution.py:16
  30.3 1.9 collective-permute-done.3
  32.3 1.8 all_gather.21
  34.1 2.0 %collective-permute-start.4 = (bf16[64,128]{1,0:T(8,128)(2,1)S(1)}, bf16[64,128]{1,0:T(8,128)(2,1)S(1)}, u32[]{:S(2)}, u32[]{:S(2)}) collective-permute-start(bf16[64,128]{1,0:T(8,128)(2,1)S(1)} %all_gather.21), channel_id=1, source_target_pairs={{0,2},{2,0},{4,6},{6,4},{8,10},{10,8},{12,14},{14,12},{16,18},{18,... | collective-permute-start | bytes 49160 | tf_op jit(solution)/shard_map/ppermute | solution.py:16
  37.9 2.1 %collective-permute-start.5 = (bf16[128,128]{1,0:T(8,128)(2,1)S(1)}, bf16[128,128]{1,0:T(8,128)(2,1)S(1)}, u32[]{:S(2)}, u32[]{:S(2)}) collective-permute-start(bf16[128,128]{1,0:T(8,128)(2,1)S(1)} %maximum_select_fusion.16), channel_id=1, source_target_pairs={{0,4},{4,0},{2,6},{6,2},{8,12},{12,8},{10,14},{14,10},{16,20},{20,... | collective-permute-start | bytes 98312 | tf_op jit(solution)/shard_map/ppermute | solution.py:16
  40.0 1.9 collective-permute-done.5
  42.0 1.8 all_gather.22
  43.8 2.0 %collective-permute-start.6 = (bf16[64,128]{1,0:T(8,128)(2,1)S(1)}, bf16[64,128]{1,0:T(8,128)(2,1)S(1)}, u32[]{:S(2)}, u32[]{:S(2)}) collective-permute-start(bf16[64,128]{1,0:T(8,128)(2,1)S(1)} %all_gather.22), channel_id=1, source_target_pairs={{0,2},{2,0},{4,6},{6,4},{8,10},{10,8},{12,14},{14,12},{16,18},{18,... | collective-permute-start | bytes 49160 | tf_op jit(solution)/shard_map/ppermute | solution.py:16
  47.6 2.1 %collective-permute-start.7 = (bf16[128,128]{1,0:T(8,128)(2,1)S(1)}, bf16[128,128]{1,0:T(8,128)(2,1)S(1)}, u32[]{:S(2)}, u32[]{:S(2)}) collective-permute-start(bf16[128,128]{1,0:T(8,128)(2,1)S(1)} %maximum_select_fusion.17), channel_id=1, source_target_pairs={{0,4},{4,0},{2,6},{6,2},{8,12},{12,8},{10,14},{14,10},{16,20},{20,... | collective-permute-start | bytes 98312 | tf_op jit(solution)/shard_map/ppermute | solution.py:16
  49.7 1.9 collective-permute-done.7
  51.6 2.1 %collective-permute-start.8 = (bf16[256,128]{1,0:T(8,128)(2,1)S(1)}, bf16[256,128]{1,0:T(8,128)(2,1)S(1)}, u32[]{:S(2)}, u32[]{:S(2)}) collective-permute-start(bf16[256,128]{1,0:T(8,128)(2,1)S(1)} %maximum_select_fusion.9), channel_id=1, source_target_pairs={{0,8},{8,0},{2,10},{10,2},{4,12},{12,4},{6,14},{14,6},{16,24},{24,... | collective-permute-start | bytes 196616 | tf_op jit(solution)/shard_map/ppermute | solution.py:16
  53.7 2.2 %collective-permute-done.8 = bf16[256,128]{1,0:T(8,128)(2,1)S(1)} collective-permute-done((bf16[256,128]{1,0:T(8,128)(2,1)S(1)}, bf16[256,128]{1,0:T(8,128)(2,1)S(1)}, u32[]{:S(2)}, u32[]{:S(2)}) %collective-permute-start.8) | collective-permute-done | bytes 65568 | tf_op jit(solution)/shard_map/ppermute | solution.py:16
  56.1 1.8 all_gather.23
  57.9 2.0 %collective-permute-start.9 = (bf16[64,128]{1,0:T(8,128)(2,1)S(1)}, bf16[64,128]{1,0:T(8,128)(2,1)S(1)}, u32[]{:S(2)}, u32[]{:S(2)}) collective-permute-start(bf16[64,128]{1,0:T(8,128)(2,1)S(1)} %all_gather.23), channel_id=1, source_target_pairs={{0,2},{2,0},{4,6},{6,4},{8,10},{10,8},{12,14},{14,12},{16,18},{18,... | collective-permute-start | bytes 49160 | tf_op jit(solution)/shard_map/ppermute | solution.py:16
  59.9 1.8 collective-permute-done.9
  61.7 2.0 %collective-permute-start.10 = (bf16[128,128]{1,0:T(8,128)(2,1)S(1)}, bf16[128,128]{1,0:T(8,128)(2,1)S(1)}, u32[]{:S(2)}, u32[]{:S(2)}) collective-permute-start(bf16[128,128]{1,0:T(8,128)(2,1)S(1)} %maximum_select_fusion.18), channel_id=1, source_target_pairs={{0,4},{4,0},{2,6},{6,2},{8,12},{12,8},{10,14},{14,10},{16,20},{20,... | collective-permute-start | bytes 98312 | tf_op jit(solution)/shard_map/ppermute | solution.py:16
  63.8 1.9 collective-permute-done.10
  65.7 2.1 %collective-permute-start.11 = (bf16[256,128]{1,0:T(8,128)(2,1)S(1)}, bf16[256,128]{1,0:T(8,128)(2,1)S(1)}, u32[]{:S(2)}, u32[]{:S(2)}) collective-permute-start(bf16[256,128]{1,0:T(8,128)(2,1)S(1)} %maximum_select_fusion.10), channel_id=1, source_target_pairs={{0,8},{8,0},{2,10},{10,2},{4,12},{12,4},{6,14},{14,6},{16,24},{24,... | collective-permute-start | bytes 196616 | tf_op jit(solution)/shard_map/ppermute | solution.py:16
  67.8 2.2 %collective-permute-done.11 = bf16[256,128]{1,0:T(8,128)(2,1)S(1)} collective-permute-done((bf16[256,128]{1,0:T(8,128)(2,1)S(1)}, bf16[256,128]{1,0:T(8,128)(2,1)S(1)}, u32[]{:S(2)}, u32[]{:S(2)}) %collective-permute-start.11) | collective-permute-done | bytes 65568 | tf_op jit(solution)/shard_map/ppermute | solution.py:16
  70.4 2.4 %collective-permute-start.12 = (f32[256,128]{0,1:T(8,128)S(1)}, f32[256,128]{0,1:T(8,128)S(1)}, u32[]{:S(2)}, u32[]{:S(2)}) collective-permute-start(f32[256,128]{0,1:T(8,128)S(1)} %slice_select_fusion.1), channel_id=1, source_target_pairs={{0,8},{8,0},{2,10},{10,2},{4,12},{12,4},{6,14},{14,6},{16,24},{24,... | collective-permute-start | bytes 393224 | tf_op jit(solution)/shard_map/ppermute | solution.py:16
  72.9 2.9 %collective-permute-done.12 = f32[256,128]{0,1:T(8,128)S(1)} collective-permute-done((f32[256,128]{0,1:T(8,128)S(1)}, f32[256,128]{0,1:T(8,128)S(1)}, u32[]{:S(2)}, u32[]{:S(2)}) %collective-permute-start.12) | collective-permute-done | bytes 131104 | tf_op jit(solution)/shard_map/ppermute | solution.py:16
  75.9 2.0 %collective-permute-start.13 = (f32[128,128]{0,1:T(8,128)S(1)}, f32[128,128]{0,1:T(8,128)S(1)}, u32[]{:S(2)}, u32[]{:S(2)}) collective-permute-start(f32[128,128]{0,1:T(8,128)S(1)} %slice_select_fusion.11), channel_id=1, source_target_pairs={{0,4},{4,0},{2,6},{6,2},{8,12},{12,8},{10,14},{14,10},{16,20},{20,... | collective-permute-start | bytes 196616 | tf_op jit(solution)/shard_map/ppermute | solution.py:16
  77.9 2.3 %collective-permute-done.13 = f32[128,128]{0,1:T(8,128)S(1)} collective-permute-done((f32[128,128]{0,1:T(8,128)S(1)}, f32[128,128]{0,1:T(8,128)S(1)}, u32[]{:S(2)}, u32[]{:S(2)}) %collective-permute-start.13) | collective-permute-done | bytes 65568 | tf_op jit(solution)/shard_map/ppermute | solution.py:16
  80.3 2.0 %collective-permute-start.14 = (f32[64,128]{0,1:T(8,128)S(1)}, f32[64,128]{0,1:T(8,128)S(1)}, u32[]{:S(2)}, u32[]{:S(2)}) collective-permute-start(f32[64,128]{0,1:T(8,128)S(1)} %slice_select_fusion.10), channel_id=1, source_target_pairs={{0,2},{2,0},{4,6},{6,4},{8,10},{10,8},{12,14},{14,12},{16,18},{18,... | collective-permute-start | bytes 98312 | tf_op jit(solution)/shard_map/ppermute | solution.py:16
  82.3 2.3 %collective-permute-done.14 = f32[64,128]{0,1:T(8,128)S(1)} collective-permute-done((f32[64,128]{0,1:T(8,128)S(1)}, f32[64,128]{0,1:T(8,128)S(1)}, u32[]{:S(2)}, u32[]{:S(2)}) %collective-permute-start.14) | collective-permute-done | bytes 32800 | tf_op jit(solution)/shard_map/ppermute | solution.py:16
  85.5 9.2 %reduce-scatter.19.cloned.1.call-done = f32[32,128]{1,0:T(8,128)} async-done(((f32[64,128]{1,0:T(8,128)}), f32[32,128]{1,0:T(8,128)}) %reduce-scatter.19.cloned.1.call-update) | async-done | bytes 16400
  95.8 1.8 collective-permute-start.15
  97.6 4.0 %collective-permute-done.15 = f32[256,128]{0,1:T(8,128)S(1)} collective-permute-done((f32[256,128]{0,1:T(8,128)S(1)}, f32[256,128]{0,1:T(8,128)S(1)}, u32[]{:S(2)}, u32[]{:S(2)}) %collective-permute-start.15) | collective-permute-done | bytes 131104 | tf_op jit(solution)/shard_map/ppermute | solution.py:16
  103.4 2.5 %collective-permute-done.16 = f32[128,128]{0,1:T(8,128)S(1)} collective-permute-done((f32[128,128]{0,1:T(8,128)S(1)}, f32[128,128]{0,1:T(8,128)S(1)}, u32[]{:S(2)}, u32[]{:S(2)}) %collective-permute-start.16) | collective-permute-done | bytes 65568 | tf_op jit(solution)/shard_map/ppermute | solution.py:16
  107.8 2.5 %collective-permute-done.17 = f32[64,128]{0,1:T(8,128)S(1)} collective-permute-done((f32[64,128]{0,1:T(8,128)S(1)}, f32[64,128]{0,1:T(8,128)S(1)}, u32[]{:S(2)}, u32[]{:S(2)}) %collective-permute-start.17) | collective-permute-done | bytes 32800 | tf_op jit(solution)/shard_map/ppermute | solution.py:16
  111.2 8.7 %reduce-scatter.21.cloned.1.call-done = f32[32,128]{1,0:T(8,128)} async-done(((f32[64,128]{1,0:T(8,128)}), f32[32,128]{1,0:T(8,128)}) %reduce-scatter.21.cloned.1.call-update) | async-done | bytes 16400 | tf_op jit(solution)/shard_map/reduce_scatter | solution.py:50
  122.6 2.6 %collective-permute-done.18 = f32[128,128]{0,1:T(8,128)S(1)} collective-permute-done((f32[128,128]{0,1:T(8,128)S(1)}, f32[128,128]{0,1:T(8,128)S(1)}, u32[]{:S(2)}, u32[]{:S(2)}) %collective-permute-start.18) | collective-permute-done | bytes 65568 | tf_op jit(solution)/shard_map/ppermute | solution.py:16
  127.1 2.5 %collective-permute-done.19 = f32[64,128]{0,1:T(8,128)S(1)} collective-permute-done((f32[64,128]{0,1:T(8,128)S(1)}, f32[64,128]{0,1:T(8,128)S(1)}, u32[]{:S(2)}, u32[]{:S(2)}) %collective-permute-start.19) | collective-permute-done | bytes 32800 | tf_op jit(solution)/shard_map/ppermute | solution.py:16
  130.5 8.7 %reduce-scatter.23.cloned.1.call-done = f32[32,128]{1,0:T(8,128)} async-done(((f32[64,128]{1,0:T(8,128)}), f32[32,128]{1,0:T(8,128)}) %reduce-scatter.23.cloned.1.call-update) | async-done | bytes 16400
  141.9 2.6 %collective-permute-done.20 = f32[128,128]{0,1:T(8,128)S(1)} collective-permute-done((f32[128,128]{0,1:T(8,128)S(1)}, f32[128,128]{0,1:T(8,128)S(1)}, u32[]{:S(2)}, u32[]{:S(2)}) %collective-permute-start.20) | collective-permute-done | bytes 65568 | tf_op jit(solution)/shard_map/ppermute | solution.py:16
  144.6 1.8 collective-permute-start.21
  146.4 2.5 %collective-permute-done.21 = f32[64,128]{0,1:T(8,128)S(1)} collective-permute-done((f32[64,128]{0,1:T(8,128)S(1)}, f32[64,128]{0,1:T(8,128)S(1)}, u32[]{:S(2)}, u32[]{:S(2)}) %collective-permute-start.21) | collective-permute-done | bytes 32800 | tf_op jit(solution)/shard_map/ppermute | solution.py:16
  150.0 8.5 %reduce-scatter.25.cloned.1.call-done = f32[32,128]{1,0:T(8,128)} async-done(((f32[64,128]{1,0:T(8,128)}), f32[32,128]{1,0:T(8,128)}) %reduce-scatter.25.cloned.1.call-update) | async-done | bytes 16400 | tf_op jit(solution)/shard_map/reduce_scatter | solution.py:50
  161.4 2.5 %collective-permute-done.22 = f32[64,128]{0,1:T(8,128)S(1)} collective-permute-done((f32[64,128]{0,1:T(8,128)S(1)}, f32[64,128]{0,1:T(8,128)S(1)}, u32[]{:S(2)}, u32[]{:S(2)}) %collective-permute-start.22) | collective-permute-done | bytes 32800 | tf_op jit(solution)/shard_map/ppermute | solution.py:16
  164.8 8.6 %reduce-scatter.27.cloned.1.call-done = f32[32,128]{1,0:T(8,128)} async-done(((f32[64,128]{1,0:T(8,128)}), f32[32,128]{1,0:T(8,128)}) %reduce-scatter.27.cloned.1.call-update) | async-done | bytes 16400
  176.3 2.5 %collective-permute-done.23 = f32[64,128]{0,1:T(8,128)S(1)} collective-permute-done((f32[64,128]{0,1:T(8,128)S(1)}, f32[64,128]{0,1:T(8,128)S(1)}, u32[]{:S(2)}, u32[]{:S(2)}) %collective-permute-start.23) | collective-permute-done | bytes 32800 | tf_op jit(solution)/shard_map/ppermute | solution.py:16
  180.3 8.1 %reduce-scatter.29.cloned.1.call-done = f32[32,128]{1,0:T(8,128)} async-done(((f32[64,128]{1,0:T(8,128)}), f32[32,128]{1,0:T(8,128)}) %reduce-scatter.29.cloned.1.call-update) | async-done | bytes 16400
  (108 shorter events, 37.9 us)
Async XLA Ops:
  7.2 2.0 %copy-start = (bf16[1024,1024]{1,0:T(8,128)(2,1)S(1)}, bf16[1024,1024]{1,0:T(8,128)(2,1)}, u32[]{:S(2)}) copy-start(bf16[1024,1024]{1,0:T(8,128)(2,1)} %param.10) | copy-start | bytes 6291460
  7.2 9.5 %copy-start.2 = (bf16[32,896]{1,0:T(8,128)(2,1)S(1)}, bf16[32,896]{1,0:T(8,128)(2,1)}, u32[]{:S(2)}) copy-start(bf16[32,896]{1,0:T(8,128)(2,1)} %param.16) | copy-start | bytes 172036
  7.2 9.5 %copy-start.7 = (bf16[3,32,128]{2,1,0:T(8,128)(2,1)S(1)}, bf16[3,32,128]{2,1,0:T(8,128)(2,1)}, u32[]{:S(2)}) copy-start(bf16[3,32,128]{2,1,0:T(8,128)(2,1)} %param.17) | copy-start | bytes 73732
  7.2 15.2 %copy-start.4 = (bf16[32,896]{1,0:T(8,128)(2,1)S(1)}, bf16[32,896]{1,0:T(8,128)(2,1)}, u32[]{:S(2)}) copy-start(bf16[32,896]{1,0:T(8,128)(2,1)} %param.15) | copy-start | bytes 172036
  7.2 87.5 %reduce-scatter.19.cloned.1.call-start = ((), (), s32[]{:S(2)}) async-start(), calls=%async_computation.6 | async-start | bytes 49152
  9.2 60.9 %copy-start.3 = (bf16[3,32,128]{2,1,0:T(8,128)(2,1)S(1)}, bf16[3,32,128]{2,1,0:T(8,128)(2,1)}, u32[]{:S(2)}) copy-start(bf16[3,32,128]{2,1,0:T(8,128)(2,1)} %param.18) | copy-start | bytes 73732
  12.1 4.6 %collective-permute-start = (bf16[64,128]{1,0:T(8,128)(2,1)S(1)}, bf16[64,128]{1,0:T(8,128)(2,1)S(1)}, u32[]{:S(2)}, u32[]{:S(2)}) collective-permute-start(bf16[64,128]{1,0:T(8,128)(2,1)S(1)} %all_gather.18), channel_id=1, source_target_pairs={{0,2},{2,0},{4,6},{6,4},{8,10},{10,8},{12,14},{14,12},{16,18},{18,... | collective-permute-start | bytes 49160 | tf_op jit(solution)/shard_map/ppermute | solution.py:16
  18.6 3.8 %collective-permute-start.1 = (bf16[64,128]{1,0:T(8,128)(2,1)S(1)}, bf16[64,128]{1,0:T(8,128)(2,1)S(1)}, u32[]{:S(2)}, u32[]{:S(2)}) collective-permute-start(bf16[64,128]{1,0:T(8,128)(2,1)S(1)} %all_gather.19), channel_id=1, source_target_pairs={{0,2},{2,0},{4,6},{6,4},{8,10},{10,8},{12,14},{14,12},{16,18},{18,... | collective-permute-start | bytes 49160 | tf_op jit(solution)/shard_map/ppermute | solution.py:16
  24.3 3.8 %collective-permute-start.2 = (bf16[64,128]{1,0:T(8,128)(2,1)S(1)}, bf16[64,128]{1,0:T(8,128)(2,1)S(1)}, u32[]{:S(2)}, u32[]{:S(2)}) collective-permute-start(bf16[64,128]{1,0:T(8,128)(2,1)S(1)} %all_gather.20), channel_id=1, source_target_pairs={{0,2},{2,0},{4,6},{6,4},{8,10},{10,8},{12,14},{14,12},{16,18},{18,... | collective-permute-start | bytes 49160 | tf_op jit(solution)/shard_map/ppermute | solution.py:16
  28.1 4.0 %collective-permute-start.3 = (bf16[128,128]{1,0:T(8,128)(2,1)S(1)}, bf16[128,128]{1,0:T(8,128)(2,1)S(1)}, u32[]{:S(2)}, u32[]{:S(2)}) collective-permute-start(bf16[128,128]{1,0:T(8,128)(2,1)S(1)} %maximum_select_fusion.15), channel_id=1, source_target_pairs={{0,4},{4,0},{2,6},{6,2},{8,12},{12,8},{10,14},{14,10},{16,20},{20,... | collective-permute-start | bytes 98312 | tf_op jit(solution)/shard_map/ppermute | solution.py:16
  34.1 3.8 %collective-permute-start.4 = (bf16[64,128]{1,0:T(8,128)(2,1)S(1)}, bf16[64,128]{1,0:T(8,128)(2,1)S(1)}, u32[]{:S(2)}, u32[]{:S(2)}) collective-permute-start(bf16[64,128]{1,0:T(8,128)(2,1)S(1)} %all_gather.21), channel_id=1, source_target_pairs={{0,2},{2,0},{4,6},{6,4},{8,10},{10,8},{12,14},{14,12},{16,18},{18,... | collective-permute-start | bytes 49160 | tf_op jit(solution)/shard_map/ppermute | solution.py:16
  37.9 4.0 %collective-permute-start.5 = (bf16[128,128]{1,0:T(8,128)(2,1)S(1)}, bf16[128,128]{1,0:T(8,128)(2,1)S(1)}, u32[]{:S(2)}, u32[]{:S(2)}) collective-permute-start(bf16[128,128]{1,0:T(8,128)(2,1)S(1)} %maximum_select_fusion.16), channel_id=1, source_target_pairs={{0,4},{4,0},{2,6},{6,2},{8,12},{12,8},{10,14},{14,10},{16,20},{20,... | collective-permute-start | bytes 98312 | tf_op jit(solution)/shard_map/ppermute | solution.py:16
  43.8 3.8 %collective-permute-start.6 = (bf16[64,128]{1,0:T(8,128)(2,1)S(1)}, bf16[64,128]{1,0:T(8,128)(2,1)S(1)}, u32[]{:S(2)}, u32[]{:S(2)}) collective-permute-start(bf16[64,128]{1,0:T(8,128)(2,1)S(1)} %all_gather.22), channel_id=1, source_target_pairs={{0,2},{2,0},{4,6},{6,4},{8,10},{10,8},{12,14},{14,12},{16,18},{18,... | collective-permute-start | bytes 49160 | tf_op jit(solution)/shard_map/ppermute | solution.py:16
  47.6 4.0 %collective-permute-start.7 = (bf16[128,128]{1,0:T(8,128)(2,1)S(1)}, bf16[128,128]{1,0:T(8,128)(2,1)S(1)}, u32[]{:S(2)}, u32[]{:S(2)}) collective-permute-start(bf16[128,128]{1,0:T(8,128)(2,1)S(1)} %maximum_select_fusion.17), channel_id=1, source_target_pairs={{0,4},{4,0},{2,6},{6,2},{8,12},{12,8},{10,14},{14,10},{16,20},{20,... | collective-permute-start | bytes 98312 | tf_op jit(solution)/shard_map/ppermute | solution.py:16
  51.6 4.4 %collective-permute-start.8 = (bf16[256,128]{1,0:T(8,128)(2,1)S(1)}, bf16[256,128]{1,0:T(8,128)(2,1)S(1)}, u32[]{:S(2)}, u32[]{:S(2)}) collective-permute-start(bf16[256,128]{1,0:T(8,128)(2,1)S(1)} %maximum_select_fusion.9), channel_id=1, source_target_pairs={{0,8},{8,0},{2,10},{10,2},{4,12},{12,4},{6,14},{14,6},{16,24},{24,... | collective-permute-start | bytes 196616 | tf_op jit(solution)/shard_map/ppermute | solution.py:16
  57.9 3.8 %collective-permute-start.9 = (bf16[64,128]{1,0:T(8,128)(2,1)S(1)}, bf16[64,128]{1,0:T(8,128)(2,1)S(1)}, u32[]{:S(2)}, u32[]{:S(2)}) collective-permute-start(bf16[64,128]{1,0:T(8,128)(2,1)S(1)} %all_gather.23), channel_id=1, source_target_pairs={{0,2},{2,0},{4,6},{6,4},{8,10},{10,8},{12,14},{14,12},{16,18},{18,... | collective-permute-start | bytes 49160 | tf_op jit(solution)/shard_map/ppermute | solution.py:16
  61.7 4.0 %collective-permute-start.10 = (bf16[128,128]{1,0:T(8,128)(2,1)S(1)}, bf16[128,128]{1,0:T(8,128)(2,1)S(1)}, u32[]{:S(2)}, u32[]{:S(2)}) collective-permute-start(bf16[128,128]{1,0:T(8,128)(2,1)S(1)} %maximum_select_fusion.18), channel_id=1, source_target_pairs={{0,4},{4,0},{2,6},{6,2},{8,12},{12,8},{10,14},{14,10},{16,20},{20,... | collective-permute-start | bytes 98312 | tf_op jit(solution)/shard_map/ppermute | solution.py:16
  65.7 4.3 %collective-permute-start.11 = (bf16[256,128]{1,0:T(8,128)(2,1)S(1)}, bf16[256,128]{1,0:T(8,128)(2,1)S(1)}, u32[]{:S(2)}, u32[]{:S(2)}) collective-permute-start(bf16[256,128]{1,0:T(8,128)(2,1)S(1)} %maximum_select_fusion.10), channel_id=1, source_target_pairs={{0,8},{8,0},{2,10},{10,2},{4,12},{12,4},{6,14},{14,6},{16,24},{24,... | collective-permute-start | bytes 196616 | tf_op jit(solution)/shard_map/ppermute | solution.py:16
  70.4 5.4 %collective-permute-start.12 = (f32[256,128]{0,1:T(8,128)S(1)}, f32[256,128]{0,1:T(8,128)S(1)}, u32[]{:S(2)}, u32[]{:S(2)}) collective-permute-start(f32[256,128]{0,1:T(8,128)S(1)} %slice_select_fusion.1), channel_id=1, source_target_pairs={{0,8},{8,0},{2,10},{10,2},{4,12},{12,4},{6,14},{14,6},{16,24},{24,... | collective-permute-start | bytes 393224 | tf_op jit(solution)/shard_map/ppermute | solution.py:16
  75.9 4.3 %collective-permute-start.13 = (f32[128,128]{0,1:T(8,128)S(1)}, f32[128,128]{0,1:T(8,128)S(1)}, u32[]{:S(2)}, u32[]{:S(2)}) collective-permute-start(f32[128,128]{0,1:T(8,128)S(1)} %slice_select_fusion.11), channel_id=1, source_target_pairs={{0,4},{4,0},{2,6},{6,2},{8,12},{12,8},{10,14},{14,10},{16,20},{20,... | collective-permute-start | bytes 196616 | tf_op jit(solution)/shard_map/ppermute | solution.py:16
  80.3 4.3 %collective-permute-start.14 = (f32[64,128]{0,1:T(8,128)S(1)}, f32[64,128]{0,1:T(8,128)S(1)}, u32[]{:S(2)}, u32[]{:S(2)}) collective-permute-start(f32[64,128]{0,1:T(8,128)S(1)} %slice_select_fusion.10), channel_id=1, source_target_pairs={{0,2},{2,0},{4,6},{6,4},{8,10},{10,8},{12,14},{14,12},{16,18},{18,... | collective-permute-start | bytes 98312 | tf_op jit(solution)/shard_map/ppermute | solution.py:16
  85.4 34.4 %reduce-scatter.21.cloned.1.call-start = ((), (), s32[]{:S(2)}) async-start(), calls=%async_computation.7 | async-start | bytes 49152 | tf_op jit(solution)/shard_map/reduce_scatter | solution.py:50
  95.7 54.1 %copy-start.5 = (bf16[3,32]{1,0:T(4,128)(2,1)S(1)}, bf16[3,32]{1,0:T(4,128)(2,1)}, u32[]{:S(2)}) copy-start(bf16[3,32]{1,0:T(4,128)(2,1)} %param.19) | copy-start | bytes 580
  95.7 54.1 %copy-start.6 = (bf16[1024]{0:T(1024)(128)(2,1)S(1)}, bf16[1024]{0:T(1024)(128)(2,1)}, u32[]{:S(2)}) copy-start(bf16[1024]{0:T(1024)(128)(2,1)} %param.14) | copy-start | bytes 6148
  95.8 54.1 %copy-start.1 = (bf16[1024,128]{1,0:T(8,128)(2,1)S(1)}, bf16[1024,128]{1,0:T(8,128)(2,1)}, u32[]{:S(2)}) copy-start(bf16[1024,128]{1,0:T(8,128)(2,1)} %param.13) | copy-start | bytes 786436
  95.8 5.8 %collective-permute-start.15 = (f32[256,128]{0,1:T(8,128)S(1)}, f32[256,128]{0,1:T(8,128)S(1)}, u32[]{:S(2)}, u32[]{:S(2)}) collective-permute-start(f32[256,128]{0,1:T(8,128)S(1)} %slice_select_fusion), channel_id=1, source_target_pairs={{0,8},{8,0},{2,10},{10,2},{4,12},{12,4},{6,14},{14,6},{16,24},{24,... | collective-permute-start | bytes 393224 | tf_op jit(solution)/shard_map/ppermute | solution.py:16
  101.6 4.3 %collective-permute-start.16 = (f32[128,128]{0,1:T(8,128)S(1)}, f32[128,128]{0,1:T(8,128)S(1)}, u32[]{:S(2)}, u32[]{:S(2)}) collective-permute-start(f32[128,128]{0,1:T(8,128)S(1)} %slice_select_fusion.9), channel_id=1, source_target_pairs={{0,4},{4,0},{2,6},{6,2},{8,12},{12,8},{10,14},{14,10},{16,20},{20,... | collective-permute-start | bytes 196616 | tf_op jit(solution)/shard_map/ppermute | solution.py:16
  106.0 4.3 %collective-permute-start.17 = (f32[64,128]{0,1:T(8,128)S(1)}, f32[64,128]{0,1:T(8,128)S(1)}, u32[]{:S(2)}, u32[]{:S(2)}) collective-permute-start(f32[64,128]{0,1:T(8,128)S(1)} %slice_select_fusion.8), channel_id=1, source_target_pairs={{0,2},{2,0},{4,6},{6,4},{8,10},{10,8},{12,14},{14,12},{16,18},{18,... | collective-permute-start | bytes 98312 | tf_op jit(solution)/shard_map/ppermute | solution.py:16
  111.2 28.0 %reduce-scatter.23.cloned.1.call-start = ((), (), s32[]{:S(2)}) async-start(), calls=%async_computation.8 | async-start | bytes 49152
  120.8 4.4 %collective-permute-start.18 = (f32[128,128]{0,1:T(8,128)S(1)}, f32[128,128]{0,1:T(8,128)S(1)}, u32[]{:S(2)}, u32[]{:S(2)}) collective-permute-start(f32[128,128]{0,1:T(8,128)S(1)} %slice_select_fusion.7), channel_id=1, source_target_pairs={{0,4},{4,0},{2,6},{6,2},{8,12},{12,8},{10,14},{14,10},{16,20},{20,... | collective-permute-start | bytes 196616 | tf_op jit(solution)/shard_map/ppermute | solution.py:16
  125.3 4.3 %collective-permute-start.19 = (f32[64,128]{0,1:T(8,128)S(1)}, f32[64,128]{0,1:T(8,128)S(1)}, u32[]{:S(2)}, u32[]{:S(2)}) collective-permute-start(f32[64,128]{0,1:T(8,128)S(1)} %slice_select_fusion.6), channel_id=1, source_target_pairs={{0,2},{2,0},{4,6},{6,4},{8,10},{10,8},{12,14},{14,12},{16,18},{18,... | collective-permute-start | bytes 98312 | tf_op jit(solution)/shard_map/ppermute | solution.py:16
  130.4 28.1 %reduce-scatter.25.cloned.1.call-start = ((), (), s32[]{:S(2)}) async-start(), calls=%async_computation.9 | async-start | bytes 49152 | tf_op jit(solution)/shard_map/reduce_scatter | solution.py:50
  140.2 4.3 %collective-permute-start.20 = (f32[128,128]{0,1:T(8,128)S(1)}, f32[128,128]{0,1:T(8,128)S(1)}, u32[]{:S(2)}, u32[]{:S(2)}) collective-permute-start(f32[128,128]{0,1:T(8,128)S(1)} %slice_select_fusion.5), channel_id=1, source_target_pairs={{0,4},{4,0},{2,6},{6,2},{8,12},{12,8},{10,14},{14,10},{16,20},{20,... | collective-permute-start | bytes 196616 | tf_op jit(solution)/shard_map/ppermute | solution.py:16
  144.6 4.3 %collective-permute-start.21 = (f32[64,128]{0,1:T(8,128)S(1)}, f32[64,128]{0,1:T(8,128)S(1)}, u32[]{:S(2)}, u32[]{:S(2)}) collective-permute-start(f32[64,128]{0,1:T(8,128)S(1)} %slice_select_fusion.4), channel_id=1, source_target_pairs={{0,2},{2,0},{4,6},{6,4},{8,10},{10,8},{12,14},{14,12},{16,18},{18,... | collective-permute-start | bytes 98312 | tf_op jit(solution)/shard_map/ppermute | solution.py:16
  149.8 23.7 %reduce-scatter.27.cloned.1.call-start = ((), (), s32[]{:S(2)}) async-start(), calls=%async_computation.10 | async-start | bytes 49152
  159.5 4.4 %collective-permute-start.22 = (f32[64,128]{0,1:T(8,128)S(1)}, f32[64,128]{0,1:T(8,128)S(1)}, u32[]{:S(2)}, u32[]{:S(2)}) collective-permute-start(f32[64,128]{0,1:T(8,128)S(1)} %slice_select_fusion.3), channel_id=1, source_target_pairs={{0,2},{2,0},{4,6},{6,4},{8,10},{10,8},{12,14},{14,12},{16,18},{18,... | collective-permute-start | bytes 98312 | tf_op jit(solution)/shard_map/ppermute | solution.py:16
  164.7 23.7 %reduce-scatter.29.cloned.1.call-start = ((), (), s32[]{:S(2)}) async-start(), calls=%async_computation.11 | async-start | bytes 49152
  174.5 4.4 %collective-permute-start.23 = (f32[64,128]{0,1:T(8,128)S(1)}, f32[64,128]{0,1:T(8,128)S(1)}, u32[]{:S(2)}, u32[]{:S(2)}) collective-permute-start(f32[64,128]{0,1:T(8,128)S(1)} %slice_select_fusion.2), channel_id=1, source_target_pairs={{0,2},{2,0},{4,6},{6,4},{8,10},{10,8},{12,14},{14,12},{16,18},{18,... | collective-permute-start | bytes 98312 | tf_op jit(solution)/shard_map/ppermute | solution.py:16
Sparse Core Ops, SparseCore 0:
  85.6 9.1 reduce-scatter.18
  111.3 8.5 reduce-scatter.20
  130.6 8.5 reduce-scatter.22
  149.9 8.5 reduce-scatter.24
  164.8 8.5 reduce-scatter.26
  179.8 8.5 reduce-scatter.28
where the time goes:
time: 198 us; the launch traced here: 197 us
  waiting for transfers between devices  106 us (54%)
  starting transfers between devices  48.4 us (24%)
  between operations  15.3 us (8%)
  blocking collectives  11 us (6%)
  local copies, waits for them, and re-layouts  9.96 us (5%)
  matrix products  4.53 us (2%)
    ppermute x24, waiting for transfers between devices, from_partner(): return lax.ppermute(block, axis, route)  54.5 us
    ppermute x24, starting transfers between devices, from_partner(): return lax.ppermute(block, axis, route)  48.1 us
    unnamed x10, waiting for transfers between devices  34.7 us
    reduce_scatter x2, waiting for transfers between devices, group_reduce(): return lax.psum_scatter(reduced, 'sec', scatter_dimension=0, tiled=True)  17.1 us
    all_gather x6, blocking collectives, group_gather(): block = lax.all_gather(piece, 'sec', axis=0, tiled=True)  11 us
    unnamed x29, local copies, waits for them, and re-layouts  9.61 us
  transfers between devices with their start and end apart: 30, of which 30 were waited for; matrix products, arithmetic and copies ran while one was open for 1% of the time, Pallas kernels for 0%

commit v1 on v0

--- a/solution.py
+++ b/solution.py
@@ -1,9 +1,137 @@
+import functools
+
 import jax
 import jax.numpy as jnp
 from jax import lax
+from jax.experimental import pallas as pl
+from jax.experimental.pallas import tpu as pltpu
 from jax.sharding import PartitionSpec as P
 
 BLOCK = 128
+VMEM_LIMIT = 56 * 2**20
+AXES = ("leaf", "sec")
+
+
+def to_chips(block, distances):
+    leaves, sections = lax.axis_size("leaf"), lax.axis_size("sec")
+    route = []
+    for leaf in range(leaves):
+        for section, distance in enumerate(distances):
+            route.append((leaf * sections + section, (leaf ^ distance) * sections + section))
+    return lax.ppermute(block, AXES, route)
+
+
+def to_sections(block, turn):
+    sections = lax.axis_size("sec")
+    return lax.ppermute(block, "sec", [(s, (s - turn) % sections) for s in range(sections)])
+
+
+def pack_kernel(levels, blocks_ref, leaf_ref, shift_ref, panel_ref, inv_ref, rhs_ref, noise_ref, low_ref, top_ref):
+    row_count, samples = low_ref.shape[0], shift_ref.shape[1]
+    subtree_rows = shift_ref.shape[0]
+    live_from = subtree_rows - blocks_ref[0, 0] * BLOCK
+    positions = lax.broadcasted_iota(jnp.int32, shift_ref.shape, 0)
+    shift = shift_ref[...]
+    shift = jnp.where(positions >= live_from, shift, jnp.zeros_like(shift))
+    boundary = jnp.dot(leaf_ref[...], shift, preferred_element_type=jnp.float32)
+    low_ref[:, :samples] = boundary.astype(jnp.bfloat16)
+    at = samples
+    offset = 0
+    unit = panel_ref.shape[1] // (2 ** (levels + 1) - 2)
+    for height in range(1, levels + 1):
+        span = 2**height * unit
+        out = low_ref if height < levels else top_ref
+        if height == levels:
+            at = 0
+        out[:, at : at + span] = panel_ref[:, offset : offset + span]
+        out[:, at + span : at + 2 * span] = inv_ref[:, offset : offset + span]
+        out[:, at + 2 * span : at + 2 * span + samples] = rhs_ref[height - 1]
+        out[:, at + 2 * span + samples : at + 2 * span + 2 * samples] = noise_ref[height - 1]
+        at += 2 * span + 2 * samples
+        offset += span
+
+
+def place(pieces_meta, piece_refs, place_ref, whole_ref, row_count):
+    for index, (which, start) in enumerate(pieces_meta):
+        at = pl.multiple_of(place_ref[index], row_count)
+        whole_ref[pl.ds(at, row_count), :] = piece_refs[which][start : start + row_count, :]
+
+
+def solve_forward(whole, rows, at, span, samples, children):
+    panel = whole[rows, at : at + span]
+    inverse = whole[rows, at + span : at + 2 * span]
+    rhs = whole[rows, at + 2 * span : at + 2 * span + samples]
+    reduced = rhs.astype(jnp.float32) - jnp.dot(panel, children, preferred_element_type=jnp.float32)
+    reduced = reduced.astype(jnp.bfloat16)
+    return jnp.dot(inverse, reduced, preferred_element_type=jnp.float32).astype(jnp.bfloat16)
+
+
+def low_kernel(levels, unit, pieces_meta, place_ref, *refs):
+    piece_refs, (whole_ref, *solved_refs) = refs[: -levels], refs[-levels:]
+    row_count = whole_ref.shape[0] // sum(1 for _ in pieces_meta)
+    place(pieces_meta, piece_refs, place_ref, whole_ref, row_count)
+    samples = solved_refs[0].shape[1]
+    total = whole_ref.shape[0]
+    below_ref, below_at = whole_ref, 0
+    at = samples
+    for height in range(1, levels):
+        span = 2**height * unit
+        for group in range(total // span):
+            rows = slice(group * span, (group + 1) * span)
+            children = below_ref[rows, 0:samples]
+            solved_refs[height - 1][rows, :] = solve_forward(whole_ref, rows, at, span, samples, children)
+        below_ref = solved_refs[height - 1]
+        at += 2 * span + 2 * samples
+
+
+def transposed_dot(matrix, vector):
+    return lax.dot_general(matrix, vector, (((0,), (0,)), ((), ())), preferred_element_type=jnp.float32)
+
+
+def top_kernel(levels, unit, pieces_meta, place_ref, low_ref, dev_ref, partner_ref, *refs):
+    solved_refs = refs[: levels - 1]
+    sample_ref, correction_ref, whole_ref, child_ref, sum_ref, x_ref = refs[-6:]
+    piece_refs = refs[levels - 1 : -6]
+    samples = partner_ref.shape[1]
+    count = len(pieces_meta)
+    row_count = whole_ref.shape[0] // count
+    place(pieces_meta, piece_refs, place_ref, whole_ref, row_count)
+    half = child_ref.shape[0] // 2
+    upper = place_ref[count]
+    child_ref[pl.ds(pl.multiple_of(upper * half, half), half), :] = solved_refs[-1][...]
+    child_ref[pl.ds(pl.multiple_of((1 - upper) * half, half), half), :] = partner_ref[...]
+    span = 2**levels * unit
+    rows = slice(0, span)
+    own = solve_forward(whole_ref, rows, 0, span, samples, child_ref[...])
+    correction = None
+    low_at = low_ref.shape[1]
+    for height in range(levels, 0, -1):
+        span = 2**height * unit
+        first = pl.multiple_of(place_ref[count + 1 + 2 * (height - 1)], span)
+        mine = pl.multiple_of(place_ref[count + 2 + 2 * (height - 1)], row_count)
+        if height == levels:
+            source, at, rows = whole_ref, 0, pl.ds(0, span)
+        else:
+            low_at -= 2 * span + 2 * samples
+            source, at, rows = low_ref, low_at, pl.ds(first, span)
+            own = solved_refs[height - 1][rows, :]
+        summed = own.astype(jnp.float32) + source[rows, at + 2 * span + samples : at + 2 * span + 2 * samples].astype(
+            jnp.float32
+        )
+        if correction is not None:
+            summed = summed - correction
+        x = transposed_dot(source[rows, at + span : at + 2 * span], summed.astype(jnp.bfloat16))
+        x = x.astype(jnp.bfloat16)
+        x_ref[0:span, :] = x
+        sample_ref[height - 1] = (
+            dev_ref[height - 1].astype(jnp.float32) * x_ref[pl.ds(mine, row_count), :].astype(jnp.float32)
+        ).astype(jnp.bfloat16)
+        sum_ref[0:span, :] = transposed_dot(source[rows, at : at + span], x)
+        if height > 1:
+            below = pl.multiple_of(place_ref[count + 1 + 2 * levels + height - 1], span // 2)
+            correction = sum_ref[pl.ds(below, span // 2), :]
+        else:
+            correction_ref[...] = sum_ref[pl.ds(mine, row_count), :]
 
 
 def from_partner(block, axis, apart):
@@ -50,13 +178,7 @@
     return lax.psum_scatter(reduced, "sec", scatter_dimension=0, tiled=True)
 
 
-def transposed_product(matrix, vector):
-    return lax.dot_general(
-        matrix, vector, (((0,), (0,)), ((), ())), preferred_element_type=jnp.float32
-    )
-
-
-def on_device(
+def leafwise_on_device(
     leaf_inv,
     subtree_blocks,
     subtree_shift_rhs,
@@ -111,20 +233,20 @@
         if correction is not None:
             summed = summed - correction
         vector = summed.astype(jnp.bfloat16)
-        backed = group_reduce(transposed_product(inverse_block, vector), height).astype(
+        backed = group_reduce(transposed_dot(inverse_block, vector), height).astype(
             jnp.bfloat16
         )
         samples[height - 1] = (
             sep_dev[height - 1][:, None].astype(jnp.float32) * backed.astype(jnp.float32)
         ).astype(jnp.bfloat16)
-        correction = group_reduce(transposed_product(panel, backed), height)
+        correction = group_reduce(transposed_dot(panel, backed), height)
     leading = jnp.zeros((subtree_row_count - row_count, correction.shape[1]), jnp.float32)
     placed = jnp.concatenate([leading, correction], axis=0)
     subtree_summed = (
         subtree_forward_solution.astype(jnp.float32) + leaf_noise.astype(jnp.float32) - placed
     )
     subtree_weight = jnp.where(row_activity, subtree_summed, jnp.float32(0.0)).astype(jnp.bfloat16)
-    subtree_solution = transposed_product(leaf_inv, subtree_weight)
+    subtree_solution = transposed_dot(leaf_inv, subtree_weight)
     sample_scales = leaf_dev[:, None].astype(jnp.float32)
     subtree_scaled_samples = jnp.where(
         row_activity, sample_scales * subtree_solution, jnp.float32(0.0)
@@ -132,20 +254,182 @@
     return (subtree_scaled_samples, jnp.stack(samples))
 
 
+def split_pieces(pieces):
+    arrays, meta, where = [], [], []
+    for array, start, distance, section in pieces:
+        for index, known in enumerate(arrays):
+            if known is array:
+                break
+        else:
+            arrays.append(array)
+            index = len(arrays) - 1
+        meta.append((index, start))
+        where.append((distance, section))
+    return arrays, meta, where
+
+
+def row_places(where, leaves, leaf, sections, row_count):
+    return [(((leaf ^ distance) & (leaves - 1)) * sections + section) * row_count for distance, section in where]
+
+
+def on_device(
+    leaf_inv,
+    subtree_blocks,
+    subtree_shift_rhs,
+    leaf_noise,
+    leaf_dev,
+    sep_inv,
+    sep_panel,
+    sep_rhs,
+    sep_noise,
+    sep_dev,
+):
+    subtree_rows = leaf_inv.shape[0]
+    row_count = sep_inv.shape[0]
+    levels, _, samples = sep_rhs.shape
+    sections = lax.axis_size("sec")
+    unit = sections * row_count
+    leaf = lax.axis_index("leaf")
+    section = lax.axis_index("sec")
+    params = pltpu.CompilerParams(vmem_limit_bytes=VMEM_LIMIT)
+    vmem = pl.BlockSpec(memory_space=pltpu.VMEM)
+    smem = pl.BlockSpec(memory_space=pltpu.SMEM)
+
+    top_columns = 2 * 2**levels * unit + 2 * samples
+    low_columns = samples + sum(2 * 2**h * unit + 2 * samples for h in range(1, levels))
+    full = lambda array: pl.BlockSpec(array.shape, lambda i: (0,) * array.ndim)
+    low, top = pl.pallas_call(
+        functools.partial(pack_kernel, levels),
+        grid=(1,),
+        out_shape=(
+            jax.ShapeDtypeStruct((row_count, low_columns), jnp.bfloat16),
+            jax.ShapeDtypeStruct((row_count, top_columns), jnp.bfloat16),
+        ),
+        in_specs=[
+            smem,
+            pl.BlockSpec((row_count, subtree_rows), lambda i: (subtree_rows // row_count - 1, 0)),
+            full(subtree_shift_rhs),
+            full(sep_panel),
+            full(sep_inv),
+            full(sep_rhs),
+            full(sep_noise),
+        ],
+        out_specs=(
+            pl.BlockSpec((row_count, low_columns), lambda i: (0, 0)),
+            pl.BlockSpec((row_count, top_columns), lambda i: (0, 0)),
+        ),
+        compiler_params=params,
+        name="pack",
+    )(subtree_blocks, leaf_inv, subtree_shift_rhs, sep_panel, sep_inv, sep_rhs, sep_noise)
+
+    quad = 2 ** (levels - 1)
+    group = 2**levels
+    other = 1 - section
+
+    def swap(block):
+        return to_sections(block, 1)
+
+    low_other, top_other = swap(low), swap(top)
+    low_pair = jnp.concatenate([low, low_other], axis=0)
+    top_pair = jnp.concatenate([top, top_other], axis=0)
+
+    def halves(block, distance):
+        arrived = to_chips(block, (distance, distance))
+        return [(arrived, 0, distance, section), (swap(arrived), 0, distance, other)]
+
+    def pairs(block, first, second):
+        arrived = to_chips(block, (first, second))
+        passed = swap(arrived)
+        here = jnp.where(section == 0, first, second)
+        there = jnp.where(section == 0, second, first)
+        return [
+            (arrived, 0, here, section),
+            (arrived, row_count, here, other),
+            (passed, 0, there, other),
+            (passed, row_count, there, section),
+        ]
+
+    top_pieces = [(top, 0, 0, section), (top_other, 0, 0, other)]
+    low_pieces = [(low, 0, 0, section), (low_other, 0, 0, other)]
+    top_pieces += halves(top, 4)
+    low_pieces += pairs(low_pair, 1, 2)
+    low_pieces += halves(low, 3)
+    top_pieces += pairs(top_pair, 5, 6)
+    top_pieces += pairs(top_pair, 7, 1)
+    top_pieces += pairs(top_pair, 2, 3)
+
+    arrays, meta, where = split_pieces(low_pieces)
+    places = jnp.stack(row_places(where, quad, leaf, sections, row_count)).astype(jnp.int32)
+    low_whole, *solved = pl.pallas_call(
+        functools.partial(low_kernel, levels, unit, meta),
+        out_shape=[jax.ShapeDtypeStruct((quad * unit, low_columns), jnp.bfloat16)]
+        + [jax.ShapeDtypeStruct((quad * unit, samples), jnp.bfloat16)] * (levels - 1),
+        in_specs=[smem] + [vmem] * len(arrays),
+        out_specs=[vmem] * levels,
+        compiler_params=params,
+        name="low",
+    )(places, *arrays)
+    partner = to_chips(solved[-1], (quad,) * sections)
+
+    row_positions = jnp.arange(subtree_rows, dtype=jnp.int32)
+    row_activity = (row_positions >= subtree_rows - subtree_blocks[0, 0] * BLOCK)[:, None]
+    zero = jnp.float32(0.0)
+    shifted = jnp.where(row_activity, subtree_shift_rhs, jnp.zeros((), subtree_shift_rhs.dtype))
+    forward = jnp.dot(leaf_inv, shifted, preferred_element_type=jnp.float32)
+    forward = jnp.where(row_activity, forward, zero).astype(jnp.bfloat16)
+
+    arrays, meta, where = split_pieces(top_pieces)
+    places = row_places(where, group, leaf, sections, row_count)
+    places.append(leaf >> (levels - 1) & 1)
+    for height in range(1, levels + 1):
+        places.append(((leaf & (quad - 1)) >> height << height) * unit if height < levels else 0 * leaf)
+        places.append((leaf & (2**height - 1)) * unit + section * row_count)
+    for height in range(1, levels + 1):
+        places.append((leaf >> (height - 1) & 1) * 2 ** (height - 1) * unit)
+    places = jnp.stack(places).astype(jnp.int32)
+    span = group * unit
+    sep_sample, correction = pl.pallas_call(
+        functools.partial(top_kernel, levels, unit, meta),
+        out_shape=(
+            jax.ShapeDtypeStruct((levels, row_count, samples), jnp.bfloat16),
+            jax.ShapeDtypeStruct((row_count, samples), jnp.float32),
+        ),
+        in_specs=[smem] + [vmem] * (2 + levels + len(arrays)),
+        out_specs=(vmem, vmem),
+        scratch_shapes=[
+            pltpu.VMEM((span, top_columns), jnp.bfloat16),
+            pltpu.VMEM((span, samples), jnp.bfloat16),
+            pltpu.VMEM((span, samples), jnp.float32),
+            pltpu.VMEM((span, samples), jnp.bfloat16),
+        ],
+        compiler_params=params,
+        name="top",
+    )(places, low_whole, jnp.broadcast_to(sep_dev[:, :, None], sep_rhs.shape), partner, *solved, *arrays)
+
+    leading = jnp.zeros((subtree_rows - row_count, samples), jnp.float32)
+    placed = jnp.concatenate([leading, correction], axis=0)
+    summed = forward.astype(jnp.float32) + leaf_noise.astype(jnp.float32) - placed
+    weight = jnp.where(row_activity, summed, zero).astype(jnp.bfloat16)
+    solution_rows = transposed_dot(leaf_inv, weight)
+    scaled = leaf_dev[:, None].astype(jnp.float32) * solution_rows
+    return jnp.where(row_activity, scaled, zero).astype(jnp.bfloat16), sep_sample
+
+
 def solution(mesh):
+    rows = P(AXES, None)
     in_specs = (
-        P(("leaf", "sec"), None),
+        rows,
         P("leaf", "sec"),
-        P(("leaf", "sec"), None),
-        P(("leaf", "sec"), None),
-        P(("leaf", "sec")),
-        P(("leaf", "sec"), None),
-        P(("leaf", "sec"), None),
-        P(None, ("leaf", "sec"), None),
-        P(None, ("leaf", "sec"), None),
-        P(None, ("leaf", "sec")),
+        rows,
+        rows,
+        P(AXES),
+        rows,
+        rows,
+        P(None, AXES, None),
+        P(None, AXES, None),
+        P(None, AXES),
     )
-    out_specs = (P(("leaf", "sec"), None), P(None, ("leaf", "sec"), None))
-    return jax.shard_map(
-        on_device, mesh=mesh, in_specs=in_specs, out_specs=out_specs, check_vma=False
-    )
+    out_specs = (rows, P(None, AXES, None))
+    paired = mesh.shape["sec"] == 2 and mesh.shape["leaf"] % 8 == 0
+    program = on_device if paired else leafwise_on_device
+    return jax.shard_map(program, mesh=mesh, in_specs=in_specs, out_specs=out_specs, check_vma=False)

time: 198 us -> 44.5 us (0.22)
  waiting for transfers between devices: 106 us -> 10.7 us
  starting transfers between devices: 48.4 us -> 14.2 us
  between operations: 15.3 us -> 1.44 us
  blocking collectives: 11 us -> 0 us
  Pallas kernels: 0 us -> 8.75 us
  local copies, waits for them, and re-layouts: 9.96 us -> 4.29 us
    ppermute x24 -> x15, waiting for transfers between devices: 54.5 us -> 10.7 us  [the longest x7 10.3 us: to_chips(): return lax.ppermute(block, AXES, route)]
    unnamed x10 -> x0, waiting for transfers between devices: 34.7 us -> none
    ppermute x24 -> x15, starting transfers between devices: 48.1 us -> 14.2 us  [the longest x7 10.6 us: to_chips(): return lax.ppermute(block, AXES, route)]
    reduce_scatter x2 -> x0, waiting for transfers between devices: 17.1 us -> none  [group_reduce(): return lax.psum_scatter(reduced, 'sec', scatter_dimension=0, tiled=True)]
    all_gather x6 -> x0, blocking collectives: 11 us -> none  [group_gather(): block = lax.all_gather(piece, 'sec', axis=0, tiled=True)]
    pallas_call x0 -> x3, Pallas kernels: none -> 8.75 us  [the longest x1 4.39 us: on_device(): pl.pallas_call(functools.partial(top_kernel, levels, unit, meta), out_sha...]
    unnamed x29 -> x31, local copies, waits for them, and re-layouts: 9.61 us -> 1.6 us
    dot_general x13 -> x1, matrix products: 4.53 us -> 3.72 us  [transposed_dot(): lax.dot_general(matrix, vector, (((0,), (0,)), ((), ())), preferred_eleme...]
  transfers between devices with their start and end apart: 30 -> 15, of which waited for: 30 -> 5; matrix products, arithmetic and copies ran while one was open for 1% -> 7% of each run, Pallas kernels for 0% -> 6%
where the time goes in v1:
time: 44.5 us; the launch traced here: 44.1 us
  starting transfers between devices  14.2 us (32%)
  waiting for transfers between devices  10.7 us (24%)
  Pallas kernels  8.75 us (20%)
  local copies, waits for them, and re-layouts  4.29 us (10%)
  matrix products  3.72 us (8%)
  between operations  1.44 us (3%)
  other arithmetic  0.95 us (2%)
    ppermute x7, starting transfers between devices, to_chips(): return lax.ppermute(block, AXES, route)  10.6 us
    ppermute x7, waiting for transfers between devices, to_chips(): return lax.ppermute(block, AXES, route)  10.3 us
    pallas_call x1, Pallas kernels, on_device(): pl.pallas_call(functools.partial(top_kernel, levels, unit, meta), out_sha...  4.39 us
    dot_general x1, matrix products, transposed_dot(): lax.dot_general(matrix, vector, (((0,), (0,)), ((), ())), preferred_eleme...  3.72 us
    ppermute x8, starting transfers between devices, to_sections(): lax.ppermute(block, 'sec', [(s, (s - turn) % sections) for s in range(sec...  3.6 us
    pallas_call x1, Pallas kernels, on_device(): pl.pallas_call(functools.partial(low_kernel, levels, unit, meta), out_sha...  2.55 us
    pallas_call x1, Pallas kernels, on_device(): pl.pallas_call(functools.partial(pack_kernel, levels), grid=(1,), out_sha...  1.81 us
    unnamed x31, local copies, waits for them, and re-layouts  1.6 us
  transfers between devices with their start and end apart: 15, of which 5 were waited for; matrix products, arithmetic and copies ran while one was open for 7% of the time, Pallas kernels for 6%

profile of v1, /device:TPU:0, one launch (start us, length us, event | category | flops | bytes accessed | tf_op | source)
XLA Modules:
  0.0 44.1 jit_solution(1289715113573426830)
XLA Ops:
  0.6 0.0 copy-start.13
  1.3 1.8 %pack.1 = (bf16[32,1408]{1,0:T(8,128)(2,1)}, bf16[32,1280]{1,0:T(8,128)(2,1)}) custom-call(s32[1,1]{1,0:T(1,128)S(6)} %copy.15.blocks_ref, bf16[1024,1024]{1,0:T(8,128)(2,1)} %leaf_ref.1, bf16[1024,128]{1,0:T(8,128)(2,1)} %shift_ref.1, bf16[32,896]{1,0:T(8,128)(2,1)} %panel_ref.1, bf16[32,896]{1,0:T(8,128)(2,1)} %inv_ref.1, bf16[3,32,128]{2,1,0:T(8,128)(2,1)} %rhs_ref.1, ...), custom_call_target="tpu_custom_call" | custom-call | tf_op jit(solution)/shard_map/pack/pallas_call | solution.py:301
  3.1 0.5 %collective-permute-start.6 = (bf16[32,1280]{1,0:T(8,128)(2,1)}, bf16[32,1280]{1,0:T(8,128)(2,1)S(1)}, u32[]{:S(2)}, u32[]{:S(2)}) collective-permute-start(bf16[32,1280]{1,0:T(8,128)(2,1)} %get-tuple-element.13.refs_2_), channel_id=1, source_target_pairs={{0,1},{1,0},{2,3},{3,2},{4,5},{5,4},{6,7},{7,6},{8,9},{9,8},{10,11... | collective-permute-start | bytes 245768 | tf_op jit(solution)/shard_map/ppermute | solution.py:26
  3.6 2.6 %collective-permute-start.7 = (bf16[32,1280]{1,0:T(8,128)(2,1)}, bf16[32,1280]{1,0:T(8,128)(2,1)S(1)}, u32[]{:S(2)}, u32[]{:S(2)}) collective-permute-start(bf16[32,1280]{1,0:T(8,128)(2,1)} %get-tuple-element.13.refs_2_), channel_id=1, source_target_pairs={{0,8},{1,9},{2,10},{3,11},{4,12},{5,13},{6,14},{7,15},{8,0},{9,1},... | collective-permute-start | bytes 245768 | tf_op jit(solution)/shard_map/ppermute | solution.py:21
  6.3 0.2 collective-permute-start
  6.4 0.9 %constant_dynamic-update-slice_fusion.1 = bf16[64,1280]{1,0:T(8,128)(2,1)S(1)} fusion(bf16[32,1280]{1,0:T(8,128)(2,1)} %get-tuple-element.13.refs_2_), kind=kLoop, calls=%fused_computation.18 | loop fusion | bytes 163840
  7.3 0.4 collective-permute-done.refs_1_
  7.8 0.9 %pad_maximum_fusion = bf16[64,1408]{1,0:T(8,128)(2,1)S(1)} fusion(bf16[32,1408]{1,0:T(8,128)(2,1)S(1)} %collective-permute-done.refs_1_, bf16[32,1408]{1,0:T(8,128)(2,1)} %get-tuple-element.9.refs_0_), kind=kLoop, calls=%fused_computation.15 | loop fusion | flops 360448 | bytes 360448 | tf_op jit(solution)/shard_map/concatenate | solution.py:333
  8.7 1.6 %collective-permute-start.1 = (bf16[64,1408]{1,0:T(8,128)(2,1)S(1)}, bf16[64,1408]{1,0:T(8,128)(2,1)S(1)}, u32[]{:S(2)}, u32[]{:S(2)}) collective-permute-start(bf16[64,1408]{1,0:T(8,128)(2,1)S(1)} %pad_maximum_fusion), channel_id=1, source_target_pairs={{0,2},{1,5},{2,0},{3,7},{4,6},{5,1},{6,4},{7,3},{8,10},{9,13},{10,... | collective-permute-start | bytes 540680 | tf_op jit(solution)/shard_map/ppermute | solution.py:21
  10.3 0.0 collective-permute-done.6.refs_3_
  10.3 0.1 collective-permute-start.9
  10.4 3.8 %collective-permute-start.11 = (bf16[64,1280]{1,0:T(8,128)(2,1)S(1)}, bf16[64,1280]{1,0:T(8,128)(2,1)S(1)}, u32[]{:S(2)}, u32[]{:S(2)}) collective-permute-start(bf16[64,1280]{1,0:T(8,128)(2,1)S(1)} %constant_dynamic-update-slice_fusion), channel_id=1, source_target_pairs={{0,14},{1,3},{2,12},{3,1},{4,10},{5,7},{6,8},{7,5},{8,6},{9,11},{1... | collective-permute-start | bytes 491528 | tf_op jit(solution)/shard_map/ppermute | solution.py:21
  14.2 0.5 %collective-permute-start.13 = (bf16[64,1280]{1,0:T(8,128)(2,1)S(1)}, bf16[64,1280]{1,0:T(8,128)(2,1)S(1)}, u32[]{:S(2)}, u32[]{:S(2)}) collective-permute-start(bf16[64,1280]{1,0:T(8,128)(2,1)S(1)} %constant_dynamic-update-slice_fusion), channel_id=1, source_target_pairs={{0,4},{1,7},{2,6},{3,5},{4,0},{5,3},{6,2},{7,1},{8,12},{9,15},{10,... | collective-permute-start | bytes 491528 | tf_op jit(solution)/shard_map/ppermute | solution.py:21
  14.7 0.0 collective-permute-done.7.refs_4_
  14.8 1.5 %collective-permute-start.3 = (bf16[32,1408]{1,0:T(8,128)(2,1)}, bf16[32,1408]{1,0:T(8,128)(2,1)}, u32[]{:S(2)}, u32[]{:S(2)}) collective-permute-start(bf16[32,1408]{1,0:T(8,128)(2,1)} %get-tuple-element.9.refs_0_), channel_id=1, source_target_pairs={{0,6},{1,7},{2,4},{3,5},{4,2},{5,3},{6,0},{7,1},{8,14},{9,15},{10,... | collective-permute-start | bytes 270344 | tf_op jit(solution)/shard_map/ppermute | solution.py:21
  16.2 0.0 copy-done.10
  16.2 2.1 %collective-permute-done.1.refs_2_ = bf16[64,1408]{1,0:T(8,128)(2,1)S(1)} collective-permute-done((bf16[64,1408]{1,0:T(8,128)(2,1)S(1)}, bf16[64,1408]{1,0:T(8,128)(2,1)S(1)}, u32[]{:S(2)}, u32[]{:S(2)}) %collective-permute-start.1) | collective-permute-done | bytes 180256 | tf_op jit(solution)/shard_map/ppermute | solution.py:21
  18.4 0.0 collective-permute-start.2
  18.4 3.9 %collective-permute-done.3.refs_4_ = bf16[32,1408]{1,0:T(8,128)(2,1)} collective-permute-done((bf16[32,1408]{1,0:T(8,128)(2,1)}, bf16[32,1408]{1,0:T(8,128)(2,1)}, u32[]{:S(2)}, u32[]{:S(2)}) %collective-permute-start.3) | collective-permute-done | bytes 90144 | tf_op jit(solution)/shard_map/ppermute | solution.py:21
  22.3 1.9 %collective-permute-start.4 = (bf16[32,1408]{1,0:T(8,128)(2,1)}, bf16[32,1408]{1,0:T(8,128)(2,1)}, u32[]{:S(2)}, u32[]{:S(2)}) collective-permute-start(bf16[32,1408]{1,0:T(8,128)(2,1)} %collective-permute-done.3.refs_4_), channel_id=1, source_target_pairs={{0,1},{1,0},{2,3},{3,2},{4,5},{5,4},{6,7},{7,6},{8,9},{9,8},{10,11... | collective-permute-start | bytes 270344 | tf_op jit(solution)/shard_map/ppermute | solution.py:26
  24.2 0.0 collective-permute-done.9.refs_6_
  24.2 0.1 collective-permute-start.10
  24.3 0.0 collective-permute-done.11.refs_8_
  24.3 0.4 collective-permute-start.12
  24.7 0.3 collective-permute-done.13.refs_10_
  25.0 0.0 collective-permute-start.14
  25.0 0.0 copy-done.13
  25.0 0.7 %stack.139.place_ref = s32[8]{0:T(128)} concatenate(s32[1]{0:T(128)} %bitcast.27, s32[1]{0:T(128)} %bitcast.28, s32[1]{0:T(128)} %bitcast.29, s32[1]{0:T(128)} %bitcast.30, s32[1]{0:T(128)} %bitcast.31, s32[1]{0:T(128)} %bitcast.32, s32[1]{0:T(128)} %bitcast.33, s32[1]{0:T(128)} %bitcast.34), dimensions={0} | concatenate | bytes 64 | tf_op jit(solution)/shard_map/stack | solution.py:362
  25.7 0.6 %stack.130.place_ref = s32[26]{0:T(128)} concatenate(s32[1]{0:T(128)} %bitcast.2, s32[1]{0:T(128)} %bitcast.3, s32[1]{0:T(128)} %bitcast.4, s32[1]{0:T(128)} %bitcast.5, s32[1]{0:T(128)} %bitcast.6, s32[1]{0:T(128)} %bitcast.7, s32[1]{0:T(128)} %bitcast.8, s32[1]{0:T(128)} %bitcast.9, s32[1]{0:T(128)} %bitcast.10, s32[1]{0:T(128)} %bitcast.11, s32[1]{0:T(128)} %bitcast.12, ...), dimensions={0} | concatenate | bytes 208 | tf_op jit(solution)/shard_map/stack | solution.py:389
  26.3 0.0 collective-permute-done.4.refs_5_
  26.4 0.5 %collective-permute-start.8 = (bf16[32,1280]{1,0:T(8,128)(2,1)}, bf16[32,1280]{1,0:T(8,128)(2,1)S(1)}, u32[]{:S(2)}, u32[]{:S(2)}) collective-permute-start(bf16[32,1280]{1,0:T(8,128)(2,1)} %copy-done.10), channel_id=1, source_target_pairs={{0,1},{1,0},{2,3},{3,2},{4,5},{5,4},{6,7},{7,6},{8,9},{9,8},{10,11... | collective-permute-start | bytes 245768 | tf_op jit(solution)/shard_map/ppermute | solution.py:26
  26.8 0.0 collective-permute-done.2.refs_3_
  26.8 0.0 copy-done.1
  26.9 0.7 %copy-done.5 = bf16[64,1408]{1,0:T(8,128)(2,1)} copy-done((bf16[64,1408]{1,0:T(8,128)(2,1)}, bf16[64,1408]{1,0:T(8,128)(2,1)S(1)}, u32[]{:S(2)}) %copy-start.5) | copy-done | bytes 180248
  27.5 2.5 %low.1 = (bf16[256,1408]{1,0:T(8,128)(2,1)}, bf16[256,128]{1,0:T(8,128)(2,1)}, bf16[256,128]{1,0:T(8,128)(2,1)}) custom-call(s32[8]{0:T(128)} %stack.139.place_ref, bf16[32,1408]{1,0:T(8,128)(2,1)} %get-tuple-element.9.refs_0_, bf16[32,1408]{1,0:T(8,128)(2,1)} %copy-done.1, bf16[64,1408]{1,0:T(8,128)(2,1)} %copy-done.4, bf16[64,1408]{1,0:T(8,128)(2,1)} %copy-done.5, ...), custom_call_target="tpu_custom_call" | custom-call | tf_op jit(solution)/shard_map/low/pallas_call | solution.py:363
  30.1 0.4 %collective-permute-start.5 = (bf16[256,128]{1,0:T(8,128)(2,1)}, bf16[256,128]{1,0:T(8,128)(2,1)S(1)}, u32[]{:S(2)}, u32[]{:S(2)}) collective-permute-start(bf16[256,128]{1,0:T(8,128)(2,1)} %get-tuple-element.11.refs_1_), channel_id=1, source_target_pairs={{0,8},{1,9},{2,10},{3,11},{4,12},{5,13},{6,14},{7,15},{8,0},{9,1},... | collective-permute-start | bytes 196616 | tf_op jit(solution)/shard_map/ppermute | solution.py:21
  30.5 0.0 collective-permute-done.8.refs_5_
  30.5 0.0 collective-permute-done.10.refs_7_
  30.5 0.0 copy-start.9
  30.6 0.0 collective-permute-done.12.refs_9_
  30.6 0.0 collective-permute-done.14.refs_11_
  30.6 4.0 %collective-permute-done.5.partner_ref = bf16[256,128]{1,0:T(8,128)(2,1)S(1)} collective-permute-done((bf16[256,128]{1,0:T(8,128)(2,1)}, bf16[256,128]{1,0:T(8,128)(2,1)S(1)}, u32[]{:S(2)}, u32[]{:S(2)}) %collective-permute-start.5) | collective-permute-done | bytes 65568 | tf_op jit(solution)/shard_map/ppermute | solution.py:21
  34.5 1.4 %broadcast_in_dim.47.dev_ref = bf16[3,32,128]{2,1,0:T(8,128)(2,1)} broadcast(bf16[3,32]{1,0:T(4,128)(2,1)} %param.19), dimensions={0,1} | broadcast | bytes 24768 | tf_op jit(solution)/shard_map/broadcast_in_dim | solution.py:407
  35.9 0.0 copy-done.2
  35.9 0.0 copy-done.7
  36.0 4.4 %top.1 = (bf16[3,32,128]{2,1,0:T(8,128)(2,1)}, f32[32,128]{1,0:T(8,128)}) custom-call(s32[26]{0:T(128)} %stack.130.place_ref, bf16[256,1408]{1,0:T(8,128)(2,1)} %get-tuple-element.10.low_ref, bf16[3,32,128]{2,1,0:T(8,128)(2,1)} %broadcast_in_dim.47.dev_ref, bf16[256,128]{1,0:T(8,128)(2,1)} %copy-done.12, bf16[256,128]{1,0:T(8,128)(2,1)} %get-tuple-element.12.refs_0_, ...), custom_call_target="tpu_custom_call" | custom-call | tf_op jit(solution)/shard_map/top/pallas_call | solution.py:391
  40.4 0.0 copy-done
  40.4 3.7 %fusion.6 = bf16[1024,128]{1,0:T(8,128)(2,1)} fusion(bf16[1024,1024]{1,0:T(8,128)(2,1)S(1)} %copy-done, f32[32,128]{1,0:T(8,128)} %get-tuple-element.14, bf16[1024,128]{1,0:T(8,128)(2,1)S(1)} %copy-done.14, bf16[1024,128]{1,0:T(8,128)(2,1)S(1)} %copy-done.3, f32[1024]{0:T(1024)S(1)} %convert_element_type.26, pred[1024]{0:T(1024)(128)(4,1)S(1)} %iota_compare_fusion), kind=kOutput, calls=%fused_computation.8 | convolution fusion | flops 538443776 | bytes 2905088 | tf_op jit(solution)/shard_map/dot_general | solution.py:88
  (24 shorter events, 0.1 us)
Async XLA Ops:
  0.6 24.4 %copy-start.13 = (bf16[1024]{0:T(1024)(128)(2,1)S(1)}, bf16[1024]{0:T(1024)(128)(2,1)}, u32[]{:S(2)}) copy-start(bf16[1024]{0:T(1024)(128)(2,1)} %param.14) | copy-start | bytes 6148
  3.1 37.2 %copy-start = (bf16[1024,1024]{1,0:T(8,128)(2,1)S(1)}, bf16[1024,1024]{1,0:T(8,128)(2,1)}, u32[]{:S(2)}) copy-start(bf16[1024,1024]{1,0:T(8,128)(2,1)} %leaf_ref.1) | copy-start | bytes 6291460
  3.1 37.2 %copy-start.3 = (bf16[1024,128]{1,0:T(8,128)(2,1)S(1)}, bf16[1024,128]{1,0:T(8,128)(2,1)}, u32[]{:S(2)}) copy-start(bf16[1024,128]{1,0:T(8,128)(2,1)} %shift_ref.1) | copy-start | bytes 786436
  3.1 7.2 %collective-permute-start.6 = (bf16[32,1280]{1,0:T(8,128)(2,1)}, bf16[32,1280]{1,0:T(8,128)(2,1)S(1)}, u32[]{:S(2)}, u32[]{:S(2)}) collective-permute-start(bf16[32,1280]{1,0:T(8,128)(2,1)} %get-tuple-element.13.refs_2_), channel_id=1, source_target_pairs={{0,1},{1,0},{2,3},{3,2},{4,5},{5,4},{6,7},{7,6},{8,9},{9,8},{10,11... | collective-permute-start | bytes 245768 | tf_op jit(solution)/shard_map/ppermute | solution.py:26
  3.6 11.1 %collective-permute-start.7 = (bf16[32,1280]{1,0:T(8,128)(2,1)}, bf16[32,1280]{1,0:T(8,128)(2,1)S(1)}, u32[]{:S(2)}, u32[]{:S(2)}) collective-permute-start(bf16[32,1280]{1,0:T(8,128)(2,1)} %get-tuple-element.13.refs_2_), channel_id=1, source_target_pairs={{0,8},{1,9},{2,10},{3,11},{4,12},{5,13},{6,14},{7,15},{8,0},{9,1},... | collective-permute-start | bytes 245768 | tf_op jit(solution)/shard_map/ppermute | solution.py:21
  6.3 1.5 %collective-permute-start = (bf16[32,1408]{1,0:T(8,128)(2,1)}, bf16[32,1408]{1,0:T(8,128)(2,1)S(1)}, u32[]{:S(2)}, u32[]{:S(2)}) collective-permute-start(bf16[32,1408]{1,0:T(8,128)(2,1)} %get-tuple-element.9.refs_0_), channel_id=1, source_target_pairs={{0,1},{1,0},{2,3},{3,2},{4,5},{5,4},{6,7},{7,6},{8,9},{9,8},{10,11... | collective-permute-start | bytes 270344 | tf_op jit(solution)/shard_map/ppermute | solution.py:26
  7.8 19.1 %copy-start.1 = (bf16[32,1408]{1,0:T(8,128)(2,1)}, bf16[32,1408]{1,0:T(8,128)(2,1)S(1)}, u32[]{:S(2)}) copy-start(bf16[32,1408]{1,0:T(8,128)(2,1)S(1)} %collective-permute-done.refs_1_) | copy-start | bytes 270340
  8.7 9.7 %collective-permute-start.1 = (bf16[64,1408]{1,0:T(8,128)(2,1)S(1)}, bf16[64,1408]{1,0:T(8,128)(2,1)S(1)}, u32[]{:S(2)}, u32[]{:S(2)}) collective-permute-start(bf16[64,1408]{1,0:T(8,128)(2,1)S(1)} %pad_maximum_fusion), channel_id=1, source_target_pairs={{0,2},{1,5},{2,0},{3,7},{4,6},{5,1},{6,4},{7,3},{8,10},{9,13},{10,... | collective-permute-start | bytes 540680 | tf_op jit(solution)/shard_map/ppermute | solution.py:21
  10.3 25.6 %copy-start.2 = (bf16[32,1280]{1,0:T(8,128)(2,1)}, bf16[32,1280]{1,0:T(8,128)(2,1)S(1)}, u32[]{:S(2)}) copy-start(bf16[32,1280]{1,0:T(8,128)(2,1)S(1)} %collective-permute-done.6.refs_3_) | copy-start | bytes 245764
  10.3 13.9 %collective-permute-start.9 = (bf16[64,1280]{1,0:T(8,128)(2,1)S(1)}, bf16[64,1280]{1,0:T(8,128)(2,1)S(1)}, u32[]{:S(2)}, u32[]{:S(2)}) collective-permute-start(bf16[64,1280]{1,0:T(8,128)(2,1)S(1)} %constant_dynamic-update-slice_fusion), channel_id=1, source_target_pairs={{0,10},{1,13},{2,8},{3,15},{4,14},{5,9},{6,12},{7,11},{8,2},{9,5},... | collective-permute-start | bytes 491528 | tf_op jit(solution)/shard_map/ppermute | solution.py:21
  10.4 13.8 %collective-permute-start.11 = (bf16[64,1280]{1,0:T(8,128)(2,1)S(1)}, bf16[64,1280]{1,0:T(8,128)(2,1)S(1)}, u32[]{:S(2)}, u32[]{:S(2)}) collective-permute-start(bf16[64,1280]{1,0:T(8,128)(2,1)S(1)} %constant_dynamic-update-slice_fusion), channel_id=1, source_target_pairs={{0,14},{1,3},{2,12},{3,1},{4,10},{5,7},{6,8},{7,5},{8,6},{9,11},{1... | collective-permute-start | bytes 491528 | tf_op jit(solution)/shard_map/ppermute | solution.py:21
  14.2 10.8 %collective-permute-start.13 = (bf16[64,1280]{1,0:T(8,128)(2,1)S(1)}, bf16[64,1280]{1,0:T(8,128)(2,1)S(1)}, u32[]{:S(2)}, u32[]{:S(2)}) collective-permute-start(bf16[64,1280]{1,0:T(8,128)(2,1)S(1)} %constant_dynamic-update-slice_fusion), channel_id=1, source_target_pairs={{0,4},{1,7},{2,6},{3,5},{4,0},{5,3},{6,2},{7,1},{8,12},{9,15},{10,... | collective-permute-start | bytes 491528 | tf_op jit(solution)/shard_map/ppermute | solution.py:21
  14.7 1.5 %copy-start.10 = (bf16[32,1280]{1,0:T(8,128)(2,1)}, bf16[32,1280]{1,0:T(8,128)(2,1)S(1)}, u32[]{:S(2)}) copy-start(bf16[32,1280]{1,0:T(8,128)(2,1)S(1)} %collective-permute-done.7.refs_4_) | copy-start | bytes 245764
  14.8 7.5 %collective-permute-start.3 = (bf16[32,1408]{1,0:T(8,128)(2,1)}, bf16[32,1408]{1,0:T(8,128)(2,1)}, u32[]{:S(2)}, u32[]{:S(2)}) collective-permute-start(bf16[32,1408]{1,0:T(8,128)(2,1)} %get-tuple-element.9.refs_0_), channel_id=1, source_target_pairs={{0,6},{1,7},{2,4},{3,5},{4,2},{5,3},{6,0},{7,1},{8,14},{9,15},{10,... | collective-permute-start | bytes 270344 | tf_op jit(solution)/shard_map/ppermute | solution.py:21
  18.4 8.5 %copy-start.4 = (bf16[64,1408]{1,0:T(8,128)(2,1)}, bf16[64,1408]{1,0:T(8,128)(2,1)S(1)}, u32[]{:S(2)}) copy-start(bf16[64,1408]{1,0:T(8,128)(2,1)S(1)} %collective-permute-done.1.refs_2_) | copy-start | bytes 540676
  18.4 8.4 %collective-permute-start.2 = (bf16[64,1408]{1,0:T(8,128)(2,1)S(1)}, bf16[64,1408]{1,0:T(8,128)(2,1)S(1)}, u32[]{:S(2)}, u32[]{:S(2)}) collective-permute-start(bf16[64,1408]{1,0:T(8,128)(2,1)S(1)} %collective-permute-done.1.refs_2_), channel_id=1, source_target_pairs={{0,1},{1,0},{2,3},{3,2},{4,5},{5,4},{6,7},{7,6},{8,9},{9,8},{10,11... | collective-permute-start | bytes 540680 | tf_op jit(solution)/shard_map/ppermute | solution.py:26
  22.3 4.1 %collective-permute-start.4 = (bf16[32,1408]{1,0:T(8,128)(2,1)}, bf16[32,1408]{1,0:T(8,128)(2,1)}, u32[]{:S(2)}, u32[]{:S(2)}) collective-permute-start(bf16[32,1408]{1,0:T(8,128)(2,1)} %collective-permute-done.3.refs_4_), channel_id=1, source_target_pairs={{0,1},{1,0},{2,3},{3,2},{4,5},{5,4},{6,7},{7,6},{8,9},{9,8},{10,11... | collective-permute-start | bytes 270344 | tf_op jit(solution)/shard_map/ppermute | solution.py:26
  24.2 11.7 %copy-start.6 = (bf16[64,1280]{1,0:T(8,128)(2,1)}, bf16[64,1280]{1,0:T(8,128)(2,1)S(1)}, u32[]{:S(2)}) copy-start(bf16[64,1280]{1,0:T(8,128)(2,1)S(1)} %collective-permute-done.9.refs_6_) | copy-start | bytes 491524
  24.2 6.4 %collective-permute-start.10 = (bf16[64,1280]{1,0:T(8,128)(2,1)S(1)}, bf16[64,1280]{1,0:T(8,128)(2,1)S(1)}, u32[]{:S(2)}, u32[]{:S(2)}) collective-permute-start(bf16[64,1280]{1,0:T(8,128)(2,1)S(1)} %collective-permute-done.9.refs_6_), channel_id=1, source_target_pairs={{0,1},{1,0},{2,3},{3,2},{4,5},{5,4},{6,7},{7,6},{8,9},{9,8},{10,11... | collective-permute-start | bytes 491528 | tf_op jit(solution)/shard_map/ppermute | solution.py:26
  24.3 11.7 %copy-start.7 = (bf16[64,1280]{1,0:T(8,128)(2,1)}, bf16[64,1280]{1,0:T(8,128)(2,1)S(1)}, u32[]{:S(2)}) copy-start(bf16[64,1280]{1,0:T(8,128)(2,1)S(1)} %collective-permute-done.11.refs_8_) | copy-start | bytes 491524
  24.3 6.3 %collective-permute-start.12 = (bf16[64,1280]{1,0:T(8,128)(2,1)S(1)}, bf16[64,1280]{1,0:T(8,128)(2,1)}, u32[]{:S(2)}, u32[]{:S(2)}) collective-permute-start(bf16[64,1280]{1,0:T(8,128)(2,1)S(1)} %collective-permute-done.11.refs_8_), channel_id=1, source_target_pairs={{0,1},{1,0},{2,3},{3,2},{4,5},{5,4},{6,7},{7,6},{8,9},{9,8},{10,11... | collective-permute-start | bytes 491528 | tf_op jit(solution)/shard_map/ppermute | solution.py:26
  25.0 10.9 %copy-start.8 = (bf16[64,1280]{1,0:T(8,128)(2,1)}, bf16[64,1280]{1,0:T(8,128)(2,1)S(1)}, u32[]{:S(2)}) copy-start(bf16[64,1280]{1,0:T(8,128)(2,1)S(1)} %collective-permute-done.13.refs_10_) | copy-start | bytes 491524
  25.0 5.6 %collective-permute-start.14 = (bf16[64,1280]{1,0:T(8,128)(2,1)S(1)}, bf16[64,1280]{1,0:T(8,128)(2,1)}, u32[]{:S(2)}, u32[]{:S(2)}) collective-permute-start(bf16[64,1280]{1,0:T(8,128)(2,1)S(1)} %collective-permute-done.13.refs_10_), channel_id=1, source_target_pairs={{0,1},{1,0},{2,3},{3,2},{4,5},{5,4},{6,7},{7,6},{8,9},{9,8},{10,11... | collective-permute-start | bytes 491528 | tf_op jit(solution)/shard_map/ppermute | solution.py:26
  26.4 4.2 %collective-permute-start.8 = (bf16[32,1280]{1,0:T(8,128)(2,1)}, bf16[32,1280]{1,0:T(8,128)(2,1)S(1)}, u32[]{:S(2)}, u32[]{:S(2)}) collective-permute-start(bf16[32,1280]{1,0:T(8,128)(2,1)} %copy-done.10), channel_id=1, source_target_pairs={{0,1},{1,0},{2,3},{3,2},{4,5},{5,4},{6,7},{7,6},{8,9},{9,8},{10,11... | collective-permute-start | bytes 245768 | tf_op jit(solution)/shard_map/ppermute | solution.py:26
  26.9 0.7 %copy-start.5 = (bf16[64,1408]{1,0:T(8,128)(2,1)}, bf16[64,1408]{1,0:T(8,128)(2,1)S(1)}, u32[]{:S(2)}) copy-start(bf16[64,1408]{1,0:T(8,128)(2,1)S(1)} %collective-permute-done.2.refs_3_) | copy-start | bytes 540676
  30.1 10.3 %copy-start.14 = (bf16[1024,128]{1,0:T(8,128)(2,1)S(1)}, bf16[1024,128]{1,0:T(8,128)(2,1)}, u32[]{:S(2)}) copy-start(bf16[1024,128]{1,0:T(8,128)(2,1)} %param.13) | copy-start | bytes 786436
  30.1 4.5 %collective-permute-start.5 = (bf16[256,128]{1,0:T(8,128)(2,1)}, bf16[256,128]{1,0:T(8,128)(2,1)S(1)}, u32[]{:S(2)}, u32[]{:S(2)}) collective-permute-start(bf16[256,128]{1,0:T(8,128)(2,1)} %get-tuple-element.11.refs_1_), channel_id=1, source_target_pairs={{0,8},{1,9},{2,10},{3,11},{4,12},{5,13},{6,14},{7,15},{8,0},{9,1},... | collective-permute-start | bytes 196616 | tf_op jit(solution)/shard_map/ppermute | solution.py:21
  30.5 5.4 %copy-start.11 = (bf16[32,1280]{1,0:T(8,128)(2,1)}, bf16[32,1280]{1,0:T(8,128)(2,1)S(1)}, u32[]{:S(2)}) copy-start(bf16[32,1280]{1,0:T(8,128)(2,1)S(1)} %collective-permute-done.8.refs_5_) | copy-start | bytes 245764
  30.5 5.4 %copy-start.9 = (bf16[64,1280]{1,0:T(8,128)(2,1)}, bf16[64,1280]{1,0:T(8,128)(2,1)S(1)}, u32[]{:S(2)}) copy-start(bf16[64,1280]{1,0:T(8,128)(2,1)S(1)} %collective-permute-done.10.refs_7_) | copy-start | bytes 491524
  34.5 1.4 %copy-start.12 = (bf16[256,128]{1,0:T(8,128)(2,1)}, bf16[256,128]{1,0:T(8,128)(2,1)S(1)}, u32[]{:S(2)}) copy-start(bf16[256,128]{1,0:T(8,128)(2,1)S(1)} %collective-permute-done.5.partner_ref) | copy-start | bytes 196612

commit v2 on v0

--- a/solution.py
+++ b/solution.py
@@ -1,9 +1,228 @@
+import functools
+
 import jax
 import jax.numpy as jnp
 from jax import lax
+from jax.experimental import pallas as pl
+from jax.experimental.pallas import tpu as pltpu
 from jax.sharding import PartitionSpec as P
 
 BLOCK = 128
+AXES = ("leaf", "sec")
+
+
+def to_chips(block, distances):
+    leaves, sections = lax.axis_size("leaf"), lax.axis_size("sec")
+    route = []
+    for leaf in range(leaves):
+        for section, distance in enumerate(distances):
+            route.append((leaf * sections + section, (leaf ^ distance) * sections + section))
+    return lax.ppermute(block, AXES, route)
+
+
+def column_of(row):
+    count = row.shape[1]
+    across = lax.broadcasted_iota(jnp.int32, (count, count), 1)
+    down = lax.broadcasted_iota(jnp.int32, (count, count), 0)
+    return jnp.sum(jnp.where(across == down, row, jnp.zeros_like(row)), axis=1, keepdims=True)
+
+
+def live_rows(blocks_ref, rows, columns):
+    live_from = rows - blocks_ref[0:1, 0:columns] * BLOCK
+    return lax.broadcasted_iota(jnp.int32, (rows, columns), 0) >= live_from
+
+
+def pack_kernel(
+    levels,
+    blocks_ref,
+    leaf_ref,
+    shift_ref,
+    panel_ref,
+    inv_ref,
+    rhs_ref,
+    noise_ref,
+    pack_ref,
+    edge_ref,
+    moved_ref,
+    arrived,
+):
+    row_count, samples = edge_ref.shape[0], shift_ref.shape[1]
+    subtree_rows = shift_ref.shape[0]
+    copies = [
+        pltpu.make_async_copy(shift_ref, moved_ref, arrived.at[0]),
+        pltpu.make_async_copy(leaf_ref.at[pl.ds(subtree_rows - row_count, row_count)], edge_ref, arrived.at[1]),
+    ]
+    at, offset = samples, 0
+    unit = panel_ref.shape[1] // (2 ** (levels + 1) - 2)
+    for height in range(1, levels + 1):
+        span = 2**height * unit
+        for source, width in (
+            (panel_ref.at[:, pl.ds(offset, span)], span),
+            (inv_ref.at[:, pl.ds(offset, span)], span),
+            (rhs_ref.at[height - 1], samples),
+            (noise_ref.at[height - 1], samples),
+        ):
+            copies.append(
+                pltpu.make_async_copy(source, pack_ref.at[:, pl.ds(at, width)], arrived.at[len(copies)])
+            )
+            at += width
+        offset += span
+    for copy in copies:
+        copy.start()
+    for copy in copies[:2]:
+        copy.wait()
+    shift = moved_ref[...]
+    shift = jnp.where(live_rows(blocks_ref, *shift.shape), shift, jnp.zeros_like(shift))
+    boundary = jnp.dot(edge_ref[...], shift, preferred_element_type=jnp.float32)
+    pack_ref[:, :samples] = boundary.astype(jnp.bfloat16)
+    for copy in copies[2:]:
+        copy.wait()
+
+
+def pair_kernel(own_ref, other_ref, low_ref, top_ref):
+    row_count = own_ref.shape[0]
+    columns = low_ref.shape[1]
+    for start, ref in ((0, own_ref), (row_count, other_ref)):
+        low_ref[start : start + row_count, :] = ref[:, :columns]
+        top_ref[start : start + row_count, :] = ref[:, columns:]
+
+
+def join_kernel(column, *refs):
+    joined_ref, row = refs[-1], 0
+    columns = joined_ref.shape[1]
+    for ref in refs[:-1]:
+        skipped = 0 if ref.shape[1] == columns else column
+        joined_ref[row : row + ref.shape[0], :] = ref[:, skipped : skipped + columns]
+        row += ref.shape[0]
+
+
+def place(pieces, refs, whole_ref, row_count, leaves, first_column):
+    columns = whole_ref.shape[1]
+    leaf, section = lax.axis_index("leaf"), lax.axis_index("sec")
+    for which, start, distances, turned in pieces:
+        if isinstance(turned, int):
+            owner = section ^ turned
+            distance = jnp.where(section == 0, distances[0], distances[1])
+        else:
+            owner, distance = turned[0], distances[0]
+        at = (((leaf ^ distance) & (leaves - 1)) * 2 + owner) * row_count
+        ref = refs[which]
+        skipped = 0 if ref.shape[1] == columns else first_column
+        whole_ref[pl.ds(pl.multiple_of(at, row_count), row_count), :] = ref[
+            start : start + row_count, skipped : skipped + columns
+        ]
+
+
+def solve_forward(whole, rows, at, span, samples, children):
+    panel = whole[rows, at : at + span]
+    inverse = whole[rows, at + span : at + 2 * span]
+    rhs = whole[rows, at + 2 * span : at + 2 * span + samples]
+    reduced = rhs.astype(jnp.float32) - jnp.dot(panel, children, preferred_element_type=jnp.float32)
+    reduced = reduced.astype(jnp.bfloat16)
+    return jnp.dot(inverse, reduced, preferred_element_type=jnp.float32).astype(jnp.bfloat16)
+
+
+def low_kernel(levels, unit, pieces, *refs):
+    piece_refs, (whole_ref, *solved_refs) = refs[:-levels], refs[-levels:]
+    row_count = unit // 2
+    place(pieces, piece_refs, whole_ref, row_count, 2 ** (levels - 1), 0)
+    samples = solved_refs[0].shape[1]
+    total = whole_ref.shape[0]
+    below_ref, at = whole_ref, samples
+    for height in range(1, levels):
+        span = 2**height * unit
+        for group in range(total // span):
+            rows = slice(group * span, (group + 1) * span)
+            children = below_ref[rows, 0:samples]
+            solved_refs[height - 1][rows, :] = solve_forward(whole_ref, rows, at, span, samples, children)
+        below_ref = solved_refs[height - 1]
+        at += 2 * span + 2 * samples
+
+
+def leaf_kernel(
+    row_count,
+    blocks_ref,
+    leaf_ref,
+    shift_ref,
+    noise_ref,
+    dev_ref,
+    base_ref,
+    edge_ref,
+    inner_ref,
+    scale_ref,
+):
+    rows, samples = shift_ref.shape
+    live = live_rows(blocks_ref, rows, samples)
+    shift = shift_ref[...]
+    shift = jnp.where(live, shift, jnp.zeros_like(shift))
+    zero = jnp.float32(0.0)
+    forward = jnp.dot(leaf_ref[...], shift, preferred_element_type=jnp.float32)
+    forward = jnp.where(live, forward, zero).astype(jnp.bfloat16)
+    summed = forward.astype(jnp.float32) + noise_ref[...].astype(jnp.float32)
+    inner = rows - row_count
+    edge_ref[...] = summed[inner:, :]
+    within = lax.broadcasted_iota(jnp.int32, (rows, samples), 0) < inner
+    weight = jnp.where(live & within, summed, zero)
+    product = jnp.dot(weight.T.astype(jnp.bfloat16), leaf_ref[...], preferred_element_type=jnp.float32)
+    base_ref[...] = product.T
+    inner_ref[...] = leaf_ref[inner:, :].astype(jnp.float32).T.astype(jnp.bfloat16)
+    for block in range(rows // BLOCK):
+        part = slice(block * BLOCK, (block + 1) * BLOCK)
+        column = column_of(dev_ref[:, part].astype(jnp.float32))
+        scale_ref[part, :] = jnp.where(live[part, :], jnp.broadcast_to(column, (BLOCK, samples)), zero)
+
+
+def top_kernel(levels, unit, pieces, *refs):
+    low_ref, dev_ref, partner_ref, base_ref, edge_ref, inner_ref, scale_ref = refs[:7]
+    solved_refs = refs[7 : 7 + levels - 1]
+    out_ref, sample_ref, whole_ref, child_ref, x_ref, sum_ref = refs[-6:]
+    piece_refs = refs[7 + levels - 1 : -6]
+    samples = partner_ref.shape[1]
+    row_count = unit // 2
+    leaf, section = lax.axis_index("leaf"), lax.axis_index("sec")
+    place(pieces, piece_refs, whole_ref, row_count, 2**levels, low_ref.shape[1])
+    half = partner_ref.shape[0]
+    upper = leaf >> (levels - 1) & 1
+    child_ref[pl.ds(pl.multiple_of(upper * half, half), half), :] = solved_refs[-1][...]
+    child_ref[pl.ds(pl.multiple_of((1 - upper) * half, half), half), :] = partner_ref[...]
+    top_span = 2**levels * unit
+    own = solve_forward(whole_ref, slice(0, top_span), 0, top_span, samples, child_ref[...])
+    correction = None
+    low_at = low_ref.shape[1]
+    for height in range(levels, 0, -1):
+        span = 2**height * unit
+        if height == levels:
+            source, at, rows = whole_ref, 0, slice(0, span)
+        else:
+            low_at -= 2 * span + 2 * samples
+            first = ((leaf & (2 ** (levels - 1) - 1)) >> height) * span
+            source, at, rows = low_ref, low_at, pl.ds(pl.multiple_of(first, span), span)
+            own = solved_refs[height - 1][rows, :]
+        noise = source[rows, at + 2 * span + samples : at + 2 * span + 2 * samples]
+        summed = (own.astype(jnp.float32) + noise.astype(jnp.float32)).T
+        if correction is not None:
+            summed = summed - correction
+        x = jnp.dot(
+            summed.astype(jnp.bfloat16), source[rows, at + span : at + 2 * span], preferred_element_type=jnp.float32
+        ).astype(jnp.bfloat16)
+        pushed = jnp.dot(x, source[rows, at : at + span], preferred_element_type=jnp.float32)
+        x_ref[0:span, :] = x.astype(jnp.float32).T
+        mine = pl.ds(pl.multiple_of(((leaf & (2**height - 1)) * 2 + section) * row_count, row_count), row_count)
+        scale = column_of(dev_ref[height - 1 : height, :].astype(jnp.float32))
+        sample_ref[height - 1] = (scale * x_ref[mine, :]).astype(jnp.bfloat16)
+        if height > 1:
+            upper = leaf >> (height - 1) & 1
+            correction = jnp.where(upper == 1, pushed[:, span // 2 :], pushed[:, : span // 2])
+        else:
+            sum_ref[...] = pushed.T
+            correction = sum_ref[mine, :]
+    weight = (edge_ref[...] - correction).astype(jnp.bfloat16)
+    back = base_ref[...] + jnp.dot(inner_ref[...], weight, preferred_element_type=jnp.float32)
+    out_ref[...] = (scale_ref[...] * back).astype(jnp.bfloat16)
+
+
+def transposed_dot(matrix, vector):
+    return lax.dot_general(matrix, vector, (((0,), (0,)), ((), ())), preferred_element_type=jnp.float32)
 
 
 def from_partner(block, axis, apart):
@@ -50,13 +269,7 @@
     return lax.psum_scatter(reduced, "sec", scatter_dimension=0, tiled=True)
 
 
-def transposed_product(matrix, vector):
-    return lax.dot_general(
-        matrix, vector, (((0,), (0,)), ((), ())), preferred_element_type=jnp.float32
-    )
-
-
-def on_device(
+def leafwise_on_device(
     leaf_inv,
     subtree_blocks,
     subtree_shift_rhs,
@@ -111,20 +324,20 @@
         if correction is not None:
             summed = summed - correction
         vector = summed.astype(jnp.bfloat16)
-        backed = group_reduce(transposed_product(inverse_block, vector), height).astype(
+        backed = group_reduce(transposed_dot(inverse_block, vector), height).astype(
             jnp.bfloat16
         )
         samples[height - 1] = (
             sep_dev[height - 1][:, None].astype(jnp.float32) * backed.astype(jnp.float32)
         ).astype(jnp.bfloat16)
-        correction = group_reduce(transposed_product(panel, backed), height)
+        correction = group_reduce(transposed_dot(panel, backed), height)
     leading = jnp.zeros((subtree_row_count - row_count, correction.shape[1]), jnp.float32)
     placed = jnp.concatenate([leading, correction], axis=0)
     subtree_summed = (
         subtree_forward_solution.astype(jnp.float32) + leaf_noise.astype(jnp.float32) - placed
     )
     subtree_weight = jnp.where(row_activity, subtree_summed, jnp.float32(0.0)).astype(jnp.bfloat16)
-    subtree_solution = transposed_product(leaf_inv, subtree_weight)
+    subtree_solution = transposed_dot(leaf_inv, subtree_weight)
     sample_scales = leaf_dev[:, None].astype(jnp.float32)
     subtree_scaled_samples = jnp.where(
         row_activity, sample_scales * subtree_solution, jnp.float32(0.0)
@@ -132,20 +345,180 @@
     return (subtree_scaled_samples, jnp.stack(samples))
 
 
+def on_device(
+    leaf_inv,
+    subtree_blocks,
+    subtree_shift_rhs,
+    leaf_noise,
+    leaf_dev,
+    sep_inv,
+    sep_panel,
+    sep_rhs,
+    sep_noise,
+    sep_dev,
+):
+    subtree_rows = leaf_inv.shape[0]
+    row_count = sep_inv.shape[0]
+    levels, _, samples = sep_rhs.shape
+    unit = 2 * row_count
+    vmem = pl.BlockSpec(memory_space=pltpu.VMEM)
+    short = pl.CostEstimate(flops=1, bytes_accessed=1, transcendentals=0)
+
+    def params(mib):
+        return pltpu.CompilerParams(vmem_limit_bytes=mib * 2**20)
+
+    top_columns = 2 * 2**levels * unit + 2 * samples
+    low_columns = samples + sum(2 * 2**h * unit + 2 * samples for h in range(1, levels))
+    hbm = pl.BlockSpec(memory_space=pltpu.HBM)
+
+    def in_hbm(array):
+        return pltpu.with_memory_space_constraint(array, pltpu.HBM)
+
+    blocks = jnp.broadcast_to(subtree_blocks, (8, samples))
+    pack = pl.pallas_call(
+        functools.partial(pack_kernel, levels),
+        out_shape=jax.ShapeDtypeStruct((row_count, low_columns + top_columns), jnp.bfloat16),
+        in_specs=[vmem] + [hbm] * 6,
+        out_specs=vmem,
+        scratch_shapes=[
+            pltpu.VMEM((row_count, subtree_rows), jnp.bfloat16),
+            pltpu.VMEM((subtree_rows, samples), jnp.bfloat16),
+            pltpu.SemaphoreType.DMA((2 + 4 * levels,)),
+        ],
+        compiler_params=params(4),
+        cost_estimate=short,
+        name="pack",
+    )(blocks, *(in_hbm(x) for x in (leaf_inv, subtree_shift_rhs, sep_panel, sep_inv, sep_rhs, sep_noise)))
+
+    def swap(block):
+        return lax.ppermute(block, "sec", [(0, 1), (1, 0)])
+
+    def join(arrays, columns, column, *after):
+        rows = sum(array.shape[0] for array in arrays)
+        return pl.pallas_call(
+            lambda *refs: join_kernel(column, *refs[len(after) :]),
+            out_shape=jax.ShapeDtypeStruct((rows, columns), jnp.bfloat16),
+            in_specs=[pl.BlockSpec(memory_space=pl.ANY)] * len(after) + [vmem] * len(arrays),
+            out_specs=vmem,
+            compiler_params=params(4),
+            cost_estimate=short,
+            name="join",
+        )(*after, *arrays)
+
+    pack_other = swap(pack)
+    low_pair, top_pair = pl.pallas_call(
+        pair_kernel,
+        out_shape=(
+            jax.ShapeDtypeStruct((unit, low_columns), jnp.bfloat16),
+            jax.ShapeDtypeStruct((unit, top_columns), jnp.bfloat16),
+        ),
+        in_specs=[vmem, vmem],
+        out_specs=(vmem, vmem),
+        compiler_params=params(4),
+        cost_estimate=short,
+        name="pair",
+    )(pack, pack_other)
+    third = to_chips(pack, (3, 3))
+    first = to_chips(low_pair, (1, 2))
+    both = lax.all_gather(join([third, first], low_columns, 0), "sec", axis=0, tiled=True)
+    own = [(pack, 0, (0, 0), 0), (pack_other, 0, (0, 0), 1)]
+    quarter = list(own)
+    for owner, distance in ((0, 1), (1, 2)):
+        row = 3 * row_count * owner
+        quarter.append((both, row, (3,), (owner,)))
+        quarter.append((both, row + row_count, (distance,), (owner,)))
+        quarter.append((both, row + 2 * row_count, (distance,), (1 - owner,)))
+
+    def listed(pieces):
+        arrays, places = [], []
+        for array, start, distances, turned in pieces:
+            if not any(array is known for known in arrays):
+                arrays.append(array)
+            which = [array is known for known in arrays].index(True)
+            places.append((which, start, distances, turned))
+        return arrays, places
+
+    arrays, places = listed(quarter)
+    quad = 2 ** (levels - 1)
+    low_whole, *solved = pl.pallas_call(
+        functools.partial(low_kernel, levels, unit, places),
+        out_shape=[jax.ShapeDtypeStruct((quad * unit, low_columns), jnp.bfloat16)]
+        + [jax.ShapeDtypeStruct((quad * unit, samples), jnp.bfloat16)] * (levels - 1),
+        in_specs=[vmem] * len(arrays),
+        out_specs=[vmem] * levels,
+        compiler_params=params(8),
+        cost_estimate=short,
+        name="low",
+    )(*arrays)
+    partner = to_chips(solved[-1], (quad, quad))
+
+    trips = [(pack, (3, 3)), (top_pair, (1, 2)), (top_pair, (4, 5)), (top_pair, (6, 7))]
+    arrived = [third] + [to_chips(block, distances) for block, distances in trips[1:]]
+    here = join(arrived, top_columns, low_columns, solved[-1])
+    there = swap(here)
+    far = own
+    row = 0
+    for block, (first, second) in trips:
+        for turned in range(block.shape[0] // row_count):
+            far.append((here, row, (first, second), turned))
+            far.append((there, row, (second, first), 1 - turned))
+            row += row_count
+
+    base, edge, inner, scale = pl.pallas_call(
+        functools.partial(leaf_kernel, row_count),
+        out_shape=(
+            jax.ShapeDtypeStruct((subtree_rows, samples), jnp.float32),
+            jax.ShapeDtypeStruct((row_count, samples), jnp.float32),
+            jax.ShapeDtypeStruct((subtree_rows, row_count), jnp.bfloat16),
+            jax.ShapeDtypeStruct((subtree_rows, samples), jnp.float32),
+        ),
+        in_specs=[vmem] * 5,
+        out_specs=(vmem,) * 4,
+        compiler_params=params(12),
+        cost_estimate=short,
+        name="leaf",
+    )(blocks, leaf_inv, subtree_shift_rhs, leaf_noise, leaf_dev[None, :])
+
+    arrays, places = listed(far)
+    span = 2**levels * unit
+    return pl.pallas_call(
+        functools.partial(top_kernel, levels, unit, places),
+        out_shape=(
+            jax.ShapeDtypeStruct((subtree_rows, samples), jnp.bfloat16),
+            jax.ShapeDtypeStruct((levels, row_count, samples), jnp.bfloat16),
+        ),
+        in_specs=[vmem] * (7 + levels - 1 + len(arrays)),
+        out_specs=(vmem, vmem),
+        scratch_shapes=[
+            pltpu.VMEM((span, top_columns), jnp.bfloat16),
+            pltpu.VMEM((span, samples), jnp.bfloat16),
+            pltpu.VMEM((span, samples), jnp.float32),
+            pltpu.VMEM((unit * 2, samples), jnp.float32),
+        ],
+        compiler_params=params(16),
+        name="top",
+    )(low_whole, sep_dev, partner, base, edge, inner, scale, *solved, *arrays)
+
+
 def solution(mesh):
+    rows = P(AXES, None)
     in_specs = (
-        P(("leaf", "sec"), None),
+        rows,
         P("leaf", "sec"),
-        P(("leaf", "sec"), None),
-        P(("leaf", "sec"), None),
-        P(("leaf", "sec")),
-        P(("leaf", "sec"), None),
-        P(("leaf", "sec"), None),
-        P(None, ("leaf", "sec"), None),
-        P(None, ("leaf", "sec"), None),
-        P(None, ("leaf", "sec")),
+        rows,
+        rows,
+        P(AXES),
+        rows,
+        rows,
+        P(None, AXES, None),
+        P(None, AXES, None),
+        P(None, AXES),
     )
-    out_specs = (P(("leaf", "sec"), None), P(None, ("leaf", "sec"), None))
-    return jax.shard_map(
-        on_device, mesh=mesh, in_specs=in_specs, out_specs=out_specs, check_vma=False
-    )
+    out_specs = (rows, P(None, AXES, None))
+
+    def program(*arrays):
+        levels = arrays[7].shape[0]
+        paired = levels == 3 and mesh.shape["sec"] == 2 and mesh.shape["leaf"] % 2**levels == 0
+        return on_device(*arrays) if paired else leafwise_on_device(*arrays)
+
+    return jax.shard_map(program, mesh=mesh, in_specs=in_specs, out_specs=out_specs, check_vma=False)

time: 198 us -> 29.8 us (0.15)
  waiting for transfers between devices: 106 us -> 9.36 us
  starting transfers between devices: 48.4 us -> 10.2 us
  between operations: 15.3 us -> 1.41 us
  local copies, waits for them, and re-layouts: 9.96 us -> 0.04 us
  blocking collectives: 11 us -> 2.19 us
  Pallas kernels: 0 us -> 6.51 us
  matrix products: 4.53 us -> 0 us
    ppermute x24 -> x8, waiting for transfers between devices: 54.5 us -> 9.36 us  [the longest x6 8.32 us: to_chips(): return lax.ppermute(block, AXES, route)]
    ppermute x24 -> x8, starting transfers between devices: 48.1 us -> 10.2 us  [the longest x6 9.46 us: to_chips(): return lax.ppermute(block, AXES, route)]
    unnamed x10 -> x0, waiting for transfers between devices: 34.7 us -> none
    reduce_scatter x2 -> x0, waiting for transfers between devices: 17.1 us -> none  [group_reduce(): return lax.psum_scatter(reduced, 'sec', scatter_dimension=0, tiled=True)]
    unnamed x29 -> x10, local copies, waits for them, and re-layouts: 9.61 us -> 0.03 us
    all_gather x6 -> x1, blocking collectives: 11 us -> 2.19 us  [on_device(): lax.all_gather(join([third, first], low_columns, 0), 'sec', axis=0, tiled...]
    pallas_call x0 -> x7, Pallas kernels: none -> 6.51 us  [the longest x1 2.66 us: on_device(): pl.pallas_call(functools.partial(top_kernel, levels, unit, places), out_s...]
    dot_general x13 -> x0, matrix products: 4.53 us -> none  [the longest x7 3.03 us: transposed_product(): lax.dot_general(matrix, vector, (((0,), (0,)), ((), ())), preferred_eleme...]
  transfers between devices with their start and end apart: 30 -> 8, of which waited for: 30 -> 3; matrix products, arithmetic and copies ran while one was open for 1% -> 0% of each run, Pallas kernels for 0% -> 8%
where the time goes in v2:
time: 29.8 us; the launch traced here: 29.7 us
  starting transfers between devices  10.2 us (34%)
  waiting for transfers between devices  9.36 us (31%)
  Pallas kernels  6.51 us (22%)
  blocking collectives  2.19 us (7%)
  between operations  1.41 us (5%)
    ppermute x6, starting transfers between devices, to_chips(): return lax.ppermute(block, AXES, route)  9.46 us
    ppermute x6, waiting for transfers between devices, to_chips(): return lax.ppermute(block, AXES, route)  8.32 us
    pallas_call x1, Pallas kernels, on_device(): pl.pallas_call(functools.partial(top_kernel, levels, unit, places), out_s...  2.66 us
    all_gather x1, blocking collectives, on_device(): lax.all_gather(join([third, first], low_columns, 0), 'sec', axis=0, tiled...  2.19 us
    pallas_call x1, Pallas kernels, on_device(): pl.pallas_call(functools.partial(leaf_kernel, row_count), out_shape=(jax....  1.73 us
    pallas_call x1, Pallas kernels, on_device(): pl.pallas_call(functools.partial(pack_kernel, levels), out_shape=jax.Shap...  1.31 us
    ppermute x2, waiting for transfers between devices, swap(): return lax.ppermute(block, 'sec', [(0, 1), (1, 0)])  1.04 us
    pallas_call x1, Pallas kernels, on_device(): pl.pallas_call(functools.partial(low_kernel, levels, unit, places), out_s...  0.73 us
  transfers between devices with their start and end apart: 8, of which 3 were waited for; matrix products, arithmetic and copies ran while one was open for 0% of the time, Pallas kernels for 8%

profile of v2, /device:TPU:0, one launch (start us, length us, event | category | flops | bytes accessed | tf_op | source)
XLA Modules:
  0.0 29.7 jit_solution(12895672012644532331)
XLA Ops:
  1.3 1.3 %pack.1.own_ref.refs_0_.refs_9_ = bf16[32,2688]{1,0:T(8,128)(2,1)S(1)} custom-call(s32[8,128]{1,0:T(8,128)S(1)} %broadcast_in_dim.11.blocks_ref, bf16[1024,1024]{1,0:T(8,128)(2,1)} %leaf_ref.3, bf16[1024,128]{1,0:T(8,128)(2,1)} %shift_ref.3, bf16[32,896]{1,0:T(8,128)(2,1)} %panel_ref.1, bf16[32,896]{1,0:T(8,128)(2,1)} %inv_ref.1, ...), custom_call_target="tpu_custom_call" | custom-call | flops 1 | bytes 1 | tf_op jit(solution)/shard_map/pack/pallas_call | solution.py:378
  2.6 0.0 copy-start.4
  2.6 0.0 copy-start
  2.6 0.0 copy-start.1
  2.6 0.0 copy-start.2
  2.7 0.5 %collective-permute-start = (bf16[32,2688]{1,0:T(8,128)(2,1)S(1)}, bf16[32,2688]{1,0:T(8,128)(2,1)S(1)}, u32[]{:S(2)}, u32[]{:S(2)}) collective-permute-start(bf16[32,2688]{1,0:T(8,128)(2,1)S(1)} %pack.1.own_ref.refs_0_.refs_9_), channel_id=1, source_target_pairs={{0,1},{1,0},{2,3},{3,2},{4,5},{5,4},{6,7},{7,6},{8,9},{9,8},{10,11... | collective-permute-start | bytes 516104 | tf_op jit(solution)/shard_map/ppermute | solution.py:394
  3.2 1.0 %collective-permute-done.other_ref.refs_1_.refs_10_ = bf16[32,2688]{1,0:T(8,128)(2,1)S(1)} collective-permute-done((bf16[32,2688]{1,0:T(8,128)(2,1)S(1)}, bf16[32,2688]{1,0:T(8,128)(2,1)S(1)}, u32[]{:S(2)}, u32[]{:S(2)}) %collective-permute-start) | collective-permute-done | bytes 172064 | tf_op jit(solution)/shard_map/ppermute | solution.py:394
  4.2 2.9 %collective-permute-start.2 = (bf16[64,1408]{1,0:T(8,128)(2,1)S(1)}, bf16[64,1408]{1,0:T(8,128)(2,1)S(1)}, u32[]{:S(2)}, u32[]{:S(2)}) collective-permute-start(bf16[64,1408]{1,0:T(8,128)(2,1)S(1)} %get-tuple-element.11), channel_id=1, source_target_pairs={{0,2},{1,5},{2,0},{3,7},{4,6},{5,1},{6,4},{7,3},{8,10},{9,13},{10,... | collective-permute-start | bytes 540680 | tf_op jit(solution)/shard_map/ppermute | solution.py:20
  7.2 1.5 %collective-permute-start.1 = (bf16[32,2688]{1,0:T(8,128)(2,1)S(1)}, bf16[32,2688]{1,0:T(8,128)(2,1)S(1)}, u32[]{:S(2)}, u32[]{:S(2)}) collective-permute-start(bf16[32,2688]{1,0:T(8,128)(2,1)S(1)} %pack.1.own_ref.refs_0_.refs_9_), channel_id=1, source_target_pairs={{0,6},{1,7},{2,4},{3,5},{4,2},{5,3},{6,0},{7,1},{8,14},{9,15},{10,... | collective-permute-start | bytes 516104 | tf_op jit(solution)/shard_map/ppermute | solution.py:20
  8.6 1.5 %collective-permute-start.6 = (bf16[64,1280]{1,0:T(8,128)(2,1)S(1)}, bf16[64,1280]{1,0:T(8,128)(2,1)S(1)}, u32[]{:S(2)}, u32[]{:S(2)}) collective-permute-start(bf16[64,1280]{1,0:T(8,128)(2,1)S(1)} %get-tuple-element.19), channel_id=1, source_target_pairs={{0,12},{1,15},{2,14},{3,13},{4,8},{5,11},{6,10},{7,9},{8,4},{9,7},... | collective-permute-start | bytes 491528 | tf_op jit(solution)/shard_map/ppermute | solution.py:20
  10.2 0.1 collective-permute-start.5
  10.2 1.9 %collective-permute-start.4 = (bf16[64,1280]{1,0:T(8,128)(2,1)S(1)}, bf16[64,1280]{1,0:T(8,128)(2,1)S(1)}, u32[]{:S(2)}, u32[]{:S(2)}) collective-permute-start(bf16[64,1280]{1,0:T(8,128)(2,1)S(1)} %get-tuple-element.19), channel_id=1, source_target_pairs={{0,2},{1,5},{2,0},{3,7},{4,6},{5,1},{6,4},{7,3},{8,10},{9,13},{10,... | collective-permute-start | bytes 491528 | tf_op jit(solution)/shard_map/ppermute | solution.py:20
  12.1 7.3 %collective-permute-done.1.refs_0_.refs_1_ = bf16[32,2688]{1,0:T(8,128)(2,1)S(1)} collective-permute-done((bf16[32,2688]{1,0:T(8,128)(2,1)S(1)}, bf16[32,2688]{1,0:T(8,128)(2,1)S(1)}, u32[]{:S(2)}, u32[]{:S(2)}) %collective-permute-start.1) | collective-permute-done | bytes 172064 | tf_op jit(solution)/shard_map/ppermute | solution.py:20
  19.4 0.0 collective-permute-done.2.refs_1_
  19.4 2.2 %all_gather.3.refs_2_ = bf16[192,1408]{1,0:T(8,128)(2,1)S(1)} all-gather(bf16[96,1408]{1,0:T(8,128)(2,1)S(1)} %join.2), channel_id=1, replica_groups=mesh['leaf'=16,'sec'=2] {'sec'}, dimensions={0}, use_global_device_ids=true | all-gather | bytes 811008 | tf_op jit(solution)/shard_map/all_gather | solution.py:423
  21.6 0.7 %low.1 = (bf16[256,1408]{1,0:T(8,128)(2,1)S(1)}, bf16[256,128]{1,0:T(8,128)(2,1)S(1)}, bf16[256,128]{1,0:T(8,128)(2,1)S(1)}) custom-call(bf16[32,2688]{1,0:T(8,128)(2,1)S(1)} %pack.1.own_ref.refs_0_.refs_9_, bf16[32,2688]{1,0:T(8,128)(2,1)S(1)} %collective-permute-done.other_ref.refs_1_.refs_10_, bf16[192,1408]{1,0:T(8,128)(2,1)S(1)} %all_gather.3.refs_2_), custom_call_target="tpu_custom_call" | custom-call | flops 1 | bytes 1 | tf_op jit(solution)/shard_map/low/pallas_call | solution.py:443
  22.4 0.0 copy-start.3
  22.4 0.0 collective-permute-done.6.refs_4_
  22.4 0.0 collective-permute-done.5.refs_3_
  22.4 0.0 collective-permute-done.4.refs_2_
  22.4 0.2 collective-permute-start.7
  22.6 1.6 %collective-permute-start.3 = (bf16[256,128]{1,0:T(8,128)(2,1)S(1)}, bf16[256,128]{1,0:T(8,128)(2,1)S(1)}, u32[]{:S(2)}, u32[]{:S(2)}) collective-permute-start(bf16[256,128]{1,0:T(8,128)(2,1)S(1)} %get-tuple-element.13.refs_0_.refs_8_), channel_id=1, source_target_pairs={{0,8},{1,9},{2,10},{3,11},{4,12},{5,13},{6,14},{7,15},{8,0},{9,1},... | collective-permute-start | bytes 196616 | tf_op jit(solution)/shard_map/ppermute | solution.py:20
  24.2 0.0 copy-done.4
  24.2 0.0 copy-done
  24.2 0.0 copy-done.1
  24.3 0.0 copy-done.2
  24.3 1.7 %leaf.1 = (f32[1024,128]{1,0:T(8,128)S(1)}, f32[32,128]{1,0:T(8,128)S(1)}, bf16[1024,32]{1,0:T(8,128)(2,1)S(1)}, f32[1024,128]{1,0:T(8,128)S(1)}) custom-call(s32[8,128]{1,0:T(8,128)S(1)} %broadcast_in_dim.11.blocks_ref, bf16[1024,1024]{1,0:T(8,128)(2,1)S(1)} %copy-done, bf16[1024,128]{1,0:T(8,128)(2,1)S(1)} %copy-done.1, bf16[1024,128]{1,0:T(8,128)(2,1)S(1)} %copy-done.2, ...), custom_call_target="tpu_custom_call" | custom-call | flops 1 | bytes 1 | tf_op jit(solution)/shard_map/leaf/pallas_call | solution.py:467
  26.0 1.0 %collective-permute-done.3.refs_2_ = bf16[256,128]{1,0:T(8,128)(2,1)S(1)} collective-permute-done((bf16[256,128]{1,0:T(8,128)(2,1)S(1)}, bf16[256,128]{1,0:T(8,128)(2,1)S(1)}, u32[]{:S(2)}, u32[]{:S(2)}) %collective-permute-start.3) | collective-permute-done | bytes 65568 | tf_op jit(solution)/shard_map/ppermute | solution.py:20
  27.0 0.0 collective-permute-done.7.refs_12_
  27.0 0.0 copy-done.3
  27.0 2.7 %top.1 = (bf16[1024,128]{1,0:T(8,128)(2,1)}, bf16[3,32,128]{2,1,0:T(8,128)(2,1)}) custom-call(bf16[256,1408]{1,0:T(8,128)(2,1)S(1)} %get-tuple-element.12.refs_0_, bf16[3,32]{1,0:T(4,128)(2,1)S(1)} %copy-done.3, bf16[256,128]{1,0:T(8,128)(2,1)S(1)} %collective-permute-done.3.refs_2_, f32[1024,128]{1,0:T(8,128)S(1)} %get-tuple-element.14.refs_3_, ...), custom_call_target="tpu_custom_call" | custom-call | tf_op jit(solution)/shard_map/top/pallas_call | solution.py:484
  (5 shorter events, 0.1 us)
Async XLA Ops:
  2.6 21.6 %copy-start.4 = (bf16[1024]{0:T(1024)(128)(2,1)S(1)}, bf16[1024]{0:T(1024)(128)(2,1)}, u32[]{:S(2)}) copy-start(bf16[1024]{0:T(1024)(128)(2,1)} %param.14) | copy-start | bytes 6148
  2.6 21.6 %copy-start = (bf16[1024,1024]{1,0:T(8,128)(2,1)S(1)}, bf16[1024,1024]{1,0:T(8,128)(2,1)}, u32[]{:S(2)}) copy-start(bf16[1024,1024]{1,0:T(8,128)(2,1)} %leaf_ref.3) | copy-start | bytes 6291460
  2.6 21.6 %copy-start.1 = (bf16[1024,128]{1,0:T(8,128)(2,1)S(1)}, bf16[1024,128]{1,0:T(8,128)(2,1)}, u32[]{:S(2)}) copy-start(bf16[1024,128]{1,0:T(8,128)(2,1)} %shift_ref.3) | copy-start | bytes 786436
  2.6 21.6 %copy-start.2 = (bf16[1024,128]{1,0:T(8,128)(2,1)S(1)}, bf16[1024,128]{1,0:T(8,128)(2,1)}, u32[]{:S(2)}) copy-start(bf16[1024,128]{1,0:T(8,128)(2,1)} %noise_ref.3) | copy-start | bytes 786436
  2.7 1.6 %collective-permute-start = (bf16[32,2688]{1,0:T(8,128)(2,1)S(1)}, bf16[32,2688]{1,0:T(8,128)(2,1)S(1)}, u32[]{:S(2)}, u32[]{:S(2)}) collective-permute-start(bf16[32,2688]{1,0:T(8,128)(2,1)S(1)} %pack.1.own_ref.refs_0_.refs_9_), channel_id=1, source_target_pairs={{0,1},{1,0},{2,3},{3,2},{4,5},{5,4},{6,7},{7,6},{8,9},{9,8},{10,11... | collective-permute-start | bytes 516104 | tf_op jit(solution)/shard_map/ppermute | solution.py:394
  4.2 15.2 %collective-permute-start.2 = (bf16[64,1408]{1,0:T(8,128)(2,1)S(1)}, bf16[64,1408]{1,0:T(8,128)(2,1)S(1)}, u32[]{:S(2)}, u32[]{:S(2)}) collective-permute-start(bf16[64,1408]{1,0:T(8,128)(2,1)S(1)} %get-tuple-element.11), channel_id=1, source_target_pairs={{0,2},{1,5},{2,0},{3,7},{4,6},{5,1},{6,4},{7,3},{8,10},{9,13},{10,... | collective-permute-start | bytes 540680 | tf_op jit(solution)/shard_map/ppermute | solution.py:20
  7.2 12.2 %collective-permute-start.1 = (bf16[32,2688]{1,0:T(8,128)(2,1)S(1)}, bf16[32,2688]{1,0:T(8,128)(2,1)S(1)}, u32[]{:S(2)}, u32[]{:S(2)}) collective-permute-start(bf16[32,2688]{1,0:T(8,128)(2,1)S(1)} %pack.1.own_ref.refs_0_.refs_9_), channel_id=1, source_target_pairs={{0,6},{1,7},{2,4},{3,5},{4,2},{5,3},{6,0},{7,1},{8,14},{9,15},{10,... | collective-permute-start | bytes 516104 | tf_op jit(solution)/shard_map/ppermute | solution.py:20
  8.6 13.7 %collective-permute-start.6 = (bf16[64,1280]{1,0:T(8,128)(2,1)S(1)}, bf16[64,1280]{1,0:T(8,128)(2,1)S(1)}, u32[]{:S(2)}, u32[]{:S(2)}) collective-permute-start(bf16[64,1280]{1,0:T(8,128)(2,1)S(1)} %get-tuple-element.19), channel_id=1, source_target_pairs={{0,12},{1,15},{2,14},{3,13},{4,8},{5,11},{6,10},{7,9},{8,4},{9,7},... | collective-permute-start | bytes 491528 | tf_op jit(solution)/shard_map/ppermute | solution.py:20
  10.2 12.2 %collective-permute-start.5 = (bf16[64,1280]{1,0:T(8,128)(2,1)S(1)}, bf16[64,1280]{1,0:T(8,128)(2,1)S(1)}, u32[]{:S(2)}, u32[]{:S(2)}) collective-permute-start(bf16[64,1280]{1,0:T(8,128)(2,1)S(1)} %get-tuple-element.19), channel_id=1, source_target_pairs={{0,8},{1,11},{2,10},{3,9},{4,12},{5,15},{6,14},{7,13},{8,0},{9,3},... | collective-permute-start | bytes 491528 | tf_op jit(solution)/shard_map/ppermute | solution.py:20
  10.2 12.2 %collective-permute-start.4 = (bf16[64,1280]{1,0:T(8,128)(2,1)S(1)}, bf16[64,1280]{1,0:T(8,128)(2,1)S(1)}, u32[]{:S(2)}, u32[]{:S(2)}) collective-permute-start(bf16[64,1280]{1,0:T(8,128)(2,1)S(1)} %get-tuple-element.19), channel_id=1, source_target_pairs={{0,2},{1,5},{2,0},{3,7},{4,6},{5,1},{6,4},{7,3},{8,10},{9,13},{10,... | collective-permute-start | bytes 491528 | tf_op jit(solution)/shard_map/ppermute | solution.py:20
  22.4 4.7 %copy-start.3 = (bf16[3,32]{1,0:T(4,128)(2,1)S(1)}, bf16[3,32]{1,0:T(4,128)(2,1)}, u32[]{:S(2)}) copy-start(bf16[3,32]{1,0:T(4,128)(2,1)} %refs_1_.1) | copy-start | bytes 580
  22.4 4.6 %collective-permute-start.7 = (bf16[224,1280]{1,0:T(8,128)(2,1)S(1)}, bf16[224,1280]{1,0:T(8,128)(2,1)S(1)}, u32[]{:S(2)}, u32[]{:S(2)}) collective-permute-start(bf16[224,1280]{1,0:T(8,128)(2,1)S(1)} %join.3.refs_11_), channel_id=1, source_target_pairs={{0,1},{1,0},{2,3},{3,2},{4,5},{5,4},{6,7},{7,6},{8,9},{9,8},{10,11... | collective-permute-start | bytes 1720328 | tf_op jit(solution)/shard_map/ppermute | solution.py:394
  22.6 4.4 %collective-permute-start.3 = (bf16[256,128]{1,0:T(8,128)(2,1)S(1)}, bf16[256,128]{1,0:T(8,128)(2,1)S(1)}, u32[]{:S(2)}, u32[]{:S(2)}) collective-permute-start(bf16[256,128]{1,0:T(8,128)(2,1)S(1)} %get-tuple-element.13.refs_0_.refs_8_), channel_id=1, source_target_pairs={{0,8},{1,9},{2,10},{3,11},{4,12},{5,13},{6,14},{7,15},{8,0},{9,1},... | collective-permute-start | bytes 196616 | tf_op jit(solution)/shard_map/ppermute | solution.py:20

commit v3 on v2

--- a/solution.py
+++ b/solution.py
@@ -27,21 +27,22 @@
     return jnp.sum(jnp.where(across == down, row, jnp.zeros_like(row)), axis=1, keepdims=True)
 
 
-def live_rows(blocks_ref, rows, columns):
-    live_from = rows - blocks_ref[0:1, 0:columns] * BLOCK
+def live_rows(dead_ref, rows, columns):
+    live_from = dead_ref[0:1, 0:columns]
     return lax.broadcasted_iota(jnp.int32, (rows, columns), 0) >= live_from
 
 
 def pack_kernel(
     levels,
-    blocks_ref,
+    dead_ref,
     leaf_ref,
     shift_ref,
     panel_ref,
     inv_ref,
     rhs_ref,
     noise_ref,
-    pack_ref,
+    low_ref,
+    top_ref,
     edge_ref,
     moved_ref,
     arrived,
@@ -56,6 +57,8 @@
     unit = panel_ref.shape[1] // (2 ** (levels + 1) - 2)
     for height in range(1, levels + 1):
         span = 2**height * unit
+        out = low_ref if height < levels else top_ref
+        at = at if height < levels else 0
         for source, width in (
             (panel_ref.at[:, pl.ds(offset, span)], span),
             (inv_ref.at[:, pl.ds(offset, span)], span),
@@ -63,7 +66,7 @@
             (noise_ref.at[height - 1], samples),
         ):
             copies.append(
-                pltpu.make_async_copy(source, pack_ref.at[:, pl.ds(at, width)], arrived.at[len(copies)])
+                pltpu.make_async_copy(source, out.at[:, pl.ds(at, width)], arrived.at[len(copies)])
             )
             at += width
         offset += span
@@ -72,32 +75,21 @@
     for copy in copies[:2]:
         copy.wait()
     shift = moved_ref[...]
-    shift = jnp.where(live_rows(blocks_ref, *shift.shape), shift, jnp.zeros_like(shift))
+    shift = jnp.where(live_rows(dead_ref, *shift.shape), shift, jnp.zeros_like(shift))
     boundary = jnp.dot(edge_ref[...], shift, preferred_element_type=jnp.float32)
-    pack_ref[:, :samples] = boundary.astype(jnp.bfloat16)
+    low_ref[:, :samples] = boundary.astype(jnp.bfloat16)
     for copy in copies[2:]:
         copy.wait()
 
 
-def pair_kernel(own_ref, other_ref, low_ref, top_ref):
-    row_count = own_ref.shape[0]
-    columns = low_ref.shape[1]
-    for start, ref in ((0, own_ref), (row_count, other_ref)):
-        low_ref[start : start + row_count, :] = ref[:, :columns]
-        top_ref[start : start + row_count, :] = ref[:, columns:]
-
-
-def join_kernel(column, *refs):
+def join_kernel(*refs):
     joined_ref, row = refs[-1], 0
-    columns = joined_ref.shape[1]
     for ref in refs[:-1]:
-        skipped = 0 if ref.shape[1] == columns else column
-        joined_ref[row : row + ref.shape[0], :] = ref[:, skipped : skipped + columns]
+        joined_ref[row : row + ref.shape[0], :] = ref[...]
         row += ref.shape[0]
 
 
-def place(pieces, refs, whole_ref, row_count, leaves, first_column):
-    columns = whole_ref.shape[1]
+def place(pieces, refs, whole_ref, row_count, leaves):
     leaf, section = lax.axis_index("leaf"), lax.axis_index("sec")
     for which, start, distances, turned in pieces:
         if isinstance(turned, int):
@@ -107,10 +99,7 @@
             owner, distance = turned[0], distances[0]
         at = (((leaf ^ distance) & (leaves - 1)) * 2 + owner) * row_count
         ref = refs[which]
-        skipped = 0 if ref.shape[1] == columns else first_column
-        whole_ref[pl.ds(pl.multiple_of(at, row_count), row_count), :] = ref[
-            start : start + row_count, skipped : skipped + columns
-        ]
+        whole_ref[pl.ds(pl.multiple_of(at, row_count), row_count), :] = ref[start : start + row_count, :]
 
 
 def solve_forward(whole, rows, at, span, samples, children):
@@ -125,7 +114,7 @@
 def low_kernel(levels, unit, pieces, *refs):
     piece_refs, (whole_ref, *solved_refs) = refs[:-levels], refs[-levels:]
     row_count = unit // 2
-    place(pieces, piece_refs, whole_ref, row_count, 2 ** (levels - 1), 0)
+    place(pieces, piece_refs, whole_ref, row_count, 2 ** (levels - 1))
     samples = solved_refs[0].shape[1]
     total = whole_ref.shape[0]
     below_ref, at = whole_ref, samples
@@ -141,7 +130,7 @@
 
 def leaf_kernel(
     row_count,
-    blocks_ref,
+    dead_ref,
     leaf_ref,
     shift_ref,
     noise_ref,
@@ -152,7 +141,7 @@
     scale_ref,
 ):
     rows, samples = shift_ref.shape
-    live = live_rows(blocks_ref, rows, samples)
+    live = live_rows(dead_ref, rows, samples)
     shift = shift_ref[...]
     shift = jnp.where(live, shift, jnp.zeros_like(shift))
     zero = jnp.float32(0.0)
@@ -180,7 +169,7 @@
     samples = partner_ref.shape[1]
     row_count = unit // 2
     leaf, section = lax.axis_index("leaf"), lax.axis_index("sec")
-    place(pieces, piece_refs, whole_ref, row_count, 2**levels, low_ref.shape[1])
+    place(pieces, piece_refs, whole_ref, row_count, 2**levels)
     half = partner_ref.shape[0]
     upper = leaf >> (levels - 1) & 1
     child_ref[pl.ds(pl.multiple_of(upper * half, half), half), :] = solved_refs[-1][...]
@@ -362,7 +351,6 @@
     levels, _, samples = sep_rhs.shape
     unit = 2 * row_count
     vmem = pl.BlockSpec(memory_space=pltpu.VMEM)
-    short = pl.CostEstimate(flops=1, bytes_accessed=1, transcendentals=0)
 
     def params(mib):
         return pltpu.CompilerParams(vmem_limit_bytes=mib * 2**20)
@@ -374,60 +362,49 @@
     def in_hbm(array):
         return pltpu.with_memory_space_constraint(array, pltpu.HBM)
 
-    blocks = jnp.broadcast_to(subtree_blocks, (8, samples))
-    pack = pl.pallas_call(
+    dead = jnp.full((8, samples), subtree_rows - subtree_blocks[0, 0] * BLOCK, jnp.int32)
+    low, top = pl.pallas_call(
         functools.partial(pack_kernel, levels),
-        out_shape=jax.ShapeDtypeStruct((row_count, low_columns + top_columns), jnp.bfloat16),
+        out_shape=(
+            jax.ShapeDtypeStruct((row_count, low_columns), jnp.bfloat16),
+            jax.ShapeDtypeStruct((row_count, top_columns), jnp.bfloat16),
+        ),
         in_specs=[vmem] + [hbm] * 6,
-        out_specs=vmem,
+        out_specs=(vmem, vmem),
         scratch_shapes=[
             pltpu.VMEM((row_count, subtree_rows), jnp.bfloat16),
             pltpu.VMEM((subtree_rows, samples), jnp.bfloat16),
             pltpu.SemaphoreType.DMA((2 + 4 * levels,)),
         ],
         compiler_params=params(4),
-        cost_estimate=short,
         name="pack",
-    )(blocks, *(in_hbm(x) for x in (leaf_inv, subtree_shift_rhs, sep_panel, sep_inv, sep_rhs, sep_noise)))
+    )(dead, *(in_hbm(x) for x in (leaf_inv, subtree_shift_rhs, sep_panel, sep_inv, sep_rhs, sep_noise)))
 
     def swap(block):
         return lax.ppermute(block, "sec", [(0, 1), (1, 0)])
 
-    def join(arrays, columns, column, *after):
+    def join(arrays, *after, flops=0):
         rows = sum(array.shape[0] for array in arrays)
         return pl.pallas_call(
-            lambda *refs: join_kernel(column, *refs[len(after) :]),
-            out_shape=jax.ShapeDtypeStruct((rows, columns), jnp.bfloat16),
+            lambda *refs: join_kernel(*refs[len(after) :]),
+            out_shape=jax.ShapeDtypeStruct((rows, arrays[0].shape[1]), arrays[0].dtype),
             in_specs=[pl.BlockSpec(memory_space=pl.ANY)] * len(after) + [vmem] * len(arrays),
             out_specs=vmem,
             compiler_params=params(4),
-            cost_estimate=short,
+            cost_estimate=pl.CostEstimate(flops=flops, bytes_accessed=0, transcendentals=0) if flops else None,
             name="join",
         )(*after, *arrays)
 
-    pack_other = swap(pack)
-    low_pair, top_pair = pl.pallas_call(
-        pair_kernel,
-        out_shape=(
-            jax.ShapeDtypeStruct((unit, low_columns), jnp.bfloat16),
-            jax.ShapeDtypeStruct((unit, top_columns), jnp.bfloat16),
-        ),
-        in_specs=[vmem, vmem],
-        out_specs=(vmem, vmem),
-        compiler_params=params(4),
-        cost_estimate=short,
-        name="pair",
-    )(pack, pack_other)
-    third = to_chips(pack, (3, 3))
-    first = to_chips(low_pair, (1, 2))
-    both = lax.all_gather(join([third, first], low_columns, 0), "sec", axis=0, tiled=True)
-    own = [(pack, 0, (0, 0), 0), (pack_other, 0, (0, 0), 1)]
-    quarter = list(own)
-    for owner, distance in ((0, 1), (1, 2)):
-        row = 3 * row_count * owner
-        quarter.append((both, row, (3,), (owner,)))
-        quarter.append((both, row + row_count, (distance,), (owner,)))
-        quarter.append((both, row + 2 * row_count, (distance,), (1 - owner,)))
+    quad = 2 ** (levels - 1)
+    near = join([low] + [to_chips(low, (distance, distance)) for distance in range(1, quad)])
+    near = lax.all_gather(near, "sec", axis=0, tiled=True)
+    quarter = []
+    for owner in range(2):
+        for distance in range(quad):
+            quarter.append((near, (owner * quad + distance) * row_count, (distance,), (owner,)))
+
+    top_other = swap(top)
+    top_pair = join([top, top_other])
 
     def listed(pieces):
         arrays, places = [], []
@@ -439,7 +416,6 @@
         return arrays, places
 
     arrays, places = listed(quarter)
-    quad = 2 ** (levels - 1)
     low_whole, *solved = pl.pallas_call(
         functools.partial(low_kernel, levels, unit, places),
         out_shape=[jax.ShapeDtypeStruct((quad * unit, low_columns), jnp.bfloat16)]
@@ -447,16 +423,14 @@
         in_specs=[vmem] * len(arrays),
         out_specs=[vmem] * levels,
         compiler_params=params(8),
-        cost_estimate=short,
         name="low",
     )(*arrays)
     partner = to_chips(solved[-1], (quad, quad))
 
-    trips = [(pack, (3, 3)), (top_pair, (1, 2)), (top_pair, (4, 5)), (top_pair, (6, 7))]
-    arrived = [third] + [to_chips(block, distances) for block, distances in trips[1:]]
-    here = join(arrived, top_columns, low_columns, solved[-1])
+    trips = [(top, (3, 3)), (top_pair, (1, 2)), (top_pair, (4, 5)), (top_pair, (6, 7))]
+    here = join([to_chips(block, distances) for block, distances in trips], solved[-1])
     there = swap(here)
-    far = own
+    far = [(top, 0, (0, 0), 0), (top_other, 0, (0, 0), 1)]
     row = 0
     for block, (first, second) in trips:
         for turned in range(block.shape[0] // row_count):
@@ -475,10 +449,10 @@
         in_specs=[vmem] * 5,
         out_specs=(vmem,) * 4,
         compiler_params=params(12),
-        cost_estimate=short,
         name="leaf",
-    )(blocks, leaf_inv, subtree_shift_rhs, leaf_noise, leaf_dev[None, :])
-
+    )(dead, leaf_inv, subtree_shift_rhs, leaf_noise, leaf_dev[None, :])
+
+    edge = join([edge], partner, flops=10**10)
     arrays, places = listed(far)
     span = 2**levels * unit
     return pl.pallas_call(

time: 29.8 us -> 25.8 us (0.87)
  waiting for transfers between devices: 9.36 us -> 2.6 us
  starting transfers between devices: 10.2 us -> 12.5 us
    ppermute x6 -> x8, waiting for transfers between devices: 8.32 us -> 1.86 us  [to_chips(): return lax.ppermute(block, AXES, route)]
    ppermute x6 -> x8, starting transfers between devices: 9.46 us -> 12.5 us  [to_chips(): return lax.ppermute(block, AXES, route)]
    ppermute x2, starting transfers between devices: 0.72 us -> 0.07 us  [swap(): return lax.ppermute(block, 'sec', [(0, 1), (1, 0)])]
    ppermute x2, waiting for transfers between devices: 1.04 us -> 0.73 us  [swap(): return lax.ppermute(block, 'sec', [(0, 1), (1, 0)])]
    pallas_call x4 -> x5, Pallas kernels: 1.39 us -> 1.53 us  [the longest x1 1.46 us: on_device(): pl.pallas_call(functools.partial(pack_kernel, levels), out_shape=(jax.Sha...]
  transfers between devices with their start and end apart: 8 -> 10, of which waited for: 3 -> 3; matrix products, arithmetic and copies ran while one was open for 0% -> 0% of each run, Pallas kernels for 8% -> 10%
where the time goes in v3:
time: 25.8 us; the launch traced here: 25.6 us
  starting transfers between devices  12.5 us (48%)
  Pallas kernels  6.63 us (26%)
  waiting for transfers between devices  2.6 us (10%)
  blocking collectives  2.43 us (9%)
  between operations  1.39 us (5%)
    ppermute x8, starting transfers between devices, to_chips(): return lax.ppermute(block, AXES, route)  12.5 us
    pallas_call x1, Pallas kernels, on_device(): pl.pallas_call(functools.partial(top_kernel, levels, unit, places), out_s...  2.66 us
    all_gather x1, blocking collectives, on_device(): near = lax.all_gather(near, 'sec', axis=0, tiled=True)  2.43 us
    ppermute x8, waiting for transfers between devices, to_chips(): return lax.ppermute(block, AXES, route)  1.86 us
    pallas_call x1, Pallas kernels, on_device(): pl.pallas_call(functools.partial(leaf_kernel, row_count), out_shape=(jax....  1.73 us
    pallas_call x1, Pallas kernels, on_device(): pl.pallas_call(functools.partial(pack_kernel, levels), out_shape=(jax.Sha...  1.46 us
    ppermute x2, waiting for transfers between devices, swap(): return lax.ppermute(block, 'sec', [(0, 1), (1, 0)])  0.73 us
    pallas_call x1, Pallas kernels, on_device(): pl.pallas_call(functools.partial(low_kernel, levels, unit, places), out_s...  0.71 us
  transfers between devices with their start and end apart: 10, of which 3 were waited for; matrix products, arithmetic and copies ran while one was open for 0% of the time, Pallas kernels for 10%

profile of v3, /device:TPU:0, one launch (start us, length us, event | category | flops | bytes accessed | tf_op | source)
XLA Modules:
  0.0 25.6 jit_solution(8630482813265655805)
XLA Ops:
  1.3 0.0 copy-start.4
  1.3 0.0 copy-start
  1.3 0.0 copy-start.1
  1.3 0.0 copy-start.2
  1.3 1.5 %pack.1 = (bf16[32,1408]{1,0:T(8,128)(2,1)S(1)}, bf16[32,1280]{1,0:T(8,128)(2,1)S(1)}) custom-call(s32[8,128]{1,0:T(8,128)S(1)} %broadcast_in_dim.6.dead_ref, bf16[1024,1024]{1,0:T(8,128)(2,1)} %leaf_ref.3, bf16[1024,128]{1,0:T(8,128)(2,1)} %shift_ref.3, bf16[32,896]{1,0:T(8,128)(2,1)} %panel_ref.1, bf16[32,896]{1,0:T(8,128)(2,1)} %inv_ref.1, ...), custom_call_target="tpu_custom_call" | custom-call | tf_op jit(solution)/shard_map/pack/pallas_call | solution.py:366
  2.8 4.0 %collective-permute-start.2 = (bf16[32,1408]{1,0:T(8,128)(2,1)S(1)}, bf16[32,1408]{1,0:T(8,128)(2,1)S(1)}, u32[]{:S(2)}, u32[]{:S(2)}) collective-permute-start(bf16[32,1408]{1,0:T(8,128)(2,1)S(1)} %get-tuple-element.11.refs_0_), channel_id=1, source_target_pairs={{0,6},{1,7},{2,4},{3,5},{4,2},{5,3},{6,0},{7,1},{8,14},{9,15},{10,... | collective-permute-start | bytes 270344 | tf_op jit(solution)/shard_map/ppermute | solution.py:20
  6.8 0.5 %collective-permute-start.1 = (bf16[32,1408]{1,0:T(8,128)(2,1)S(1)}, bf16[32,1408]{1,0:T(8,128)(2,1)S(1)}, u32[]{:S(2)}, u32[]{:S(2)}) collective-permute-start(bf16[32,1408]{1,0:T(8,128)(2,1)S(1)} %get-tuple-element.11.refs_0_), channel_id=1, source_target_pairs={{0,4},{1,5},{2,6},{3,7},{4,0},{5,1},{6,2},{7,3},{8,12},{9,13},{10,... | collective-permute-start | bytes 270344 | tf_op jit(solution)/shard_map/ppermute | solution.py:20
  7.3 0.1 collective-permute-start
  7.4 0.0 collective-permute-start.4
  7.4 2.8 %collective-permute-start.5 = (bf16[32,1280]{1,0:T(8,128)(2,1)S(1)}, bf16[32,1280]{1,0:T(8,128)(2,1)S(1)}, u32[]{:S(2)}, u32[]{:S(2)}) collective-permute-start(bf16[32,1280]{1,0:T(8,128)(2,1)S(1)} %get-tuple-element.19.refs_0_.refs_9_), channel_id=1, source_target_pairs={{0,6},{1,7},{2,4},{3,5},{4,2},{5,3},{6,0},{7,1},{8,14},{9,15},{10,... | collective-permute-start | bytes 245768 | tf_op jit(solution)/shard_map/ppermute | solution.py:20
  10.3 0.0 collective-permute-done.4.refs_1_.refs_10_
  10.3 1.6 %collective-permute-start.8 = (bf16[64,1280]{1,0:T(8,128)(2,1)S(1)}, bf16[64,1280]{1,0:T(8,128)(2,1)S(1)}, u32[]{:S(2)}, u32[]{:S(2)}) collective-permute-start(bf16[64,1280]{1,0:T(8,128)(2,1)S(1)} %join.6), channel_id=1, source_target_pairs={{0,12},{1,15},{2,14},{3,13},{4,8},{5,11},{6,10},{7,9},{8,4},{9,7},... | collective-permute-start | bytes 491528 | tf_op jit(solution)/shard_map/ppermute | solution.py:20
  11.9 0.0 collective-permute-done.2.refs_3_
  11.9 0.5 %collective-permute-start.7 = (bf16[64,1280]{1,0:T(8,128)(2,1)S(1)}, bf16[64,1280]{1,0:T(8,128)(2,1)S(1)}, u32[]{:S(2)}, u32[]{:S(2)}) collective-permute-start(bf16[64,1280]{1,0:T(8,128)(2,1)S(1)} %join.6), channel_id=1, source_target_pairs={{0,8},{1,11},{2,10},{3,9},{4,12},{5,15},{6,14},{7,13},{8,0},{9,3},... | collective-permute-start | bytes 491528 | tf_op jit(solution)/shard_map/ppermute | solution.py:20
  12.3 0.0 collective-permute-done.1.refs_2_
  12.3 1.3 %collective-permute-start.6 = (bf16[64,1280]{1,0:T(8,128)(2,1)S(1)}, bf16[64,1280]{1,0:T(8,128)(2,1)S(1)}, u32[]{:S(2)}, u32[]{:S(2)}) collective-permute-start(bf16[64,1280]{1,0:T(8,128)(2,1)S(1)} %join.6), channel_id=1, source_target_pairs={{0,2},{1,5},{2,0},{3,7},{4,6},{5,1},{6,4},{7,3},{8,10},{9,13},{10,... | collective-permute-start | bytes 491528 | tf_op jit(solution)/shard_map/ppermute | solution.py:20
  13.6 0.0 collective-permute-done.refs_1_
  13.7 2.4 %all_gather.3.refs_0_ = bf16[256,1408]{1,0:T(8,128)(2,1)S(1)} all-gather(bf16[128,1408]{1,0:T(8,128)(2,1)S(1)} %join.4), channel_id=1, replica_groups=mesh['leaf'=16,'sec'=2] {'sec'}, dimensions={0}, use_global_device_ids=true | all-gather | bytes 1081344 | tf_op jit(solution)/shard_map/all_gather | solution.py:400
  16.1 0.7 %low.1 = (bf16[256,1408]{1,0:T(8,128)(2,1)S(1)}, bf16[256,128]{1,0:T(8,128)(2,1)S(1)}, bf16[256,128]{1,0:T(8,128)(2,1)S(1)}) custom-call(bf16[256,1408]{1,0:T(8,128)(2,1)S(1)} %all_gather.3.refs_0_), custom_call_target="tpu_custom_call" | custom-call | tf_op jit(solution)/shard_map/low/pallas_call | solution.py:419
  16.8 1.7 %collective-permute-start.3 = (bf16[256,128]{1,0:T(8,128)(2,1)S(1)}, bf16[256,128]{1,0:T(8,128)(2,1)S(1)}, u32[]{:S(2)}, u32[]{:S(2)}) collective-permute-start(bf16[256,128]{1,0:T(8,128)(2,1)S(1)} %get-tuple-element.13.refs_0_.refs_8_), channel_id=1, source_target_pairs={{0,8},{1,9},{2,10},{3,11},{4,12},{5,13},{6,14},{7,15},{8,0},{9,1},... | collective-permute-start | bytes 196616 | tf_op jit(solution)/shard_map/ppermute | solution.py:20
  18.5 0.0 copy-done.4
  18.5 0.0 copy-done
  18.5 0.0 copy-done.1
  18.5 0.0 copy-done.2
  18.5 1.7 %leaf.1 = (f32[1024,128]{1,0:T(8,128)S(1)}, f32[32,128]{1,0:T(8,128)S(1)}, bf16[1024,32]{1,0:T(8,128)(2,1)S(1)}, f32[1024,128]{1,0:T(8,128)S(1)}) custom-call(s32[8,128]{1,0:T(8,128)S(1)} %broadcast_in_dim.6.dead_ref, bf16[1024,1024]{1,0:T(8,128)(2,1)S(1)} %copy-done, bf16[1024,128]{1,0:T(8,128)(2,1)S(1)} %copy-done.1, bf16[1024,128]{1,0:T(8,128)(2,1)S(1)} %copy-done.2, ...), custom_call_target="tpu_custom_call" | custom-call | tf_op jit(solution)/shard_map/leaf/pallas_call | solution.py:441
  20.2 0.0 collective-permute-done.5.refs_1_
  20.2 0.0 collective-permute-done.8.refs_4_
  20.2 0.6 %collective-permute-done.7.refs_3_ = bf16[64,1280]{1,0:T(8,128)(2,1)S(1)} collective-permute-done((bf16[64,1280]{1,0:T(8,128)(2,1)S(1)}, bf16[64,1280]{1,0:T(8,128)(2,1)S(1)}, u32[]{:S(2)}, u32[]{:S(2)}) %collective-permute-start.7) | collective-permute-done | bytes 163872 | tf_op jit(solution)/shard_map/ppermute | solution.py:20
  20.9 0.0 collective-permute-done.6.refs_2_
  20.9 0.1 collective-permute-start.9
  21.0 1.2 %collective-permute-done.3.refs_0_.refs_2_ = bf16[256,128]{1,0:T(8,128)(2,1)S(1)} collective-permute-done((bf16[256,128]{1,0:T(8,128)(2,1)S(1)}, bf16[256,128]{1,0:T(8,128)(2,1)S(1)}, u32[]{:S(2)}, u32[]{:S(2)}) %collective-permute-start.3) | collective-permute-done | bytes 65568 | tf_op jit(solution)/shard_map/ppermute | solution.py:20
  22.2 0.0 copy-start.3
  22.2 0.7 %collective-permute-done.9.refs_12_ = bf16[224,1280]{1,0:T(8,128)(2,1)S(1)} collective-permute-done((bf16[224,1280]{1,0:T(8,128)(2,1)S(1)}, bf16[224,1280]{1,0:T(8,128)(2,1)S(1)}, u32[]{:S(2)}, u32[]{:S(2)}) %collective-permute-start.9) | collective-permute-done | bytes 573472 | tf_op jit(solution)/shard_map/ppermute | solution.py:384
  23.0 0.0 copy-done.3
  23.0 2.7 %top.1 = (bf16[1024,128]{1,0:T(8,128)(2,1)}, bf16[3,32,128]{2,1,0:T(8,128)(2,1)}) custom-call(bf16[256,1408]{1,0:T(8,128)(2,1)S(1)} %get-tuple-element.12.refs_0_, bf16[3,32]{1,0:T(4,128)(2,1)S(1)} %copy-done.3, bf16[256,128]{1,0:T(8,128)(2,1)S(1)} %collective-permute-done.3.refs_0_.refs_2_, f32[1024,128]{1,0:T(8,128)S(1)} %get-tuple-element.14.refs_3_, ...), custom_call_target="tpu_custom_call" | custom-call | tf_op jit(solution)/shard_map/top/pallas_call | solution.py:458
  (6 shorter events, 0.1 us)
Async XLA Ops:
  1.3 17.2 %copy-start.4 = (bf16[1024]{0:T(1024)(128)(2,1)S(1)}, bf16[1024]{0:T(1024)(128)(2,1)}, u32[]{:S(2)}) copy-start(bf16[1024]{0:T(1024)(128)(2,1)} %param.14) | copy-start | bytes 6148
  1.3 17.2 %copy-start = (bf16[1024,1024]{1,0:T(8,128)(2,1)S(1)}, bf16[1024,1024]{1,0:T(8,128)(2,1)}, u32[]{:S(2)}) copy-start(bf16[1024,1024]{1,0:T(8,128)(2,1)} %leaf_ref.3) | copy-start | bytes 6291460
  1.3 17.2 %copy-start.1 = (bf16[1024,128]{1,0:T(8,128)(2,1)S(1)}, bf16[1024,128]{1,0:T(8,128)(2,1)}, u32[]{:S(2)}) copy-start(bf16[1024,128]{1,0:T(8,128)(2,1)} %shift_ref.3) | copy-start | bytes 786436
  1.3 17.2 %copy-start.2 = (bf16[1024,128]{1,0:T(8,128)(2,1)S(1)}, bf16[1024,128]{1,0:T(8,128)(2,1)}, u32[]{:S(2)}) copy-start(bf16[1024,128]{1,0:T(8,128)(2,1)} %noise_ref.3) | copy-start | bytes 786436
  2.8 9.1 %collective-permute-start.2 = (bf16[32,1408]{1,0:T(8,128)(2,1)S(1)}, bf16[32,1408]{1,0:T(8,128)(2,1)S(1)}, u32[]{:S(2)}, u32[]{:S(2)}) collective-permute-start(bf16[32,1408]{1,0:T(8,128)(2,1)S(1)} %get-tuple-element.11.refs_0_), channel_id=1, source_target_pairs={{0,6},{1,7},{2,4},{3,5},{4,2},{5,3},{6,0},{7,1},{8,14},{9,15},{10,... | collective-permute-start | bytes 270344 | tf_op jit(solution)/shard_map/ppermute | solution.py:20
  6.8 5.6 %collective-permute-start.1 = (bf16[32,1408]{1,0:T(8,128)(2,1)S(1)}, bf16[32,1408]{1,0:T(8,128)(2,1)S(1)}, u32[]{:S(2)}, u32[]{:S(2)}) collective-permute-start(bf16[32,1408]{1,0:T(8,128)(2,1)S(1)} %get-tuple-element.11.refs_0_), channel_id=1, source_target_pairs={{0,4},{1,5},{2,6},{3,7},{4,0},{5,1},{6,2},{7,3},{8,12},{9,13},{10,... | collective-permute-start | bytes 270344 | tf_op jit(solution)/shard_map/ppermute | solution.py:20
  7.3 6.4 %collective-permute-start = (bf16[32,1408]{1,0:T(8,128)(2,1)S(1)}, bf16[32,1408]{1,0:T(8,128)(2,1)S(1)}, u32[]{:S(2)}, u32[]{:S(2)}) collective-permute-start(bf16[32,1408]{1,0:T(8,128)(2,1)S(1)} %get-tuple-element.11.refs_0_), channel_id=1, source_target_pairs={{0,2},{1,3},{2,0},{3,1},{4,6},{5,7},{6,4},{7,5},{8,10},{9,11},{10,... | collective-permute-start | bytes 270344 | tf_op jit(solution)/shard_map/ppermute | solution.py:20
  7.4 2.9 %collective-permute-start.4 = (bf16[32,1280]{1,0:T(8,128)(2,1)S(1)}, bf16[32,1280]{1,0:T(8,128)(2,1)S(1)}, u32[]{:S(2)}, u32[]{:S(2)}) collective-permute-start(bf16[32,1280]{1,0:T(8,128)(2,1)S(1)} %get-tuple-element.19.refs_0_.refs_9_), channel_id=1, source_target_pairs={{0,1},{1,0},{2,3},{3,2},{4,5},{5,4},{6,7},{7,6},{8,9},{9,8},{10,11... | collective-permute-start | bytes 245768 | tf_op jit(solution)/shard_map/ppermute | solution.py:384
  7.4 12.8 %collective-permute-start.5 = (bf16[32,1280]{1,0:T(8,128)(2,1)S(1)}, bf16[32,1280]{1,0:T(8,128)(2,1)S(1)}, u32[]{:S(2)}, u32[]{:S(2)}) collective-permute-start(bf16[32,1280]{1,0:T(8,128)(2,1)S(1)} %get-tuple-element.19.refs_0_.refs_9_), channel_id=1, source_target_pairs={{0,6},{1,7},{2,4},{3,5},{4,2},{5,3},{6,0},{7,1},{8,14},{9,15},{10,... | collective-permute-start | bytes 245768 | tf_op jit(solution)/shard_map/ppermute | solution.py:20
  10.3 10.0 %collective-permute-start.8 = (bf16[64,1280]{1,0:T(8,128)(2,1)S(1)}, bf16[64,1280]{1,0:T(8,128)(2,1)S(1)}, u32[]{:S(2)}, u32[]{:S(2)}) collective-permute-start(bf16[64,1280]{1,0:T(8,128)(2,1)S(1)} %join.6), channel_id=1, source_target_pairs={{0,12},{1,15},{2,14},{3,13},{4,8},{5,11},{6,10},{7,9},{8,4},{9,7},... | collective-permute-start | bytes 491528 | tf_op jit(solution)/shard_map/ppermute | solution.py:20
  11.9 9.0 %collective-permute-start.7 = (bf16[64,1280]{1,0:T(8,128)(2,1)S(1)}, bf16[64,1280]{1,0:T(8,128)(2,1)S(1)}, u32[]{:S(2)}, u32[]{:S(2)}) collective-permute-start(bf16[64,1280]{1,0:T(8,128)(2,1)S(1)} %join.6), channel_id=1, source_target_pairs={{0,8},{1,11},{2,10},{3,9},{4,12},{5,15},{6,14},{7,13},{8,0},{9,3},... | collective-permute-start | bytes 491528 | tf_op jit(solution)/shard_map/ppermute | solution.py:20
  12.3 8.6 %collective-permute-start.6 = (bf16[64,1280]{1,0:T(8,128)(2,1)S(1)}, bf16[64,1280]{1,0:T(8,128)(2,1)S(1)}, u32[]{:S(2)}, u32[]{:S(2)}) collective-permute-start(bf16[64,1280]{1,0:T(8,128)(2,1)S(1)} %join.6), channel_id=1, source_target_pairs={{0,2},{1,5},{2,0},{3,7},{4,6},{5,1},{6,4},{7,3},{8,10},{9,13},{10,... | collective-permute-start | bytes 491528 | tf_op jit(solution)/shard_map/ppermute | solution.py:20
  16.8 5.4 %collective-permute-start.3 = (bf16[256,128]{1,0:T(8,128)(2,1)S(1)}, bf16[256,128]{1,0:T(8,128)(2,1)S(1)}, u32[]{:S(2)}, u32[]{:S(2)}) collective-permute-start(bf16[256,128]{1,0:T(8,128)(2,1)S(1)} %get-tuple-element.13.refs_0_.refs_8_), channel_id=1, source_target_pairs={{0,8},{1,9},{2,10},{3,11},{4,12},{5,13},{6,14},{7,15},{8,0},{9,1},... | collective-permute-start | bytes 196616 | tf_op jit(solution)/shard_map/ppermute | solution.py:20
  20.9 2.0 %collective-permute-start.9 = (bf16[224,1280]{1,0:T(8,128)(2,1)S(1)}, bf16[224,1280]{1,0:T(8,128)(2,1)S(1)}, u32[]{:S(2)}, u32[]{:S(2)}) collective-permute-start(bf16[224,1280]{1,0:T(8,128)(2,1)S(1)} %join.7.refs_11_), channel_id=1, source_target_pairs={{0,1},{1,0},{2,3},{3,2},{4,5},{5,4},{6,7},{7,6},{8,9},{9,8},{10,11... | collective-permute-start | bytes 1720328 | tf_op jit(solution)/shard_map/ppermute | solution.py:384
  22.2 0.7 %copy-start.3 = (bf16[3,32]{1,0:T(4,128)(2,1)S(1)}, bf16[3,32]{1,0:T(4,128)(2,1)}, u32[]{:S(2)}) copy-start(bf16[3,32]{1,0:T(4,128)(2,1)} %refs_1_.1) | copy-start | bytes 580

commit v4 on v3

--- a/solution.py
+++ b/solution.py
@@ -27,59 +27,40 @@
     return jnp.sum(jnp.where(across == down, row, jnp.zeros_like(row)), axis=1, keepdims=True)
 
 
-def live_rows(dead_ref, rows, columns):
-    live_from = dead_ref[0:1, 0:columns]
-    return lax.broadcasted_iota(jnp.int32, (rows, columns), 0) >= live_from
-
-
-def pack_kernel(
-    levels,
-    dead_ref,
-    leaf_ref,
-    shift_ref,
-    panel_ref,
-    inv_ref,
-    rhs_ref,
-    noise_ref,
-    low_ref,
-    top_ref,
-    edge_ref,
-    moved_ref,
-    arrived,
-):
-    row_count, samples = edge_ref.shape[0], shift_ref.shape[1]
-    subtree_rows = shift_ref.shape[0]
-    copies = [
-        pltpu.make_async_copy(shift_ref, moved_ref, arrived.at[0]),
-        pltpu.make_async_copy(leaf_ref.at[pl.ds(subtree_rows - row_count, row_count)], edge_ref, arrived.at[1]),
-    ]
+def live_rows(blocks_ref, shape, dimension):
+    return lax.broadcasted_iota(jnp.int32, shape, dimension) >= shape[dimension] - blocks_ref[0, 0] * BLOCK
+
+
+def pack_kernel(levels, blocks_ref, *refs):
+    sources, (low_ref, top_ref), moved, arrived = refs[:6], refs[6:8], refs[8:14], refs[14]
+    rows = sources[0].shape[0]
+    row_count = moved[0].shape[0]
+    parts = (sources[0].at[pl.ds(rows - row_count, row_count)],) + sources[1:]
+    copies = [pltpu.make_async_copy(part, ref, arrived.at[n]) for n, (part, ref) in enumerate(zip(parts, moved))]
+    for copy in copies:
+        copy.start()
+    edge_ref, shift_ref, panel_ref, inv_ref, rhs_ref, noise_ref = moved
+    samples = shift_ref.shape[1]
+    for copy in copies[2:]:
+        copy.wait()
+    unit = panel_ref.shape[1] // (2 ** (levels + 1) - 2)
     at, offset = samples, 0
-    unit = panel_ref.shape[1] // (2 ** (levels + 1) - 2)
     for height in range(1, levels + 1):
         span = 2**height * unit
         out = low_ref if height < levels else top_ref
         at = at if height < levels else 0
-        for source, width in (
-            (panel_ref.at[:, pl.ds(offset, span)], span),
-            (inv_ref.at[:, pl.ds(offset, span)], span),
-            (rhs_ref.at[height - 1], samples),
-            (noise_ref.at[height - 1], samples),
-        ):
-            copies.append(
-                pltpu.make_async_copy(source, out.at[:, pl.ds(at, width)], arrived.at[len(copies)])
-            )
-            at += width
+        out[:, at : at + span] = panel_ref[:, offset : offset + span]
+        out[:, at + span : at + 2 * span] = inv_ref[:, offset : offset + span]
+        out[:, at + 2 * span : at + 2 * span + samples] = rhs_ref[height - 1]
+        out[:, at + 2 * span + samples : at + 2 * span + 2 * samples] = noise_ref[height - 1]
+        at += 2 * span + 2 * samples
         offset += span
-    for copy in copies:
-        copy.start()
     for copy in copies[:2]:
         copy.wait()
-    shift = moved_ref[...]
-    shift = jnp.where(live_rows(dead_ref, *shift.shape), shift, jnp.zeros_like(shift))
-    boundary = jnp.dot(edge_ref[...], shift, preferred_element_type=jnp.float32)
+    inverse = edge_ref[...]
+    inverse = jnp.where(live_rows(blocks_ref, inverse.shape, 1), inverse, jnp.zeros_like(inverse))
+    boundary = jnp.dot(inverse, shift_ref[...], preferred_element_type=jnp.float32)
     low_ref[:, :samples] = boundary.astype(jnp.bfloat16)
-    for copy in copies[2:]:
-        copy.wait()
 
 
 def join_kernel(*refs):
@@ -112,7 +93,7 @@
 
 
 def low_kernel(levels, unit, pieces, *refs):
-    piece_refs, (whole_ref, *solved_refs) = refs[:-levels], refs[-levels:]
+    piece_refs, (whole_ref, *solved_refs) = refs[: -levels - 1], refs[-levels:]
     row_count = unit // 2
     place(pieces, piece_refs, whole_ref, row_count, 2 ** (levels - 1))
     samples = solved_refs[0].shape[1]
@@ -130,18 +111,20 @@
 
 def leaf_kernel(
     row_count,
-    dead_ref,
+    blocks_ref,
     leaf_ref,
     shift_ref,
     noise_ref,
     dev_ref,
+    sep_dev_ref,
     base_ref,
     edge_ref,
     inner_ref,
     scale_ref,
+    sep_scale_ref,
 ):
     rows, samples = shift_ref.shape
-    live = live_rows(dead_ref, rows, samples)
+    live = live_rows(blocks_ref, (rows, samples), 0)
     shift = shift_ref[...]
     shift = jnp.where(live, shift, jnp.zeros_like(shift))
     zero = jnp.float32(0.0)
@@ -159,10 +142,13 @@
         part = slice(block * BLOCK, (block + 1) * BLOCK)
         column = column_of(dev_ref[:, part].astype(jnp.float32))
         scale_ref[part, :] = jnp.where(live[part, :], jnp.broadcast_to(column, (BLOCK, samples)), zero)
+    for height in range(sep_scale_ref.shape[0]):
+        column = column_of(sep_dev_ref[height : height + 1, :].astype(jnp.float32))
+        sep_scale_ref[height] = jnp.broadcast_to(column, (row_count, samples))
 
 
 def top_kernel(levels, unit, pieces, *refs):
-    low_ref, dev_ref, partner_ref, base_ref, edge_ref, inner_ref, scale_ref = refs[:7]
+    low_ref, sep_scale_ref, partner_ref, base_ref, edge_ref, inner_ref, scale_ref = refs[:7]
     solved_refs = refs[7 : 7 + levels - 1]
     out_ref, sample_ref, whole_ref, child_ref, x_ref, sum_ref = refs[-6:]
     piece_refs = refs[7 + levels - 1 : -6]
@@ -197,8 +183,7 @@
         pushed = jnp.dot(x, source[rows, at : at + span], preferred_element_type=jnp.float32)
         x_ref[0:span, :] = x.astype(jnp.float32).T
         mine = pl.ds(pl.multiple_of(((leaf & (2**height - 1)) * 2 + section) * row_count, row_count), row_count)
-        scale = column_of(dev_ref[height - 1 : height, :].astype(jnp.float32))
-        sample_ref[height - 1] = (scale * x_ref[mine, :]).astype(jnp.bfloat16)
+        sample_ref[height - 1] = (sep_scale_ref[height - 1] * x_ref[mine, :]).astype(jnp.bfloat16)
         if height > 1:
             upper = leaf >> (height - 1) & 1
             correction = jnp.where(upper == 1, pushed[:, span // 2 :], pushed[:, : span // 2])
@@ -351,6 +336,7 @@
     levels, _, samples = sep_rhs.shape
     unit = 2 * row_count
     vmem = pl.BlockSpec(memory_space=pltpu.VMEM)
+    smem = pl.BlockSpec(memory_space=pltpu.SMEM)
 
     def params(mib):
         return pltpu.CompilerParams(vmem_limit_bytes=mib * 2**20)
@@ -362,23 +348,26 @@
     def in_hbm(array):
         return pltpu.with_memory_space_constraint(array, pltpu.HBM)
 
-    dead = jnp.full((8, samples), subtree_rows - subtree_blocks[0, 0] * BLOCK, jnp.int32)
     low, top = pl.pallas_call(
         functools.partial(pack_kernel, levels),
         out_shape=(
             jax.ShapeDtypeStruct((row_count, low_columns), jnp.bfloat16),
             jax.ShapeDtypeStruct((row_count, top_columns), jnp.bfloat16),
         ),
-        in_specs=[vmem] + [hbm] * 6,
+        in_specs=[smem] + [hbm] * 6,
         out_specs=(vmem, vmem),
         scratch_shapes=[
             pltpu.VMEM((row_count, subtree_rows), jnp.bfloat16),
-            pltpu.VMEM((subtree_rows, samples), jnp.bfloat16),
-            pltpu.SemaphoreType.DMA((2 + 4 * levels,)),
+            pltpu.VMEM(subtree_shift_rhs.shape, jnp.bfloat16),
+            pltpu.VMEM(sep_panel.shape, jnp.bfloat16),
+            pltpu.VMEM(sep_inv.shape, jnp.bfloat16),
+            pltpu.VMEM(sep_rhs.shape, jnp.bfloat16),
+            pltpu.VMEM(sep_noise.shape, jnp.bfloat16),
+            pltpu.SemaphoreType.DMA((6,)),
         ],
         compiler_params=params(4),
         name="pack",
-    )(dead, *(in_hbm(x) for x in (leaf_inv, subtree_shift_rhs, sep_panel, sep_inv, sep_rhs, sep_noise)))
+    )(subtree_blocks, *(in_hbm(x) for x in (leaf_inv, subtree_shift_rhs, sep_panel, sep_inv, sep_rhs, sep_noise)))
 
     def swap(block):
         return lax.ppermute(block, "sec", [(0, 1), (1, 0)])
@@ -397,14 +386,14 @@
 
     quad = 2 ** (levels - 1)
     near = join([low] + [to_chips(low, (distance, distance)) for distance in range(1, quad)])
-    near = lax.all_gather(near, "sec", axis=0, tiled=True)
+    passed = swap(near)
     quarter = []
-    for owner in range(2):
+    for turned, array in enumerate((near, passed)):
         for distance in range(quad):
-            quarter.append((near, (owner * quad + distance) * row_count, (distance,), (owner,)))
+            quarter.append((array, distance * row_count, (distance, distance), turned))
 
     top_other = swap(top)
-    top_pair = join([top, top_other])
+    top_pair = join([top, top_other], flops=10**10)
 
     def listed(pieces):
         arrays, places = [], []
@@ -415,42 +404,46 @@
             places.append((which, start, distances, turned))
         return arrays, places
 
-    arrays, places = listed(quarter)
-    low_whole, *solved = pl.pallas_call(
-        functools.partial(low_kernel, levels, unit, places),
-        out_shape=[jax.ShapeDtypeStruct((quad * unit, low_columns), jnp.bfloat16)]
-        + [jax.ShapeDtypeStruct((quad * unit, samples), jnp.bfloat16)] * (levels - 1),
-        in_specs=[vmem] * len(arrays),
-        out_specs=[vmem] * levels,
-        compiler_params=params(8),
-        name="low",
-    )(*arrays)
-    partner = to_chips(solved[-1], (quad, quad))
-
-    trips = [(top, (3, 3)), (top_pair, (1, 2)), (top_pair, (4, 5)), (top_pair, (6, 7))]
-    here = join([to_chips(block, distances) for block, distances in trips], solved[-1])
-    there = swap(here)
-    far = [(top, 0, (0, 0), 0), (top_other, 0, (0, 0), 1)]
-    row = 0
-    for block, (first, second) in trips:
-        for turned in range(block.shape[0] // row_count):
-            far.append((here, row, (first, second), turned))
-            far.append((there, row, (second, first), 1 - turned))
-            row += row_count
-
-    base, edge, inner, scale = pl.pallas_call(
+    base, edge, inner, scale, sep_scale = pl.pallas_call(
         functools.partial(leaf_kernel, row_count),
         out_shape=(
             jax.ShapeDtypeStruct((subtree_rows, samples), jnp.float32),
             jax.ShapeDtypeStruct((row_count, samples), jnp.float32),
             jax.ShapeDtypeStruct((subtree_rows, row_count), jnp.bfloat16),
             jax.ShapeDtypeStruct((subtree_rows, samples), jnp.float32),
+            jax.ShapeDtypeStruct((levels, row_count, samples), jnp.float32),
         ),
-        in_specs=[vmem] * 5,
-        out_specs=(vmem,) * 4,
+        in_specs=[smem] + [vmem] * 5,
+        out_specs=(vmem,) * 5,
         compiler_params=params(12),
+        cost_estimate=pl.CostEstimate(flops=10**10, bytes_accessed=1, transcendentals=0),
         name="leaf",
-    )(dead, leaf_inv, subtree_shift_rhs, leaf_noise, leaf_dev[None, :])
+    )(subtree_blocks, leaf_inv, subtree_shift_rhs, leaf_noise, leaf_dev[None, :], sep_dev)
+
+    arrays, places = listed(quarter)
+    low_whole, *solved = pl.pallas_call(
+        functools.partial(low_kernel, levels, unit, places),
+        out_shape=[jax.ShapeDtypeStruct((quad * unit, low_columns), jnp.bfloat16)]
+        + [jax.ShapeDtypeStruct((quad * unit, samples), jnp.bfloat16)] * (levels - 1),
+        in_specs=[vmem] * len(arrays) + [pl.BlockSpec(memory_space=pl.ANY)],
+        out_specs=[vmem] * levels,
+        compiler_params=params(8),
+        name="low",
+    )(*arrays, edge)
+    partner = to_chips(solved[-1], (quad, quad))
+
+    trips = [(join([top], top_pair), (2, 2)), (top_pair, (1, 3)), (top_pair, (4, 5)), (top_pair, (6, 7))]
+    far = [(top, 0, (0, 0), 0), (top_other, 0, (0, 0), 1)]
+    arrived = [to_chips(block, distances) for block, distances in trips]
+    for chosen in ((2, 3), (0, 1)):
+        here = join([arrived[index] for index in chosen], solved[-1])
+        there = swap(here)
+        row = 0
+        for block, (first, second) in (trips[index] for index in chosen):
+            for turned in range(block.shape[0] // row_count):
+                far.append((here, row, (first, second), turned))
+                far.append((there, row, (second, first), 1 - turned))
+                row += row_count
 
     edge = join([edge], partner, flops=10**10)
     arrays, places = listed(far)
@@ -471,7 +464,7 @@
         ],
         compiler_params=params(16),
         name="top",
-    )(low_whole, sep_dev, partner, base, edge, inner, scale, *solved, *arrays)
+    )(low_whole, sep_scale, partner, base, edge, inner, scale, *solved, *arrays)
 
 
 def solution(mesh):

time: 25.8 us -> 24.4 us (0.946)
  blocking collectives: 2.43 us -> 0 us
  starting transfers between devices: 12.5 us -> 13.8 us
    all_gather x1 -> x0, blocking collectives: 2.43 us -> none  [on_device(): near = lax.all_gather(near, 'sec', axis=0, tiled=True)]
    ppermute x2 -> x4, starting transfers between devices: 0.07 us -> 1.23 us  [swap(): return lax.ppermute(block, 'sec', [(0, 1), (1, 0)])]
    ppermute x2 -> x4, waiting for transfers between devices: 0.73 us -> 0.37 us  [swap(): return lax.ppermute(block, 'sec', [(0, 1), (1, 0)])]
    ppermute x8, waiting for transfers between devices: 1.86 us -> 2.21 us  [to_chips(): return lax.ppermute(block, AXES, route)]
  transfers between devices with their start and end apart: 10 -> 12, of which waited for: 3 -> 3; matrix products, arithmetic and copies ran while one was open for 0% -> 0% of each run, Pallas kernels for 10% -> 10%
where the time goes in v4:
time: 24.4 us; the launch traced here: 24.3 us
  starting transfers between devices  13.8 us (57%)
  Pallas kernels  6.42 us (26%)
  waiting for transfers between devices  2.58 us (11%)
  between operations  1.44 us (6%)
    ppermute x8, starting transfers between devices, to_chips(): return lax.ppermute(block, AXES, route)  12.6 us
    pallas_call x1, Pallas kernels, on_device(): pl.pallas_call(functools.partial(top_kernel, levels, unit, places), out_s...  2.65 us
    ppermute x8, waiting for transfers between devices, to_chips(): return lax.ppermute(block, AXES, route)  2.21 us
    pallas_call x1, Pallas kernels, on_device(): pl.pallas_call(functools.partial(leaf_kernel, row_count), out_shape=(jax....  1.71 us
    ppermute x4, starting transfers between devices, swap(): return lax.ppermute(block, 'sec', [(0, 1), (1, 0)])  1.23 us
    pallas_call x1, Pallas kernels, on_device(): pl.pallas_call(functools.partial(pack_kernel, levels), out_shape=(jax.Sha...  1.22 us
    pallas_call x1, Pallas kernels, on_device(): pl.pallas_call(functools.partial(low_kernel, levels, unit, places), out_s...  0.75 us
  transfers between devices with their start and end apart: 12, of which 3 were waited for; matrix products, arithmetic and copies ran while one was open for 0% of the time, Pallas kernels for 10%

profile of v4, /device:TPU:0, one launch (start us, length us, event | category | flops | bytes accessed | tf_op | source)
XLA Modules:
  0.0 24.3 jit_solution(11172643719664497054)
XLA Ops:
  0.6 0.0 copy-start.4
  1.3 1.2 %pack.1 = (bf16[32,1408]{1,0:T(8,128)(2,1)S(1)}, bf16[32,1280]{1,0:T(8,128)(2,1)S(1)}) custom-call(s32[1,1]{1,0:T(1,128)S(6)} %copy.12.blocks_ref, bf16[1024,1024]{1,0:T(8,128)(2,1)} %leaf_ref.1, bf16[1024,128]{1,0:T(8,128)(2,1)} %shift_ref.1, bf16[32,896]{1,0:T(8,128)(2,1)} %refs_2_.1, bf16[32,896]{1,0:T(8,128)(2,1)} %refs_3_.1, ...), custom_call_target="tpu_custom_call" | custom-call | tf_op jit(solution)/shard_map/pack/pallas_call | solution.py:351
  2.5 0.5 %collective-permute-start.5 = (bf16[32,1280]{1,0:T(8,128)(2,1)S(1)}, bf16[32,1280]{1,0:T(8,128)(2,1)S(1)}, u32[]{:S(2)}, u32[]{:S(2)}) collective-permute-start(bf16[32,1280]{1,0:T(8,128)(2,1)S(1)} %get-tuple-element.21.refs_0_.refs_1_.refs_9_), channel_id=1, source_target_pairs={{0,1},{1,0},{2,3},{3,2},{4,5},{5,4},{6,7},{7,6},{8,9},{9,8},{10,11... | collective-permute-start | bytes 245768 | tf_op jit(solution)/shard_map/ppermute | solution.py:373
  3.0 3.5 %collective-permute-start.2 = (bf16[32,1408]{1,0:T(8,128)(2,1)S(1)}, bf16[32,1408]{1,0:T(8,128)(2,1)S(1)}, u32[]{:S(2)}, u32[]{:S(2)}) collective-permute-start(bf16[32,1408]{1,0:T(8,128)(2,1)S(1)} %get-tuple-element.12.refs_0_), channel_id=1, source_target_pairs={{0,6},{1,7},{2,4},{3,5},{4,2},{5,3},{6,0},{7,1},{8,14},{9,15},{10,... | collective-permute-start | bytes 270344 | tf_op jit(solution)/shard_map/ppermute | solution.py:20
  6.6 0.5 %collective-permute-start.1 = (bf16[32,1408]{1,0:T(8,128)(2,1)S(1)}, bf16[32,1408]{1,0:T(8,128)(2,1)S(1)}, u32[]{:S(2)}, u32[]{:S(2)}) collective-permute-start(bf16[32,1408]{1,0:T(8,128)(2,1)S(1)} %get-tuple-element.12.refs_0_), channel_id=1, source_target_pairs={{0,4},{1,5},{2,6},{3,7},{4,0},{5,1},{6,2},{7,3},{8,12},{9,13},{10,... | collective-permute-start | bytes 270344 | tf_op jit(solution)/shard_map/ppermute | solution.py:20
  7.1 0.1 collective-permute-start
  7.2 0.0 copy-done.4
  7.2 0.0 copy-start
  7.2 0.0 copy-start.1
  7.2 0.0 copy-start.2
  7.2 0.0 copy-start.3
  7.3 0.0 collective-permute-done.5.refs_1_.refs_10_
  7.3 2.0 %collective-permute-start.10 = (bf16[64,1280]{1,0:T(8,128)(2,1)S(1)}, bf16[64,1280]{1,0:T(8,128)(2,1)S(1)}, u32[]{:S(2)}, u32[]{:S(2)}) collective-permute-start(bf16[64,1280]{1,0:T(8,128)(2,1)S(1)} %join.8.refs_0_), channel_id=1, source_target_pairs={{0,2},{1,7},{2,0},{3,5},{4,6},{5,3},{6,4},{7,1},{8,10},{9,15},{10,... | collective-permute-start | bytes 491528 | tf_op jit(solution)/shard_map/ppermute | solution.py:20
  9.3 2.5 %collective-permute-start.7 = (bf16[64,1280]{1,0:T(8,128)(2,1)S(1)}, bf16[64,1280]{1,0:T(8,128)(2,1)S(1)}, u32[]{:S(2)}, u32[]{:S(2)}) collective-permute-start(bf16[64,1280]{1,0:T(8,128)(2,1)S(1)} %join.8.refs_0_), channel_id=1, source_target_pairs={{0,12},{1,15},{2,14},{3,13},{4,8},{5,11},{6,10},{7,9},{8,4},{9,7},... | collective-permute-start | bytes 491528 | tf_op jit(solution)/shard_map/ppermute | solution.py:20
  11.8 0.0 collective-permute-done.2.refs_3_
  11.8 0.5 %collective-permute-start.6 = (bf16[64,1280]{1,0:T(8,128)(2,1)S(1)}, bf16[64,1280]{1,0:T(8,128)(2,1)S(1)}, u32[]{:S(2)}, u32[]{:S(2)}) collective-permute-start(bf16[64,1280]{1,0:T(8,128)(2,1)S(1)} %join.8.refs_0_), channel_id=1, source_target_pairs={{0,8},{1,11},{2,10},{3,9},{4,12},{5,15},{6,14},{7,13},{8,0},{9,3},... | collective-permute-start | bytes 491528 | tf_op jit(solution)/shard_map/ppermute | solution.py:20
  12.2 0.0 collective-permute-done.1.refs_2_
  12.2 1.8 %collective-permute-start.9 = (bf16[32,1280]{1,0:T(8,128)(2,1)S(1)}, bf16[32,1280]{1,0:T(8,128)(2,1)S(1)}, u32[]{:S(2)}, u32[]{:S(2)}) collective-permute-start(bf16[32,1280]{1,0:T(8,128)(2,1)S(1)} %join.10), channel_id=1, source_target_pairs={{0,4},{1,5},{2,6},{3,7},{4,0},{5,1},{6,2},{7,3},{8,12},{9,13},{10,... | collective-permute-start | bytes 245768 | tf_op jit(solution)/shard_map/ppermute | solution.py:20
  14.1 0.0 collective-permute-done.refs_1_
  14.1 0.1 collective-permute-start.3
  14.2 0.0 copy-done
  14.2 0.0 copy-done.1
  14.2 0.0 copy-done.2
  14.2 0.0 copy-done.3
  14.2 1.7 %leaf.1 = (f32[1024,128]{1,0:T(8,128)S(1)}, f32[32,128]{1,0:T(8,128)S(1)}, bf16[1024,32]{1,0:T(8,128)(2,1)S(1)}, f32[1024,128]{1,0:T(8,128)S(1)}, f32[3,32,128]{2,1,0:T(8,128)S(1)}) custom-call(s32[1,1]{1,0:T(1,128)S(6)} %copy.12.blocks_ref, bf16[1024,1024]{1,0:T(8,128)(2,1)S(1)} %copy-done, bf16[1024,128]{1,0:T(8,128)(2,1)S(1)} %copy-done.1, ...), custom_call_target="tpu_custom_call" | custom-call | flops 10000000000 | bytes 1 | tf_op jit(solution)/shard_map/leaf/pallas_call | solution.py:407
  16.0 0.0 collective-permute-done.3.refs_1_
  16.0 0.8 %low.1 = (bf16[256,1408]{1,0:T(8,128)(2,1)S(1)}, bf16[256,128]{1,0:T(8,128)(2,1)S(1)}, bf16[256,128]{1,0:T(8,128)(2,1)S(1)}) custom-call(bf16[128,1408]{1,0:T(8,128)(2,1)S(1)} %join.6.refs_0_, bf16[128,1408]{1,0:T(8,128)(2,1)S(1)} %collective-permute-done.3.refs_1_, f32[32,128]{1,0:T(8,128)S(1)} %get-tuple-element.13.refs_2_.refs_1_), custom_call_target="tpu_custom_call" | custom-call | tf_op jit(solution)/shard_map/low/pallas_call | solution.py:424
  16.7 1.6 %collective-permute-start.4 = (bf16[256,128]{1,0:T(8,128)(2,1)S(1)}, bf16[256,128]{1,0:T(8,128)(2,1)S(1)}, u32[]{:S(2)}, u32[]{:S(2)}) collective-permute-start(bf16[256,128]{1,0:T(8,128)(2,1)S(1)} %get-tuple-element.16.refs_0_.refs_8_), channel_id=1, source_target_pairs={{0,8},{1,9},{2,10},{3,11},{4,12},{5,13},{6,14},{7,15},{8,0},{9,1},... | collective-permute-start | bytes 196616 | tf_op jit(solution)/shard_map/ppermute | solution.py:20
  18.4 1.2 %collective-permute-done.9.refs_1_ = bf16[32,1280]{1,0:T(8,128)(2,1)S(1)} collective-permute-done((bf16[32,1280]{1,0:T(8,128)(2,1)S(1)}, bf16[32,1280]{1,0:T(8,128)(2,1)S(1)}, u32[]{:S(2)}, u32[]{:S(2)}) %collective-permute-start.9) | collective-permute-done | bytes 81952 | tf_op jit(solution)/shard_map/ppermute | solution.py:20
  19.6 0.0 collective-permute-done.10.refs_2_
  19.6 0.2 collective-permute-start.11
  19.8 0.0 collective-permute-done.7.refs_2_
  19.8 0.0 collective-permute-done.6.refs_1_
  19.8 0.5 %collective-permute-start.8 = (bf16[128,1280]{1,0:T(8,128)(2,1)S(1)}, bf16[128,1280]{1,0:T(8,128)(2,1)S(1)}, u32[]{:S(2)}, u32[]{:S(2)}) collective-permute-start(bf16[128,1280]{1,0:T(8,128)(2,1)S(1)} %join.9.refs_11_), channel_id=1, source_target_pairs={{0,1},{1,0},{2,3},{3,2},{4,5},{5,4},{6,7},{7,6},{8,9},{9,8},{10,11... | collective-permute-start | bytes 983048 | tf_op jit(solution)/shard_map/ppermute | solution.py:373
  20.3 1.0 %collective-permute-done.4.refs_0_.refs_2_ = bf16[256,128]{1,0:T(8,128)(2,1)S(1)} collective-permute-done((bf16[256,128]{1,0:T(8,128)(2,1)S(1)}, bf16[256,128]{1,0:T(8,128)(2,1)S(1)}, u32[]{:S(2)}, u32[]{:S(2)}) %collective-permute-start.4) | collective-permute-done | bytes 65568 | tf_op jit(solution)/shard_map/ppermute | solution.py:20
  21.3 0.0 collective-permute-done.11.refs_14_
  21.3 0.4 %collective-permute-done.8.refs_12_ = bf16[128,1280]{1,0:T(8,128)(2,1)S(1)} collective-permute-done((bf16[128,1280]{1,0:T(8,128)(2,1)S(1)}, bf16[128,1280]{1,0:T(8,128)(2,1)S(1)}, u32[]{:S(2)}, u32[]{:S(2)}) %collective-permute-start.8) | collective-permute-done | bytes 327712 | tf_op jit(solution)/shard_map/ppermute | solution.py:373
  21.6 2.7 %top.1 = (bf16[1024,128]{1,0:T(8,128)(2,1)}, bf16[3,32,128]{2,1,0:T(8,128)(2,1)}) custom-call(bf16[256,1408]{1,0:T(8,128)(2,1)S(1)} %get-tuple-element.14.refs_0_, f32[3,32,128]{2,1,0:T(8,128)S(1)} %get-tuple-element.15.refs_1_, bf16[256,128]{1,0:T(8,128)(2,1)S(1)} %collective-permute-done.4.refs_0_.refs_2_, f32[1024,128]{1,0:T(8,128)S(1)} %get-tuple-element.17.refs_3_, ...), custom_call_target="tpu_custom_call" | custom-call | tf_op jit(solution)/shard_map/top/pallas_call | solution.py:451
  (7 shorter events, 0.1 us)
Async XLA Ops:
  0.6 6.6 %copy-start.4 = (bf16[1024]{0:T(1024)(128)(2,1)S(1)}, bf16[1024]{0:T(1024)(128)(2,1)}, u32[]{:S(2)}) copy-start(bf16[1024]{0:T(1024)(128)(2,1)} %param.14) | copy-start | bytes 6148
  2.5 4.7 %collective-permute-start.5 = (bf16[32,1280]{1,0:T(8,128)(2,1)S(1)}, bf16[32,1280]{1,0:T(8,128)(2,1)S(1)}, u32[]{:S(2)}, u32[]{:S(2)}) collective-permute-start(bf16[32,1280]{1,0:T(8,128)(2,1)S(1)} %get-tuple-element.21.refs_0_.refs_1_.refs_9_), channel_id=1, source_target_pairs={{0,1},{1,0},{2,3},{3,2},{4,5},{5,4},{6,7},{7,6},{8,9},{9,8},{10,11... | collective-permute-start | bytes 245768 | tf_op jit(solution)/shard_map/ppermute | solution.py:373
  3.0 8.8 %collective-permute-start.2 = (bf16[32,1408]{1,0:T(8,128)(2,1)S(1)}, bf16[32,1408]{1,0:T(8,128)(2,1)S(1)}, u32[]{:S(2)}, u32[]{:S(2)}) collective-permute-start(bf16[32,1408]{1,0:T(8,128)(2,1)S(1)} %get-tuple-element.12.refs_0_), channel_id=1, source_target_pairs={{0,6},{1,7},{2,4},{3,5},{4,2},{5,3},{6,0},{7,1},{8,14},{9,15},{10,... | collective-permute-start | bytes 270344 | tf_op jit(solution)/shard_map/ppermute | solution.py:20
  6.6 5.7 %collective-permute-start.1 = (bf16[32,1408]{1,0:T(8,128)(2,1)S(1)}, bf16[32,1408]{1,0:T(8,128)(2,1)S(1)}, u32[]{:S(2)}, u32[]{:S(2)}) collective-permute-start(bf16[32,1408]{1,0:T(8,128)(2,1)S(1)} %get-tuple-element.12.refs_0_), channel_id=1, source_target_pairs={{0,4},{1,5},{2,6},{3,7},{4,0},{5,1},{6,2},{7,3},{8,12},{9,13},{10,... | collective-permute-start | bytes 270344 | tf_op jit(solution)/shard_map/ppermute | solution.py:20
  7.1 7.0 %collective-permute-start = (bf16[32,1408]{1,0:T(8,128)(2,1)S(1)}, bf16[32,1408]{1,0:T(8,128)(2,1)S(1)}, u32[]{:S(2)}, u32[]{:S(2)}) collective-permute-start(bf16[32,1408]{1,0:T(8,128)(2,1)S(1)} %get-tuple-element.12.refs_0_), channel_id=1, source_target_pairs={{0,2},{1,3},{2,0},{3,1},{4,6},{5,7},{6,4},{7,5},{8,10},{9,11},{10,... | collective-permute-start | bytes 270344 | tf_op jit(solution)/shard_map/ppermute | solution.py:20
  7.2 7.0 %copy-start = (bf16[1024,1024]{1,0:T(8,128)(2,1)S(1)}, bf16[1024,1024]{1,0:T(8,128)(2,1)}, u32[]{:S(2)}) copy-start(bf16[1024,1024]{1,0:T(8,128)(2,1)} %leaf_ref.1) | copy-start | bytes 6291460
  7.2 7.0 %copy-start.1 = (bf16[1024,128]{1,0:T(8,128)(2,1)S(1)}, bf16[1024,128]{1,0:T(8,128)(2,1)}, u32[]{:S(2)}) copy-start(bf16[1024,128]{1,0:T(8,128)(2,1)} %shift_ref.1) | copy-start | bytes 786436
  7.2 7.0 %copy-start.2 = (bf16[1024,128]{1,0:T(8,128)(2,1)S(1)}, bf16[1024,128]{1,0:T(8,128)(2,1)}, u32[]{:S(2)}) copy-start(bf16[1024,128]{1,0:T(8,128)(2,1)} %noise_ref.1) | copy-start | bytes 786436
  7.2 7.0 %copy-start.3 = (bf16[3,32]{1,0:T(4,128)(2,1)S(1)}, bf16[3,32]{1,0:T(4,128)(2,1)}, u32[]{:S(2)}) copy-start(bf16[3,32]{1,0:T(4,128)(2,1)} %sep_dev_ref.1) | copy-start | bytes 580
  7.3 12.2 %collective-permute-start.10 = (bf16[64,1280]{1,0:T(8,128)(2,1)S(1)}, bf16[64,1280]{1,0:T(8,128)(2,1)S(1)}, u32[]{:S(2)}, u32[]{:S(2)}) collective-permute-start(bf16[64,1280]{1,0:T(8,128)(2,1)S(1)} %join.8.refs_0_), channel_id=1, source_target_pairs={{0,2},{1,7},{2,0},{3,5},{4,6},{5,3},{6,4},{7,1},{8,10},{9,15},{10,... | collective-permute-start | bytes 491528 | tf_op jit(solution)/shard_map/ppermute | solution.py:20
  9.3 10.5 %collective-permute-start.7 = (bf16[64,1280]{1,0:T(8,128)(2,1)S(1)}, bf16[64,1280]{1,0:T(8,128)(2,1)S(1)}, u32[]{:S(2)}, u32[]{:S(2)}) collective-permute-start(bf16[64,1280]{1,0:T(8,128)(2,1)S(1)} %join.8.refs_0_), channel_id=1, source_target_pairs={{0,12},{1,15},{2,14},{3,13},{4,8},{5,11},{6,10},{7,9},{8,4},{9,7},... | collective-permute-start | bytes 491528 | tf_op jit(solution)/shard_map/ppermute | solution.py:20
  11.8 8.0 %collective-permute-start.6 = (bf16[64,1280]{1,0:T(8,128)(2,1)S(1)}, bf16[64,1280]{1,0:T(8,128)(2,1)S(1)}, u32[]{:S(2)}, u32[]{:S(2)}) collective-permute-start(bf16[64,1280]{1,0:T(8,128)(2,1)S(1)} %join.8.refs_0_), channel_id=1, source_target_pairs={{0,8},{1,11},{2,10},{3,9},{4,12},{5,15},{6,14},{7,13},{8,0},{9,3},... | collective-permute-start | bytes 491528 | tf_op jit(solution)/shard_map/ppermute | solution.py:20
  12.2 7.3 %collective-permute-start.9 = (bf16[32,1280]{1,0:T(8,128)(2,1)S(1)}, bf16[32,1280]{1,0:T(8,128)(2,1)S(1)}, u32[]{:S(2)}, u32[]{:S(2)}) collective-permute-start(bf16[32,1280]{1,0:T(8,128)(2,1)S(1)} %join.10), channel_id=1, source_target_pairs={{0,4},{1,5},{2,6},{3,7},{4,0},{5,1},{6,2},{7,3},{8,12},{9,13},{10,... | collective-permute-start | bytes 245768 | tf_op jit(solution)/shard_map/ppermute | solution.py:20
  14.1 1.8 %collective-permute-start.3 = (bf16[128,1408]{1,0:T(8,128)(2,1)S(1)}, bf16[128,1408]{1,0:T(8,128)(2,1)S(1)}, u32[]{:S(2)}, u32[]{:S(2)}) collective-permute-start(bf16[128,1408]{1,0:T(8,128)(2,1)S(1)} %join.6.refs_0_), channel_id=1, source_target_pairs={{0,1},{1,0},{2,3},{3,2},{4,5},{5,4},{6,7},{7,6},{8,9},{9,8},{10,11... | collective-permute-start | bytes 1081352 | tf_op jit(solution)/shard_map/ppermute | solution.py:373
  16.7 4.5 %collective-permute-start.4 = (bf16[256,128]{1,0:T(8,128)(2,1)S(1)}, bf16[256,128]{1,0:T(8,128)(2,1)S(1)}, u32[]{:S(2)}, u32[]{:S(2)}) collective-permute-start(bf16[256,128]{1,0:T(8,128)(2,1)S(1)} %get-tuple-element.16.refs_0_.refs_8_), channel_id=1, source_target_pairs={{0,8},{1,9},{2,10},{3,11},{4,12},{5,13},{6,14},{7,15},{8,0},{9,1},... | collective-permute-start | bytes 196616 | tf_op jit(solution)/shard_map/ppermute | solution.py:20
  19.6 1.7 %collective-permute-start.11 = (bf16[96,1280]{1,0:T(8,128)(2,1)S(1)}, bf16[96,1280]{1,0:T(8,128)(2,1)S(1)}, u32[]{:S(2)}, u32[]{:S(2)}) collective-permute-start(bf16[96,1280]{1,0:T(8,128)(2,1)S(1)} %join.11.refs_13_), channel_id=1, source_target_pairs={{0,1},{1,0},{2,3},{3,2},{4,5},{5,4},{6,7},{7,6},{8,9},{9,8},{10,11... | collective-permute-start | bytes 737288 | tf_op jit(solution)/shard_map/ppermute | solution.py:373
  19.8 1.8 %collective-permute-start.8 = (bf16[128,1280]{1,0:T(8,128)(2,1)S(1)}, bf16[128,1280]{1,0:T(8,128)(2,1)S(1)}, u32[]{:S(2)}, u32[]{:S(2)}) collective-permute-start(bf16[128,1280]{1,0:T(8,128)(2,1)S(1)} %join.9.refs_11_), channel_id=1, source_target_pairs={{0,1},{1,0},{2,3},{3,2},{4,5},{5,4},{6,7},{7,6},{8,9},{9,8},{10,11... | collective-permute-start | bytes 983048 | tf_op jit(solution)/shard_map/ppermute | solution.py:373

commit v5 on v4

--- a/solution.py
+++ b/solution.py
@@ -432,7 +432,7 @@
     )(*arrays, edge)
     partner = to_chips(solved[-1], (quad, quad))
 
-    trips = [(join([top], top_pair), (2, 2)), (top_pair, (1, 3)), (top_pair, (4, 5)), (top_pair, (6, 7))]
+    trips = [(join([top], top_pair), (1, 1)), (top_pair, (3, 2)), (top_pair, (4, 5)), (top_pair, (6, 7))]
     far = [(top, 0, (0, 0), 0), (top_other, 0, (0, 0), 1)]
     arrived = [to_chips(block, distances) for block, distances in trips]
     for chosen in ((2, 3), (0, 1)):

time: 24.4 us -> 23.9 us (0.980)
  starting transfers between devices: 13.8 us -> 13.2 us
    ppermute x8, starting transfers between devices: 12.6 us -> 12 us  [to_chips(): return lax.ppermute(block, AXES, route)]
  transfers between devices with their start and end apart: 12 -> 12, of which waited for: 3 -> 3; matrix products, arithmetic and copies ran while one was open for 0% -> 0% of each run, Pallas kernels for 10% -> 11%
where the time goes in v5:
time: 23.9 us; the launch traced here: 23.8 us
  starting transfers between devices  13.2 us (55%)
  Pallas kernels  6.42 us (27%)
  waiting for transfers between devices  2.68 us (11%)
  between operations  1.46 us (6%)
    ppermute x8, starting transfers between devices, to_chips(): return lax.ppermute(block, AXES, route)  12 us
    pallas_call x1, Pallas kernels, on_device(): pl.pallas_call(functools.partial(top_kernel, levels, unit, places), out_s...  2.65 us
    ppermute x8, waiting for transfers between devices, to_chips(): return lax.ppermute(block, AXES, route)  2.22 us
    pallas_call x1, Pallas kernels, on_device(): pl.pallas_call(functools.partial(leaf_kernel, row_count), out_shape=(jax....  1.71 us
    pallas_call x1, Pallas kernels, on_device(): pl.pallas_call(functools.partial(pack_kernel, levels), out_shape=(jax.Sha...  1.22 us
    ppermute x4, starting transfers between devices, swap(): return lax.ppermute(block, 'sec', [(0, 1), (1, 0)])  1.2 us
    pallas_call x1, Pallas kernels, on_device(): pl.pallas_call(functools.partial(low_kernel, levels, unit, places), out_s...  0.75 us
  transfers between devices with their start and end apart: 12, of which 3 were waited for; matrix products, arithmetic and copies ran while one was open for 0% of the time, Pallas kernels for 11%

profile of v5, /device:TPU:0, one launch (start us, length us, event | category | flops | bytes accessed | tf_op | source)
XLA Modules:
  0.0 23.8 jit_solution(218927656174688167)
XLA Ops:
  0.6 0.0 copy-start.4
  1.3 1.2 %pack.1 = (bf16[32,1408]{1,0:T(8,128)(2,1)S(1)}, bf16[32,1280]{1,0:T(8,128)(2,1)S(1)}) custom-call(s32[1,1]{1,0:T(1,128)S(6)} %copy.12.blocks_ref, bf16[1024,1024]{1,0:T(8,128)(2,1)} %leaf_ref.1, bf16[1024,128]{1,0:T(8,128)(2,1)} %shift_ref.1, bf16[32,896]{1,0:T(8,128)(2,1)} %refs_2_.1, bf16[32,896]{1,0:T(8,128)(2,1)} %refs_3_.1, ...), custom_call_target="tpu_custom_call" | custom-call | tf_op jit(solution)/shard_map/pack/pallas_call | solution.py:351
  2.5 0.5 %collective-permute-start.5 = (bf16[32,1280]{1,0:T(8,128)(2,1)S(1)}, bf16[32,1280]{1,0:T(8,128)(2,1)S(1)}, u32[]{:S(2)}, u32[]{:S(2)}) collective-permute-start(bf16[32,1280]{1,0:T(8,128)(2,1)S(1)} %get-tuple-element.21.refs_0_.refs_1_.refs_9_), channel_id=1, source_target_pairs={{0,1},{1,0},{2,3},{3,2},{4,5},{5,4},{6,7},{7,6},{8,9},{9,8},{10,11... | collective-permute-start | bytes 245768 | tf_op jit(solution)/shard_map/ppermute | solution.py:373
  3.0 3.5 %collective-permute-start.2 = (bf16[32,1408]{1,0:T(8,128)(2,1)S(1)}, bf16[32,1408]{1,0:T(8,128)(2,1)S(1)}, u32[]{:S(2)}, u32[]{:S(2)}) collective-permute-start(bf16[32,1408]{1,0:T(8,128)(2,1)S(1)} %get-tuple-element.12.refs_0_), channel_id=1, source_target_pairs={{0,6},{1,7},{2,4},{3,5},{4,2},{5,3},{6,0},{7,1},{8,14},{9,15},{10,... | collective-permute-start | bytes 270344 | tf_op jit(solution)/shard_map/ppermute | solution.py:20
  6.6 0.5 %collective-permute-start.1 = (bf16[32,1408]{1,0:T(8,128)(2,1)S(1)}, bf16[32,1408]{1,0:T(8,128)(2,1)S(1)}, u32[]{:S(2)}, u32[]{:S(2)}) collective-permute-start(bf16[32,1408]{1,0:T(8,128)(2,1)S(1)} %get-tuple-element.12.refs_0_), channel_id=1, source_target_pairs={{0,4},{1,5},{2,6},{3,7},{4,0},{5,1},{6,2},{7,3},{8,12},{9,13},{10,... | collective-permute-start | bytes 270344 | tf_op jit(solution)/shard_map/ppermute | solution.py:20
  7.1 0.1 collective-permute-start
  7.2 0.0 copy-done.4
  7.2 0.0 copy-start
  7.2 0.0 copy-start.1
  7.2 0.0 copy-start.2
  7.2 0.0 copy-start.3
  7.3 0.0 collective-permute-done.5.refs_1_.refs_10_
  7.3 2.9 %collective-permute-start.10 = (bf16[64,1280]{1,0:T(8,128)(2,1)S(1)}, bf16[64,1280]{1,0:T(8,128)(2,1)S(1)}, u32[]{:S(2)}, u32[]{:S(2)}) collective-permute-start(bf16[64,1280]{1,0:T(8,128)(2,1)S(1)} %join.8.refs_0_), channel_id=1, source_target_pairs={{0,6},{1,5},{2,4},{3,7},{4,2},{5,1},{6,0},{7,3},{8,14},{9,13},{10,... | collective-permute-start | bytes 491528 | tf_op jit(solution)/shard_map/ppermute | solution.py:20
  10.2 1.5 %collective-permute-start.7 = (bf16[64,1280]{1,0:T(8,128)(2,1)S(1)}, bf16[64,1280]{1,0:T(8,128)(2,1)S(1)}, u32[]{:S(2)}, u32[]{:S(2)}) collective-permute-start(bf16[64,1280]{1,0:T(8,128)(2,1)S(1)} %join.8.refs_0_), channel_id=1, source_target_pairs={{0,12},{1,15},{2,14},{3,13},{4,8},{5,11},{6,10},{7,9},{8,4},{9,7},... | collective-permute-start | bytes 491528 | tf_op jit(solution)/shard_map/ppermute | solution.py:20
  11.7 0.0 collective-permute-done.2.refs_3_
  11.7 0.4 %collective-permute-start.6 = (bf16[64,1280]{1,0:T(8,128)(2,1)S(1)}, bf16[64,1280]{1,0:T(8,128)(2,1)S(1)}, u32[]{:S(2)}, u32[]{:S(2)}) collective-permute-start(bf16[64,1280]{1,0:T(8,128)(2,1)S(1)} %join.8.refs_0_), channel_id=1, source_target_pairs={{0,8},{1,11},{2,10},{3,9},{4,12},{5,15},{6,14},{7,13},{8,0},{9,3},... | collective-permute-start | bytes 491528 | tf_op jit(solution)/shard_map/ppermute | solution.py:20
  12.2 0.0 collective-permute-done.1.refs_2_
  12.2 1.3 %collective-permute-start.9 = (bf16[32,1280]{1,0:T(8,128)(2,1)S(1)}, bf16[32,1280]{1,0:T(8,128)(2,1)S(1)}, u32[]{:S(2)}, u32[]{:S(2)}) collective-permute-start(bf16[32,1280]{1,0:T(8,128)(2,1)S(1)} %join.10), channel_id=1, source_target_pairs={{0,2},{1,3},{2,0},{3,1},{4,6},{5,7},{6,4},{7,5},{8,10},{9,11},{10,... | collective-permute-start | bytes 245768 | tf_op jit(solution)/shard_map/ppermute | solution.py:20
  13.5 0.0 collective-permute-done.refs_1_
  13.5 0.1 collective-permute-start.3
  13.6 0.0 copy-done
  13.6 0.0 copy-done.1
  13.6 0.0 copy-done.2
  13.6 0.0 copy-done.3
  13.6 1.7 %leaf.1 = (f32[1024,128]{1,0:T(8,128)S(1)}, f32[32,128]{1,0:T(8,128)S(1)}, bf16[1024,32]{1,0:T(8,128)(2,1)S(1)}, f32[1024,128]{1,0:T(8,128)S(1)}, f32[3,32,128]{2,1,0:T(8,128)S(1)}) custom-call(s32[1,1]{1,0:T(1,128)S(6)} %copy.12.blocks_ref, bf16[1024,1024]{1,0:T(8,128)(2,1)S(1)} %copy-done, bf16[1024,128]{1,0:T(8,128)(2,1)S(1)} %copy-done.1, ...), custom_call_target="tpu_custom_call" | custom-call | flops 10000000000 | bytes 1 | tf_op jit(solution)/shard_map/leaf/pallas_call | solution.py:407
  15.4 0.0 collective-permute-done.3.refs_1_
  15.4 0.8 %low.1 = (bf16[256,1408]{1,0:T(8,128)(2,1)S(1)}, bf16[256,128]{1,0:T(8,128)(2,1)S(1)}, bf16[256,128]{1,0:T(8,128)(2,1)S(1)}) custom-call(bf16[128,1408]{1,0:T(8,128)(2,1)S(1)} %join.6.refs_0_, bf16[128,1408]{1,0:T(8,128)(2,1)S(1)} %collective-permute-done.3.refs_1_, f32[32,128]{1,0:T(8,128)S(1)} %get-tuple-element.13.refs_2_.refs_1_), custom_call_target="tpu_custom_call" | custom-call | tf_op jit(solution)/shard_map/low/pallas_call | solution.py:424
  16.1 1.6 %collective-permute-start.4 = (bf16[256,128]{1,0:T(8,128)(2,1)S(1)}, bf16[256,128]{1,0:T(8,128)(2,1)S(1)}, u32[]{:S(2)}, u32[]{:S(2)}) collective-permute-start(bf16[256,128]{1,0:T(8,128)(2,1)S(1)} %get-tuple-element.16.refs_0_.refs_8_), channel_id=1, source_target_pairs={{0,8},{1,9},{2,10},{3,11},{4,12},{5,13},{6,14},{7,15},{8,0},{9,1},... | collective-permute-start | bytes 196616 | tf_op jit(solution)/shard_map/ppermute | solution.py:20
  17.8 1.3 %collective-permute-done.9.refs_1_ = bf16[32,1280]{1,0:T(8,128)(2,1)S(1)} collective-permute-done((bf16[32,1280]{1,0:T(8,128)(2,1)S(1)}, bf16[32,1280]{1,0:T(8,128)(2,1)S(1)}, u32[]{:S(2)}, u32[]{:S(2)}) %collective-permute-start.9) | collective-permute-done | bytes 81952 | tf_op jit(solution)/shard_map/ppermute | solution.py:20
  19.0 0.0 collective-permute-done.10.refs_2_
  19.1 0.1 collective-permute-start.11
  19.1 0.0 collective-permute-done.7.refs_2_
  19.2 0.0 collective-permute-done.6.refs_1_
  19.2 0.5 %collective-permute-start.8 = (bf16[128,1280]{1,0:T(8,128)(2,1)S(1)}, bf16[128,1280]{1,0:T(8,128)(2,1)S(1)}, u32[]{:S(2)}, u32[]{:S(2)}) collective-permute-start(bf16[128,1280]{1,0:T(8,128)(2,1)S(1)} %join.9.refs_11_), channel_id=1, source_target_pairs={{0,1},{1,0},{2,3},{3,2},{4,5},{5,4},{6,7},{7,6},{8,9},{9,8},{10,11... | collective-permute-start | bytes 983048 | tf_op jit(solution)/shard_map/ppermute | solution.py:373
  19.7 0.9 %collective-permute-done.4.refs_0_.refs_2_ = bf16[256,128]{1,0:T(8,128)(2,1)S(1)} collective-permute-done((bf16[256,128]{1,0:T(8,128)(2,1)S(1)}, bf16[256,128]{1,0:T(8,128)(2,1)S(1)}, u32[]{:S(2)}, u32[]{:S(2)}) %collective-permute-start.4) | collective-permute-done | bytes 65568 | tf_op jit(solution)/shard_map/ppermute | solution.py:20
  20.7 0.0 collective-permute-done.11.refs_14_
  20.7 0.4 %collective-permute-done.8.refs_12_ = bf16[128,1280]{1,0:T(8,128)(2,1)S(1)} collective-permute-done((bf16[128,1280]{1,0:T(8,128)(2,1)S(1)}, bf16[128,1280]{1,0:T(8,128)(2,1)S(1)}, u32[]{:S(2)}, u32[]{:S(2)}) %collective-permute-start.8) | collective-permute-done | bytes 327712 | tf_op jit(solution)/shard_map/ppermute | solution.py:373
  21.1 2.7 %top.1 = (bf16[1024,128]{1,0:T(8,128)(2,1)}, bf16[3,32,128]{2,1,0:T(8,128)(2,1)}) custom-call(bf16[256,1408]{1,0:T(8,128)(2,1)S(1)} %get-tuple-element.14.refs_0_, f32[3,32,128]{2,1,0:T(8,128)S(1)} %get-tuple-element.15.refs_1_, bf16[256,128]{1,0:T(8,128)(2,1)S(1)} %collective-permute-done.4.refs_0_.refs_2_, f32[1024,128]{1,0:T(8,128)S(1)} %get-tuple-element.17.refs_3_, ...), custom_call_target="tpu_custom_call" | custom-call | tf_op jit(solution)/shard_map/top/pallas_call | solution.py:451
  (7 shorter events, 0.1 us)
Async XLA Ops:
  0.6 6.6 %copy-start.4 = (bf16[1024]{0:T(1024)(128)(2,1)S(1)}, bf16[1024]{0:T(1024)(128)(2,1)}, u32[]{:S(2)}) copy-start(bf16[1024]{0:T(1024)(128)(2,1)} %param.14) | copy-start | bytes 6148
  2.5 4.7 %collective-permute-start.5 = (bf16[32,1280]{1,0:T(8,128)(2,1)S(1)}, bf16[32,1280]{1,0:T(8,128)(2,1)S(1)}, u32[]{:S(2)}, u32[]{:S(2)}) collective-permute-start(bf16[32,1280]{1,0:T(8,128)(2,1)S(1)} %get-tuple-element.21.refs_0_.refs_1_.refs_9_), channel_id=1, source_target_pairs={{0,1},{1,0},{2,3},{3,2},{4,5},{5,4},{6,7},{7,6},{8,9},{9,8},{10,11... | collective-permute-start | bytes 245768 | tf_op jit(solution)/shard_map/ppermute | solution.py:373
  3.0 8.7 %collective-permute-start.2 = (bf16[32,1408]{1,0:T(8,128)(2,1)S(1)}, bf16[32,1408]{1,0:T(8,128)(2,1)S(1)}, u32[]{:S(2)}, u32[]{:S(2)}) collective-permute-start(bf16[32,1408]{1,0:T(8,128)(2,1)S(1)} %get-tuple-element.12.refs_0_), channel_id=1, source_target_pairs={{0,6},{1,7},{2,4},{3,5},{4,2},{5,3},{6,0},{7,1},{8,14},{9,15},{10,... | collective-permute-start | bytes 270344 | tf_op jit(solution)/shard_map/ppermute | solution.py:20
  6.6 5.6 %collective-permute-start.1 = (bf16[32,1408]{1,0:T(8,128)(2,1)S(1)}, bf16[32,1408]{1,0:T(8,128)(2,1)S(1)}, u32[]{:S(2)}, u32[]{:S(2)}) collective-permute-start(bf16[32,1408]{1,0:T(8,128)(2,1)S(1)} %get-tuple-element.12.refs_0_), channel_id=1, source_target_pairs={{0,4},{1,5},{2,6},{3,7},{4,0},{5,1},{6,2},{7,3},{8,12},{9,13},{10,... | collective-permute-start | bytes 270344 | tf_op jit(solution)/shard_map/ppermute | solution.py:20
  7.1 6.4 %collective-permute-start = (bf16[32,1408]{1,0:T(8,128)(2,1)S(1)}, bf16[32,1408]{1,0:T(8,128)(2,1)S(1)}, u32[]{:S(2)}, u32[]{:S(2)}) collective-permute-start(bf16[32,1408]{1,0:T(8,128)(2,1)S(1)} %get-tuple-element.12.refs_0_), channel_id=1, source_target_pairs={{0,2},{1,3},{2,0},{3,1},{4,6},{5,7},{6,4},{7,5},{8,10},{9,11},{10,... | collective-permute-start | bytes 270344 | tf_op jit(solution)/shard_map/ppermute | solution.py:20
  7.2 6.4 %copy-start = (bf16[1024,1024]{1,0:T(8,128)(2,1)S(1)}, bf16[1024,1024]{1,0:T(8,128)(2,1)}, u32[]{:S(2)}) copy-start(bf16[1024,1024]{1,0:T(8,128)(2,1)} %leaf_ref.1) | copy-start | bytes 6291460
  7.2 6.4 %copy-start.1 = (bf16[1024,128]{1,0:T(8,128)(2,1)S(1)}, bf16[1024,128]{1,0:T(8,128)(2,1)}, u32[]{:S(2)}) copy-start(bf16[1024,128]{1,0:T(8,128)(2,1)} %shift_ref.1) | copy-start | bytes 786436
  7.2 6.4 %copy-start.2 = (bf16[1024,128]{1,0:T(8,128)(2,1)S(1)}, bf16[1024,128]{1,0:T(8,128)(2,1)}, u32[]{:S(2)}) copy-start(bf16[1024,128]{1,0:T(8,128)(2,1)} %noise_ref.1) | copy-start | bytes 786436
  7.2 6.4 %copy-start.3 = (bf16[3,32]{1,0:T(4,128)(2,1)S(1)}, bf16[3,32]{1,0:T(4,128)(2,1)}, u32[]{:S(2)}) copy-start(bf16[3,32]{1,0:T(4,128)(2,1)} %sep_dev_ref.1) | copy-start | bytes 580
  7.3 11.7 %collective-permute-start.10 = (bf16[64,1280]{1,0:T(8,128)(2,1)S(1)}, bf16[64,1280]{1,0:T(8,128)(2,1)S(1)}, u32[]{:S(2)}, u32[]{:S(2)}) collective-permute-start(bf16[64,1280]{1,0:T(8,128)(2,1)S(1)} %join.8.refs_0_), channel_id=1, source_target_pairs={{0,6},{1,5},{2,4},{3,7},{4,2},{5,1},{6,0},{7,3},{8,14},{9,13},{10,... | collective-permute-start | bytes 491528 | tf_op jit(solution)/shard_map/ppermute | solution.py:20
  10.2 8.9 %collective-permute-start.7 = (bf16[64,1280]{1,0:T(8,128)(2,1)S(1)}, bf16[64,1280]{1,0:T(8,128)(2,1)S(1)}, u32[]{:S(2)}, u32[]{:S(2)}) collective-permute-start(bf16[64,1280]{1,0:T(8,128)(2,1)S(1)} %join.8.refs_0_), channel_id=1, source_target_pairs={{0,12},{1,15},{2,14},{3,13},{4,8},{5,11},{6,10},{7,9},{8,4},{9,7},... | collective-permute-start | bytes 491528 | tf_op jit(solution)/shard_map/ppermute | solution.py:20
  11.7 7.4 %collective-permute-start.6 = (bf16[64,1280]{1,0:T(8,128)(2,1)S(1)}, bf16[64,1280]{1,0:T(8,128)(2,1)S(1)}, u32[]{:S(2)}, u32[]{:S(2)}) collective-permute-start(bf16[64,1280]{1,0:T(8,128)(2,1)S(1)} %join.8.refs_0_), channel_id=1, source_target_pairs={{0,8},{1,11},{2,10},{3,9},{4,12},{5,15},{6,14},{7,13},{8,0},{9,3},... | collective-permute-start | bytes 491528 | tf_op jit(solution)/shard_map/ppermute | solution.py:20
  12.2 6.8 %collective-permute-start.9 = (bf16[32,1280]{1,0:T(8,128)(2,1)S(1)}, bf16[32,1280]{1,0:T(8,128)(2,1)S(1)}, u32[]{:S(2)}, u32[]{:S(2)}) collective-permute-start(bf16[32,1280]{1,0:T(8,128)(2,1)S(1)} %join.10), channel_id=1, source_target_pairs={{0,2},{1,3},{2,0},{3,1},{4,6},{5,7},{6,4},{7,5},{8,10},{9,11},{10,... | collective-permute-start | bytes 245768 | tf_op jit(solution)/shard_map/ppermute | solution.py:20
  13.5 1.8 %collective-permute-start.3 = (bf16[128,1408]{1,0:T(8,128)(2,1)S(1)}, bf16[128,1408]{1,0:T(8,128)(2,1)S(1)}, u32[]{:S(2)}, u32[]{:S(2)}) collective-permute-start(bf16[128,1408]{1,0:T(8,128)(2,1)S(1)} %join.6.refs_0_), channel_id=1, source_target_pairs={{0,1},{1,0},{2,3},{3,2},{4,5},{5,4},{6,7},{7,6},{8,9},{9,8},{10,11... | collective-permute-start | bytes 1081352 | tf_op jit(solution)/shard_map/ppermute | solution.py:373
  16.1 4.5 %collective-permute-start.4 = (bf16[256,128]{1,0:T(8,128)(2,1)S(1)}, bf16[256,128]{1,0:T(8,128)(2,1)S(1)}, u32[]{:S(2)}, u32[]{:S(2)}) collective-permute-start(bf16[256,128]{1,0:T(8,128)(2,1)S(1)} %get-tuple-element.16.refs_0_.refs_8_), channel_id=1, source_target_pairs={{0,8},{1,9},{2,10},{3,11},{4,12},{5,13},{6,14},{7,15},{8,0},{9,1},... | collective-permute-start | bytes 196616 | tf_op jit(solution)/shard_map/ppermute | solution.py:20
  19.1 1.6 %collective-permute-start.11 = (bf16[96,1280]{1,0:T(8,128)(2,1)S(1)}, bf16[96,1280]{1,0:T(8,128)(2,1)S(1)}, u32[]{:S(2)}, u32[]{:S(2)}) collective-permute-start(bf16[96,1280]{1,0:T(8,128)(2,1)S(1)} %join.11.refs_13_), channel_id=1, source_target_pairs={{0,1},{1,0},{2,3},{3,2},{4,5},{5,4},{6,7},{7,6},{8,9},{9,8},{10,11... | collective-permute-start | bytes 737288 | tf_op jit(solution)/shard_map/ppermute | solution.py:373
  19.2 1.9 %collective-permute-start.8 = (bf16[128,1280]{1,0:T(8,128)(2,1)S(1)}, bf16[128,1280]{1,0:T(8,128)(2,1)S(1)}, u32[]{:S(2)}, u32[]{:S(2)}) collective-permute-start(bf16[128,1280]{1,0:T(8,128)(2,1)S(1)} %join.9.refs_11_), channel_id=1, source_target_pairs={{0,1},{1,0},{2,3},{3,2},{4,5},{5,4},{6,7},{7,6},{8,9},{9,8},{10,11... | collective-permute-start | bytes 983048 | tf_op jit(solution)/shard_map/ppermute | solution.py:373

commit v6 on v5

--- a/solution.py
+++ b/solution.py
@@ -161,7 +161,18 @@
     child_ref[pl.ds(pl.multiple_of(upper * half, half), half), :] = solved_refs[-1][...]
     child_ref[pl.ds(pl.multiple_of((1 - upper) * half, half), half), :] = partner_ref[...]
     top_span = 2**levels * unit
-    own = solve_forward(whole_ref, slice(0, top_span), 0, top_span, samples, child_ref[...])
+    across = (((1,), (1,)), ((), ()))
+    children = child_ref[...].astype(jnp.float32).T.astype(jnp.bfloat16)
+    rhs = whole_ref[:, 2 * top_span : 2 * top_span + samples].astype(jnp.float32).T
+    reduced = rhs - lax.dot_general(
+        children, whole_ref[:, 0:top_span], across, preferred_element_type=jnp.float32
+    )
+    own = lax.dot_general(
+        reduced.astype(jnp.bfloat16),
+        whole_ref[:, top_span : 2 * top_span],
+        across,
+        preferred_element_type=jnp.float32,
+    ).astype(jnp.bfloat16)
     correction = None
     low_at = low_ref.shape[1]
     for height in range(levels, 0, -1):
@@ -174,7 +185,10 @@
             source, at, rows = low_ref, low_at, pl.ds(pl.multiple_of(first, span), span)
             own = solved_refs[height - 1][rows, :]
         noise = source[rows, at + 2 * span + samples : at + 2 * span + 2 * samples]
-        summed = (own.astype(jnp.float32) + noise.astype(jnp.float32)).T
+        if height == levels:
+            summed = own.astype(jnp.float32) + noise.astype(jnp.float32).T
+        else:
+            summed = (own.astype(jnp.float32) + noise.astype(jnp.float32)).T
         if correction is not None:
             summed = summed - correction
         x = jnp.dot(
@@ -435,7 +449,7 @@
     trips = [(join([top], top_pair), (1, 1)), (top_pair, (3, 2)), (top_pair, (4, 5)), (top_pair, (6, 7))]
     far = [(top, 0, (0, 0), 0), (top_other, 0, (0, 0), 1)]
     arrived = [to_chips(block, distances) for block, distances in trips]
-    for chosen in ((2, 3), (0, 1)):
+    for chosen in ((2, 3, 0), (1,)):
         here = join([arrived[index] for index in chosen], solved[-1])
         there = swap(here)
         row = 0

time: 23.9 us -> 23.6 us (0.987)
  transfers between devices with their start and end apart: 12 -> 12, of which waited for: 3 -> 5; matrix products, arithmetic and copies ran while one was open for 0% -> 0% of each run, Pallas kernels for 11% -> 11%
where the time goes in v6:
time: 23.6 us; the launch traced here: 23.4 us
  starting transfers between devices  13.1 us (56%)
  Pallas kernels  6.23 us (26%)
  waiting for transfers between devices  2.61 us (11%)
  between operations  1.44 us (6%)
    ppermute x8, starting transfers between devices, to_chips(): return lax.ppermute(block, AXES, route)  12 us
    pallas_call x1, Pallas kernels, on_device(): pl.pallas_call(functools.partial(top_kernel, levels, unit, places), out_s...  2.46 us
    ppermute x8, waiting for transfers between devices, to_chips(): return lax.ppermute(block, AXES, route)  2.33 us
    pallas_call x1, Pallas kernels, on_device(): pl.pallas_call(functools.partial(leaf_kernel, row_count), out_shape=(jax....  1.71 us
    pallas_call x1, Pallas kernels, on_device(): pl.pallas_call(functools.partial(pack_kernel, levels), out_shape=(jax.Sha...  1.22 us
    ppermute x4, starting transfers between devices, swap(): return lax.ppermute(block, 'sec', [(0, 1), (1, 0)])  1.12 us
    pallas_call x1, Pallas kernels, on_device(): pl.pallas_call(functools.partial(low_kernel, levels, unit, places), out_s...  0.75 us
  transfers between devices with their start and end apart: 12, of which 5 were waited for; matrix products, arithmetic and copies ran while one was open for 0% of the time, Pallas kernels for 11%

profile of v6, /device:TPU:0, one launch (start us, length us, event | category | flops | bytes accessed | tf_op | source)
XLA Modules:
  0.0 23.4 jit_solution(3816575846674781958)
XLA Ops:
  0.6 0.0 copy-start.4
  1.3 1.2 %pack.1 = (bf16[32,1408]{1,0:T(8,128)(2,1)S(1)}, bf16[32,1280]{1,0:T(8,128)(2,1)S(1)}) custom-call(s32[1,1]{1,0:T(1,128)S(6)} %copy.12.blocks_ref, bf16[1024,1024]{1,0:T(8,128)(2,1)} %leaf_ref.1, bf16[1024,128]{1,0:T(8,128)(2,1)} %shift_ref.1, bf16[32,896]{1,0:T(8,128)(2,1)} %refs_2_.1, bf16[32,896]{1,0:T(8,128)(2,1)} %refs_3_.1, ...), custom_call_target="tpu_custom_call" | custom-call | tf_op jit(solution)/shard_map/pack/pallas_call | solution.py:365
  2.5 0.5 %collective-permute-start.5 = (bf16[32,1280]{1,0:T(8,128)(2,1)S(1)}, bf16[32,1280]{1,0:T(8,128)(2,1)S(1)}, u32[]{:S(2)}, u32[]{:S(2)}) collective-permute-start(bf16[32,1280]{1,0:T(8,128)(2,1)S(1)} %get-tuple-element.21.refs_0_.refs_1_.refs_9_), channel_id=1, source_target_pairs={{0,1},{1,0},{2,3},{3,2},{4,5},{5,4},{6,7},{7,6},{8,9},{9,8},{10,11... | collective-permute-start | bytes 245768 | tf_op jit(solution)/shard_map/ppermute | solution.py:387
  3.0 3.5 %collective-permute-start.2 = (bf16[32,1408]{1,0:T(8,128)(2,1)S(1)}, bf16[32,1408]{1,0:T(8,128)(2,1)S(1)}, u32[]{:S(2)}, u32[]{:S(2)}) collective-permute-start(bf16[32,1408]{1,0:T(8,128)(2,1)S(1)} %get-tuple-element.12.refs_0_), channel_id=1, source_target_pairs={{0,6},{1,7},{2,4},{3,5},{4,2},{5,3},{6,0},{7,1},{8,14},{9,15},{10,... | collective-permute-start | bytes 270344 | tf_op jit(solution)/shard_map/ppermute | solution.py:20
  6.6 0.5 %collective-permute-start.1 = (bf16[32,1408]{1,0:T(8,128)(2,1)S(1)}, bf16[32,1408]{1,0:T(8,128)(2,1)S(1)}, u32[]{:S(2)}, u32[]{:S(2)}) collective-permute-start(bf16[32,1408]{1,0:T(8,128)(2,1)S(1)} %get-tuple-element.12.refs_0_), channel_id=1, source_target_pairs={{0,4},{1,5},{2,6},{3,7},{4,0},{5,1},{6,2},{7,3},{8,12},{9,13},{10,... | collective-permute-start | bytes 270344 | tf_op jit(solution)/shard_map/ppermute | solution.py:20
  7.1 0.1 collective-permute-start
  7.2 0.0 copy-done.4
  7.2 0.0 copy-start
  7.2 0.0 copy-start.1
  7.2 0.0 copy-start.2
  7.2 0.0 copy-start.3
  7.3 0.0 collective-permute-done.5.refs_1_.refs_10_
  7.3 2.9 %collective-permute-start.10 = (bf16[64,1280]{1,0:T(8,128)(2,1)S(1)}, bf16[64,1280]{1,0:T(8,128)(2,1)S(1)}, u32[]{:S(2)}, u32[]{:S(2)}) collective-permute-start(bf16[64,1280]{1,0:T(8,128)(2,1)S(1)} %join.8.refs_0_), channel_id=1, source_target_pairs={{0,6},{1,5},{2,4},{3,7},{4,2},{5,1},{6,0},{7,3},{8,14},{9,13},{10,... | collective-permute-start | bytes 491528 | tf_op jit(solution)/shard_map/ppermute | solution.py:20
  10.2 1.5 %collective-permute-start.7 = (bf16[64,1280]{1,0:T(8,128)(2,1)S(1)}, bf16[64,1280]{1,0:T(8,128)(2,1)S(1)}, u32[]{:S(2)}, u32[]{:S(2)}) collective-permute-start(bf16[64,1280]{1,0:T(8,128)(2,1)S(1)} %join.8.refs_0_), channel_id=1, source_target_pairs={{0,12},{1,15},{2,14},{3,13},{4,8},{5,11},{6,10},{7,9},{8,4},{9,7},... | collective-permute-start | bytes 491528 | tf_op jit(solution)/shard_map/ppermute | solution.py:20
  11.7 0.0 collective-permute-done.2.refs_3_
  11.7 0.4 %collective-permute-start.6 = (bf16[64,1280]{1,0:T(8,128)(2,1)S(1)}, bf16[64,1280]{1,0:T(8,128)(2,1)S(1)}, u32[]{:S(2)}, u32[]{:S(2)}) collective-permute-start(bf16[64,1280]{1,0:T(8,128)(2,1)S(1)} %join.8.refs_0_), channel_id=1, source_target_pairs={{0,8},{1,11},{2,10},{3,9},{4,12},{5,15},{6,14},{7,13},{8,0},{9,3},... | collective-permute-start | bytes 491528 | tf_op jit(solution)/shard_map/ppermute | solution.py:20
  12.2 0.0 collective-permute-done.1.refs_2_
  12.2 1.3 %collective-permute-start.8 = (bf16[32,1280]{1,0:T(8,128)(2,1)S(1)}, bf16[32,1280]{1,0:T(8,128)(2,1)S(1)}, u32[]{:S(2)}, u32[]{:S(2)}) collective-permute-start(bf16[32,1280]{1,0:T(8,128)(2,1)S(1)} %join.9), channel_id=1, source_target_pairs={{0,2},{1,3},{2,0},{3,1},{4,6},{5,7},{6,4},{7,5},{8,10},{9,11},{10,... | collective-permute-start | bytes 245768 | tf_op jit(solution)/shard_map/ppermute | solution.py:20
  13.5 0.0 collective-permute-done.refs_1_
  13.5 0.1 collective-permute-start.3
  13.6 0.0 copy-done
  13.6 0.0 copy-done.1
  13.6 0.0 copy-done.2
  13.6 0.0 copy-done.3
  13.6 1.7 %leaf.1 = (f32[1024,128]{1,0:T(8,128)S(1)}, f32[32,128]{1,0:T(8,128)S(1)}, bf16[1024,32]{1,0:T(8,128)(2,1)S(1)}, f32[1024,128]{1,0:T(8,128)S(1)}, f32[3,32,128]{2,1,0:T(8,128)S(1)}) custom-call(s32[1,1]{1,0:T(1,128)S(6)} %copy.12.blocks_ref, bf16[1024,1024]{1,0:T(8,128)(2,1)S(1)} %copy-done, bf16[1024,128]{1,0:T(8,128)(2,1)S(1)} %copy-done.1, ...), custom_call_target="tpu_custom_call" | custom-call | flops 10000000000 | bytes 1 | tf_op jit(solution)/shard_map/leaf/pallas_call | solution.py:421
  15.4 0.0 collective-permute-done.3.refs_1_
  15.4 0.8 %low.1 = (bf16[256,1408]{1,0:T(8,128)(2,1)S(1)}, bf16[256,128]{1,0:T(8,128)(2,1)S(1)}, bf16[256,128]{1,0:T(8,128)(2,1)S(1)}) custom-call(bf16[128,1408]{1,0:T(8,128)(2,1)S(1)} %join.6.refs_0_, bf16[128,1408]{1,0:T(8,128)(2,1)S(1)} %collective-permute-done.3.refs_1_, f32[32,128]{1,0:T(8,128)S(1)} %get-tuple-element.13.refs_2_.refs_1_), custom_call_target="tpu_custom_call" | custom-call | tf_op jit(solution)/shard_map/low/pallas_call | solution.py:438
  16.1 1.6 %collective-permute-start.4 = (bf16[256,128]{1,0:T(8,128)(2,1)S(1)}, bf16[256,128]{1,0:T(8,128)(2,1)S(1)}, u32[]{:S(2)}, u32[]{:S(2)}) collective-permute-start(bf16[256,128]{1,0:T(8,128)(2,1)S(1)} %get-tuple-element.16.refs_0_.refs_8_), channel_id=1, source_target_pairs={{0,8},{1,9},{2,10},{3,11},{4,12},{5,13},{6,14},{7,15},{8,0},{9,1},... | collective-permute-start | bytes 196616 | tf_op jit(solution)/shard_map/ppermute | solution.py:20
  17.8 0.7 %collective-permute-done.10.refs_1_ = bf16[64,1280]{1,0:T(8,128)(2,1)S(1)} collective-permute-done((bf16[64,1280]{1,0:T(8,128)(2,1)S(1)}, bf16[64,1280]{1,0:T(8,128)(2,1)S(1)}, u32[]{:S(2)}, u32[]{:S(2)}) %collective-permute-start.10) | collective-permute-done | bytes 163872 | tf_op jit(solution)/shard_map/ppermute | solution.py:20
  18.5 0.5 %collective-permute-start.11 = (bf16[64,1280]{1,0:T(8,128)(2,1)S(1)}, bf16[64,1280]{1,0:T(8,128)(2,1)S(1)}, u32[]{:S(2)}, u32[]{:S(2)}) collective-permute-start(bf16[64,1280]{1,0:T(8,128)(2,1)S(1)} %join.11.refs_13_), channel_id=1, source_target_pairs={{0,1},{1,0},{2,3},{3,2},{4,5},{5,4},{6,7},{7,6},{8,9},{9,8},{10,11... | collective-permute-start | bytes 491528 | tf_op jit(solution)/shard_map/ppermute | solution.py:387
  18.9 0.1 collective-permute-done.8.refs_3_
  19.0 0.0 collective-permute-done.7.refs_2_
  19.0 0.1 collective-permute-done.6.refs_1_
  19.1 0.1 collective-permute-start.9
  19.2 1.4 %collective-permute-done.4.refs_0_.refs_2_ = bf16[256,128]{1,0:T(8,128)(2,1)S(1)} collective-permute-done((bf16[256,128]{1,0:T(8,128)(2,1)S(1)}, bf16[256,128]{1,0:T(8,128)(2,1)S(1)}, u32[]{:S(2)}, u32[]{:S(2)}) %collective-permute-start.4) | collective-permute-done | bytes 65568 | tf_op jit(solution)/shard_map/ppermute | solution.py:20
  20.7 0.0 collective-permute-done.11.refs_14_
  20.7 0.3 %collective-permute-done.9.refs_12_ = bf16[160,1280]{1,0:T(8,128)(2,1)S(1)} collective-permute-done((bf16[160,1280]{1,0:T(8,128)(2,1)S(1)}, bf16[160,1280]{1,0:T(8,128)(2,1)S(1)}, u32[]{:S(2)}, u32[]{:S(2)}) %collective-permute-start.9) | collective-permute-done | bytes 409632 | tf_op jit(solution)/shard_map/ppermute | solution.py:387
  20.9 2.5 %top.1 = (bf16[1024,128]{1,0:T(8,128)(2,1)}, bf16[3,32,128]{2,1,0:T(8,128)(2,1)}) custom-call(bf16[256,1408]{1,0:T(8,128)(2,1)S(1)} %get-tuple-element.14.refs_0_, f32[3,32,128]{2,1,0:T(8,128)S(1)} %get-tuple-element.15.refs_1_, bf16[256,128]{1,0:T(8,128)(2,1)S(1)} %collective-permute-done.4.refs_0_.refs_2_, f32[1024,128]{1,0:T(8,128)S(1)} %get-tuple-element.17.refs_3_, ...), custom_call_target="tpu_custom_call" | custom-call | tf_op jit(solution)/shard_map/top/pallas_call | solution.py:465
  (7 shorter events, 0.1 us)
Async XLA Ops:
  0.6 6.6 %copy-start.4 = (bf16[1024]{0:T(1024)(128)(2,1)S(1)}, bf16[1024]{0:T(1024)(128)(2,1)}, u32[]{:S(2)}) copy-start(bf16[1024]{0:T(1024)(128)(2,1)} %param.14) | copy-start | bytes 6148
  2.5 4.7 %collective-permute-start.5 = (bf16[32,1280]{1,0:T(8,128)(2,1)S(1)}, bf16[32,1280]{1,0:T(8,128)(2,1)S(1)}, u32[]{:S(2)}, u32[]{:S(2)}) collective-permute-start(bf16[32,1280]{1,0:T(8,128)(2,1)S(1)} %get-tuple-element.21.refs_0_.refs_1_.refs_9_), channel_id=1, source_target_pairs={{0,1},{1,0},{2,3},{3,2},{4,5},{5,4},{6,7},{7,6},{8,9},{9,8},{10,11... | collective-permute-start | bytes 245768 | tf_op jit(solution)/shard_map/ppermute | solution.py:387
  3.0 8.7 %collective-permute-start.2 = (bf16[32,1408]{1,0:T(8,128)(2,1)S(1)}, bf16[32,1408]{1,0:T(8,128)(2,1)S(1)}, u32[]{:S(2)}, u32[]{:S(2)}) collective-permute-start(bf16[32,1408]{1,0:T(8,128)(2,1)S(1)} %get-tuple-element.12.refs_0_), channel_id=1, source_target_pairs={{0,6},{1,7},{2,4},{3,5},{4,2},{5,3},{6,0},{7,1},{8,14},{9,15},{10,... | collective-permute-start | bytes 270344 | tf_op jit(solution)/shard_map/ppermute | solution.py:20
  6.6 5.6 %collective-permute-start.1 = (bf16[32,1408]{1,0:T(8,128)(2,1)S(1)}, bf16[32,1408]{1,0:T(8,128)(2,1)S(1)}, u32[]{:S(2)}, u32[]{:S(2)}) collective-permute-start(bf16[32,1408]{1,0:T(8,128)(2,1)S(1)} %get-tuple-element.12.refs_0_), channel_id=1, source_target_pairs={{0,4},{1,5},{2,6},{3,7},{4,0},{5,1},{6,2},{7,3},{8,12},{9,13},{10,... | collective-permute-start | bytes 270344 | tf_op jit(solution)/shard_map/ppermute | solution.py:20
  7.1 6.4 %collective-permute-start = (bf16[32,1408]{1,0:T(8,128)(2,1)S(1)}, bf16[32,1408]{1,0:T(8,128)(2,1)S(1)}, u32[]{:S(2)}, u32[]{:S(2)}) collective-permute-start(bf16[32,1408]{1,0:T(8,128)(2,1)S(1)} %get-tuple-element.12.refs_0_), channel_id=1, source_target_pairs={{0,2},{1,3},{2,0},{3,1},{4,6},{5,7},{6,4},{7,5},{8,10},{9,11},{10,... | collective-permute-start | bytes 270344 | tf_op jit(solution)/shard_map/ppermute | solution.py:20
  7.2 6.4 %copy-start = (bf16[1024,1024]{1,0:T(8,128)(2,1)S(1)}, bf16[1024,1024]{1,0:T(8,128)(2,1)}, u32[]{:S(2)}) copy-start(bf16[1024,1024]{1,0:T(8,128)(2,1)} %leaf_ref.1) | copy-start | bytes 6291460
  7.2 6.4 %copy-start.1 = (bf16[1024,128]{1,0:T(8,128)(2,1)S(1)}, bf16[1024,128]{1,0:T(8,128)(2,1)}, u32[]{:S(2)}) copy-start(bf16[1024,128]{1,0:T(8,128)(2,1)} %shift_ref.1) | copy-start | bytes 786436
  7.2 6.4 %copy-start.2 = (bf16[1024,128]{1,0:T(8,128)(2,1)S(1)}, bf16[1024,128]{1,0:T(8,128)(2,1)}, u32[]{:S(2)}) copy-start(bf16[1024,128]{1,0:T(8,128)(2,1)} %noise_ref.1) | copy-start | bytes 786436
  7.2 6.4 %copy-start.3 = (bf16[3,32]{1,0:T(4,128)(2,1)S(1)}, bf16[3,32]{1,0:T(4,128)(2,1)}, u32[]{:S(2)}) copy-start(bf16[3,32]{1,0:T(4,128)(2,1)} %sep_dev_ref.1) | copy-start | bytes 580
  7.3 11.1 %collective-permute-start.10 = (bf16[64,1280]{1,0:T(8,128)(2,1)S(1)}, bf16[64,1280]{1,0:T(8,128)(2,1)S(1)}, u32[]{:S(2)}, u32[]{:S(2)}) collective-permute-start(bf16[64,1280]{1,0:T(8,128)(2,1)S(1)} %join.8.refs_0_), channel_id=1, source_target_pairs={{0,6},{1,5},{2,4},{3,7},{4,2},{5,1},{6,0},{7,3},{8,14},{9,13},{10,... | collective-permute-start | bytes 491528 | tf_op jit(solution)/shard_map/ppermute | solution.py:20
  10.2 8.8 %collective-permute-start.7 = (bf16[64,1280]{1,0:T(8,128)(2,1)S(1)}, bf16[64,1280]{1,0:T(8,128)(2,1)S(1)}, u32[]{:S(2)}, u32[]{:S(2)}) collective-permute-start(bf16[64,1280]{1,0:T(8,128)(2,1)S(1)} %join.8.refs_0_), channel_id=1, source_target_pairs={{0,12},{1,15},{2,14},{3,13},{4,8},{5,11},{6,10},{7,9},{8,4},{9,7},... | collective-permute-start | bytes 491528 | tf_op jit(solution)/shard_map/ppermute | solution.py:20
  11.7 7.4 %collective-permute-start.6 = (bf16[64,1280]{1,0:T(8,128)(2,1)S(1)}, bf16[64,1280]{1,0:T(8,128)(2,1)S(1)}, u32[]{:S(2)}, u32[]{:S(2)}) collective-permute-start(bf16[64,1280]{1,0:T(8,128)(2,1)S(1)} %join.8.refs_0_), channel_id=1, source_target_pairs={{0,8},{1,11},{2,10},{3,9},{4,12},{5,15},{6,14},{7,13},{8,0},{9,3},... | collective-permute-start | bytes 491528 | tf_op jit(solution)/shard_map/ppermute | solution.py:20
  12.2 6.8 %collective-permute-start.8 = (bf16[32,1280]{1,0:T(8,128)(2,1)S(1)}, bf16[32,1280]{1,0:T(8,128)(2,1)S(1)}, u32[]{:S(2)}, u32[]{:S(2)}) collective-permute-start(bf16[32,1280]{1,0:T(8,128)(2,1)S(1)} %join.9), channel_id=1, source_target_pairs={{0,2},{1,3},{2,0},{3,1},{4,6},{5,7},{6,4},{7,5},{8,10},{9,11},{10,... | collective-permute-start | bytes 245768 | tf_op jit(solution)/shard_map/ppermute | solution.py:20
  13.5 1.8 %collective-permute-start.3 = (bf16[128,1408]{1,0:T(8,128)(2,1)S(1)}, bf16[128,1408]{1,0:T(8,128)(2,1)S(1)}, u32[]{:S(2)}, u32[]{:S(2)}) collective-permute-start(bf16[128,1408]{1,0:T(8,128)(2,1)S(1)} %join.6.refs_0_), channel_id=1, source_target_pairs={{0,1},{1,0},{2,3},{3,2},{4,5},{5,4},{6,7},{7,6},{8,9},{9,8},{10,11... | collective-permute-start | bytes 1081352 | tf_op jit(solution)/shard_map/ppermute | solution.py:387
  16.1 4.5 %collective-permute-start.4 = (bf16[256,128]{1,0:T(8,128)(2,1)S(1)}, bf16[256,128]{1,0:T(8,128)(2,1)S(1)}, u32[]{:S(2)}, u32[]{:S(2)}) collective-permute-start(bf16[256,128]{1,0:T(8,128)(2,1)S(1)} %get-tuple-element.16.refs_0_.refs_8_), channel_id=1, source_target_pairs={{0,8},{1,9},{2,10},{3,11},{4,12},{5,13},{6,14},{7,15},{8,0},{9,1},... | collective-permute-start | bytes 196616 | tf_op jit(solution)/shard_map/ppermute | solution.py:20
  18.5 2.2 %collective-permute-start.11 = (bf16[64,1280]{1,0:T(8,128)(2,1)S(1)}, bf16[64,1280]{1,0:T(8,128)(2,1)S(1)}, u32[]{:S(2)}, u32[]{:S(2)}) collective-permute-start(bf16[64,1280]{1,0:T(8,128)(2,1)S(1)} %join.11.refs_13_), channel_id=1, source_target_pairs={{0,1},{1,0},{2,3},{3,2},{4,5},{5,4},{6,7},{7,6},{8,9},{9,8},{10,11... | collective-permute-start | bytes 491528 | tf_op jit(solution)/shard_map/ppermute | solution.py:387
  19.1 1.8 %collective-permute-start.9 = (bf16[160,1280]{1,0:T(8,128)(2,1)S(1)}, bf16[160,1280]{1,0:T(8,128)(2,1)S(1)}, u32[]{:S(2)}, u32[]{:S(2)}) collective-permute-start(bf16[160,1280]{1,0:T(8,128)(2,1)S(1)} %join.10.refs_11_), channel_id=1, source_target_pairs={{0,1},{1,0},{2,3},{3,2},{4,5},{5,4},{6,7},{7,6},{8,9},{9,8},{10,11... | collective-permute-start | bytes 1228808 | tf_op jit(solution)/shard_map/ppermute | solution.py:387

commit v7 on v6

--- a/solution.py
+++ b/solution.py
@@ -138,12 +138,14 @@
     product = jnp.dot(weight.T.astype(jnp.bfloat16), leaf_ref[...], preferred_element_type=jnp.float32)
     base_ref[...] = product.T
     inner_ref[...] = leaf_ref[inner:, :].astype(jnp.float32).T.astype(jnp.bfloat16)
+    deviations = dev_ref[...].astype(jnp.float32)
+    sep_deviations = sep_dev_ref[...].astype(jnp.float32)
     for block in range(rows // BLOCK):
         part = slice(block * BLOCK, (block + 1) * BLOCK)
-        column = column_of(dev_ref[:, part].astype(jnp.float32))
+        column = column_of(deviations[:, part])
         scale_ref[part, :] = jnp.where(live[part, :], jnp.broadcast_to(column, (BLOCK, samples)), zero)
     for height in range(sep_scale_ref.shape[0]):
-        column = column_of(sep_dev_ref[height : height + 1, :].astype(jnp.float32))
+        column = column_of(sep_deviations[height : height + 1, :])
         sep_scale_ref[height] = jnp.broadcast_to(column, (row_count, samples))
 
 

time: 23.6 us -> 23.6 us (level)
  no operation moved by 1% of the time
where the time goes in v7:
time: 23.6 us; the launch traced here: 23.4 us
  starting transfers between devices  13.1 us (56%)
  Pallas kernels  6.23 us (26%)
  waiting for transfers between devices  2.61 us (11%)
  between operations  1.44 us (6%)
    ppermute x8, starting transfers between devices, to_chips(): return lax.ppermute(block, AXES, route)  12 us
    pallas_call x1, Pallas kernels, on_device(): pl.pallas_call(functools.partial(top_kernel, levels, unit, places), out_s...  2.46 us
    ppermute x8, waiting for transfers between devices, to_chips(): return lax.ppermute(block, AXES, route)  2.33 us
    pallas_call x1, Pallas kernels, on_device(): pl.pallas_call(functools.partial(leaf_kernel, row_count), out_shape=(jax....  1.71 us
    pallas_call x1, Pallas kernels, on_device(): pl.pallas_call(functools.partial(pack_kernel, levels), out_shape=(jax.Sha...  1.22 us
    ppermute x4, starting transfers between devices, swap(): return lax.ppermute(block, 'sec', [(0, 1), (1, 0)])  1.12 us
    pallas_call x1, Pallas kernels, on_device(): pl.pallas_call(functools.partial(low_kernel, levels, unit, places), out_s...  0.75 us
  transfers between devices with their start and end apart: 12, of which 5 were waited for; matrix products, arithmetic and copies ran while one was open for 0% of the time, Pallas kernels for 11%

profile of v7, /device:TPU:0, one launch (start us, length us, event | category | flops | bytes accessed | tf_op | source)
XLA Modules:
  0.0 23.4 jit_solution(7126554792180102435)
XLA Ops:
  0.6 0.0 copy-start.4
  1.3 1.2 %pack.1 = (bf16[32,1408]{1,0:T(8,128)(2,1)S(1)}, bf16[32,1280]{1,0:T(8,128)(2,1)S(1)}) custom-call(s32[1,1]{1,0:T(1,128)S(6)} %copy.12.blocks_ref, bf16[1024,1024]{1,0:T(8,128)(2,1)} %leaf_ref.1, bf16[1024,128]{1,0:T(8,128)(2,1)} %shift_ref.1, bf16[32,896]{1,0:T(8,128)(2,1)} %refs_2_.1, bf16[32,896]{1,0:T(8,128)(2,1)} %refs_3_.1, ...), custom_call_target="tpu_custom_call" | custom-call | tf_op jit(solution)/shard_map/pack/pallas_call | solution.py:367
  2.5 0.5 %collective-permute-start.5 = (bf16[32,1280]{1,0:T(8,128)(2,1)S(1)}, bf16[32,1280]{1,0:T(8,128)(2,1)S(1)}, u32[]{:S(2)}, u32[]{:S(2)}) collective-permute-start(bf16[32,1280]{1,0:T(8,128)(2,1)S(1)} %get-tuple-element.21.refs_0_.refs_1_.refs_9_), channel_id=1, source_target_pairs={{0,1},{1,0},{2,3},{3,2},{4,5},{5,4},{6,7},{7,6},{8,9},{9,8},{10,11... | collective-permute-start | bytes 245768 | tf_op jit(solution)/shard_map/ppermute | solution.py:389
  3.0 3.5 %collective-permute-start.2 = (bf16[32,1408]{1,0:T(8,128)(2,1)S(1)}, bf16[32,1408]{1,0:T(8,128)(2,1)S(1)}, u32[]{:S(2)}, u32[]{:S(2)}) collective-permute-start(bf16[32,1408]{1,0:T(8,128)(2,1)S(1)} %get-tuple-element.12.refs_0_), channel_id=1, source_target_pairs={{0,6},{1,7},{2,4},{3,5},{4,2},{5,3},{6,0},{7,1},{8,14},{9,15},{10,... | collective-permute-start | bytes 270344 | tf_op jit(solution)/shard_map/ppermute | solution.py:20
  6.6 0.5 %collective-permute-start.1 = (bf16[32,1408]{1,0:T(8,128)(2,1)S(1)}, bf16[32,1408]{1,0:T(8,128)(2,1)S(1)}, u32[]{:S(2)}, u32[]{:S(2)}) collective-permute-start(bf16[32,1408]{1,0:T(8,128)(2,1)S(1)} %get-tuple-element.12.refs_0_), channel_id=1, source_target_pairs={{0,4},{1,5},{2,6},{3,7},{4,0},{5,1},{6,2},{7,3},{8,12},{9,13},{10,... | collective-permute-start | bytes 270344 | tf_op jit(solution)/shard_map/ppermute | solution.py:20
  7.1 0.1 collective-permute-start
  7.2 0.0 copy-done.4
  7.2 0.0 copy-start
  7.2 0.0 copy-start.1
  7.2 0.0 copy-start.2
  7.2 0.0 copy-start.3
  7.3 0.0 collective-permute-done.5.refs_1_.refs_10_
  7.3 2.9 %collective-permute-start.10 = (bf16[64,1280]{1,0:T(8,128)(2,1)S(1)}, bf16[64,1280]{1,0:T(8,128)(2,1)S(1)}, u32[]{:S(2)}, u32[]{:S(2)}) collective-permute-start(bf16[64,1280]{1,0:T(8,128)(2,1)S(1)} %join.8.refs_0_), channel_id=1, source_target_pairs={{0,6},{1,5},{2,4},{3,7},{4,2},{5,1},{6,0},{7,3},{8,14},{9,13},{10,... | collective-permute-start | bytes 491528 | tf_op jit(solution)/shard_map/ppermute | solution.py:20
  10.2 1.5 %collective-permute-start.7 = (bf16[64,1280]{1,0:T(8,128)(2,1)S(1)}, bf16[64,1280]{1,0:T(8,128)(2,1)S(1)}, u32[]{:S(2)}, u32[]{:S(2)}) collective-permute-start(bf16[64,1280]{1,0:T(8,128)(2,1)S(1)} %join.8.refs_0_), channel_id=1, source_target_pairs={{0,12},{1,15},{2,14},{3,13},{4,8},{5,11},{6,10},{7,9},{8,4},{9,7},... | collective-permute-start | bytes 491528 | tf_op jit(solution)/shard_map/ppermute | solution.py:20
  11.7 0.0 collective-permute-done.2.refs_3_
  11.7 0.4 %collective-permute-start.6 = (bf16[64,1280]{1,0:T(8,128)(2,1)S(1)}, bf16[64,1280]{1,0:T(8,128)(2,1)S(1)}, u32[]{:S(2)}, u32[]{:S(2)}) collective-permute-start(bf16[64,1280]{1,0:T(8,128)(2,1)S(1)} %join.8.refs_0_), channel_id=1, source_target_pairs={{0,8},{1,11},{2,10},{3,9},{4,12},{5,15},{6,14},{7,13},{8,0},{9,3},... | collective-permute-start | bytes 491528 | tf_op jit(solution)/shard_map/ppermute | solution.py:20
  12.2 0.0 collective-permute-done.1.refs_2_
  12.2 1.3 %collective-permute-start.8 = (bf16[32,1280]{1,0:T(8,128)(2,1)S(1)}, bf16[32,1280]{1,0:T(8,128)(2,1)S(1)}, u32[]{:S(2)}, u32[]{:S(2)}) collective-permute-start(bf16[32,1280]{1,0:T(8,128)(2,1)S(1)} %join.9), channel_id=1, source_target_pairs={{0,2},{1,3},{2,0},{3,1},{4,6},{5,7},{6,4},{7,5},{8,10},{9,11},{10,... | collective-permute-start | bytes 245768 | tf_op jit(solution)/shard_map/ppermute | solution.py:20
  13.5 0.0 collective-permute-done.refs_1_
  13.5 0.1 collective-permute-start.3
  13.6 0.0 copy-done
  13.6 0.0 copy-done.1
  13.6 0.0 copy-done.2
  13.6 0.0 copy-done.3
  13.6 1.7 %leaf.1 = (f32[1024,128]{1,0:T(8,128)S(1)}, f32[32,128]{1,0:T(8,128)S(1)}, bf16[1024,32]{1,0:T(8,128)(2,1)S(1)}, f32[1024,128]{1,0:T(8,128)S(1)}, f32[3,32,128]{2,1,0:T(8,128)S(1)}) custom-call(s32[1,1]{1,0:T(1,128)S(6)} %copy.12.blocks_ref, bf16[1024,1024]{1,0:T(8,128)(2,1)S(1)} %copy-done, bf16[1024,128]{1,0:T(8,128)(2,1)S(1)} %copy-done.1, ...), custom_call_target="tpu_custom_call" | custom-call | flops 10000000000 | bytes 1 | tf_op jit(solution)/shard_map/leaf/pallas_call | solution.py:423
  15.4 0.0 collective-permute-done.3.refs_1_
  15.4 0.8 %low.1 = (bf16[256,1408]{1,0:T(8,128)(2,1)S(1)}, bf16[256,128]{1,0:T(8,128)(2,1)S(1)}, bf16[256,128]{1,0:T(8,128)(2,1)S(1)}) custom-call(bf16[128,1408]{1,0:T(8,128)(2,1)S(1)} %join.6.refs_0_, bf16[128,1408]{1,0:T(8,128)(2,1)S(1)} %collective-permute-done.3.refs_1_, f32[32,128]{1,0:T(8,128)S(1)} %get-tuple-element.13.refs_2_.refs_1_), custom_call_target="tpu_custom_call" | custom-call | tf_op jit(solution)/shard_map/low/pallas_call | solution.py:440
  16.1 1.6 %collective-permute-start.4 = (bf16[256,128]{1,0:T(8,128)(2,1)S(1)}, bf16[256,128]{1,0:T(8,128)(2,1)S(1)}, u32[]{:S(2)}, u32[]{:S(2)}) collective-permute-start(bf16[256,128]{1,0:T(8,128)(2,1)S(1)} %get-tuple-element.16.refs_0_.refs_8_), channel_id=1, source_target_pairs={{0,8},{1,9},{2,10},{3,11},{4,12},{5,13},{6,14},{7,15},{8,0},{9,1},... | collective-permute-start | bytes 196616 | tf_op jit(solution)/shard_map/ppermute | solution.py:20
  17.8 0.7 %collective-permute-done.10.refs_1_ = bf16[64,1280]{1,0:T(8,128)(2,1)S(1)} collective-permute-done((bf16[64,1280]{1,0:T(8,128)(2,1)S(1)}, bf16[64,1280]{1,0:T(8,128)(2,1)S(1)}, u32[]{:S(2)}, u32[]{:S(2)}) %collective-permute-start.10) | collective-permute-done | bytes 163872 | tf_op jit(solution)/shard_map/ppermute | solution.py:20
  18.5 0.5 %collective-permute-start.11 = (bf16[64,1280]{1,0:T(8,128)(2,1)S(1)}, bf16[64,1280]{1,0:T(8,128)(2,1)S(1)}, u32[]{:S(2)}, u32[]{:S(2)}) collective-permute-start(bf16[64,1280]{1,0:T(8,128)(2,1)S(1)} %join.11.refs_13_), channel_id=1, source_target_pairs={{0,1},{1,0},{2,3},{3,2},{4,5},{5,4},{6,7},{7,6},{8,9},{9,8},{10,11... | collective-permute-start | bytes 491528 | tf_op jit(solution)/shard_map/ppermute | solution.py:389
  18.9 0.1 collective-permute-done.8.refs_3_
  19.0 0.0 collective-permute-done.7.refs_2_
  19.0 0.1 collective-permute-done.6.refs_1_
  19.1 0.1 collective-permute-start.9
  19.2 1.4 %collective-permute-done.4.refs_0_.refs_2_ = bf16[256,128]{1,0:T(8,128)(2,1)S(1)} collective-permute-done((bf16[256,128]{1,0:T(8,128)(2,1)S(1)}, bf16[256,128]{1,0:T(8,128)(2,1)S(1)}, u32[]{:S(2)}, u32[]{:S(2)}) %collective-permute-start.4) | collective-permute-done | bytes 65568 | tf_op jit(solution)/shard_map/ppermute | solution.py:20
  20.7 0.0 collective-permute-done.11.refs_14_
  20.7 0.3 %collective-permute-done.9.refs_12_ = bf16[160,1280]{1,0:T(8,128)(2,1)S(1)} collective-permute-done((bf16[160,1280]{1,0:T(8,128)(2,1)S(1)}, bf16[160,1280]{1,0:T(8,128)(2,1)S(1)}, u32[]{:S(2)}, u32[]{:S(2)}) %collective-permute-start.9) | collective-permute-done | bytes 409632 | tf_op jit(solution)/shard_map/ppermute | solution.py:389
  20.9 2.5 %top.1 = (bf16[1024,128]{1,0:T(8,128)(2,1)}, bf16[3,32,128]{2,1,0:T(8,128)(2,1)}) custom-call(bf16[256,1408]{1,0:T(8,128)(2,1)S(1)} %get-tuple-element.14.refs_0_, f32[3,32,128]{2,1,0:T(8,128)S(1)} %get-tuple-element.15.refs_1_, bf16[256,128]{1,0:T(8,128)(2,1)S(1)} %collective-permute-done.4.refs_0_.refs_2_, f32[1024,128]{1,0:T(8,128)S(1)} %get-tuple-element.17.refs_3_, ...), custom_call_target="tpu_custom_call" | custom-call | tf_op jit(solution)/shard_map/top/pallas_call | solution.py:467
  (7 shorter events, 0.1 us)
Async XLA Ops:
  0.6 6.6 %copy-start.4 = (bf16[1024]{0:T(1024)(128)(2,1)S(1)}, bf16[1024]{0:T(1024)(128)(2,1)}, u32[]{:S(2)}) copy-start(bf16[1024]{0:T(1024)(128)(2,1)} %param.14) | copy-start | bytes 6148
  2.5 4.7 %collective-permute-start.5 = (bf16[32,1280]{1,0:T(8,128)(2,1)S(1)}, bf16[32,1280]{1,0:T(8,128)(2,1)S(1)}, u32[]{:S(2)}, u32[]{:S(2)}) collective-permute-start(bf16[32,1280]{1,0:T(8,128)(2,1)S(1)} %get-tuple-element.21.refs_0_.refs_1_.refs_9_), channel_id=1, source_target_pairs={{0,1},{1,0},{2,3},{3,2},{4,5},{5,4},{6,7},{7,6},{8,9},{9,8},{10,11... | collective-permute-start | bytes 245768 | tf_op jit(solution)/shard_map/ppermute | solution.py:389
  3.0 8.7 %collective-permute-start.2 = (bf16[32,1408]{1,0:T(8,128)(2,1)S(1)}, bf16[32,1408]{1,0:T(8,128)(2,1)S(1)}, u32[]{:S(2)}, u32[]{:S(2)}) collective-permute-start(bf16[32,1408]{1,0:T(8,128)(2,1)S(1)} %get-tuple-element.12.refs_0_), channel_id=1, source_target_pairs={{0,6},{1,7},{2,4},{3,5},{4,2},{5,3},{6,0},{7,1},{8,14},{9,15},{10,... | collective-permute-start | bytes 270344 | tf_op jit(solution)/shard_map/ppermute | solution.py:20
  6.6 5.6 %collective-permute-start.1 = (bf16[32,1408]{1,0:T(8,128)(2,1)S(1)}, bf16[32,1408]{1,0:T(8,128)(2,1)S(1)}, u32[]{:S(2)}, u32[]{:S(2)}) collective-permute-start(bf16[32,1408]{1,0:T(8,128)(2,1)S(1)} %get-tuple-element.12.refs_0_), channel_id=1, source_target_pairs={{0,4},{1,5},{2,6},{3,7},{4,0},{5,1},{6,2},{7,3},{8,12},{9,13},{10,... | collective-permute-start | bytes 270344 | tf_op jit(solution)/shard_map/ppermute | solution.py:20
  7.1 6.4 %collective-permute-start = (bf16[32,1408]{1,0:T(8,128)(2,1)S(1)}, bf16[32,1408]{1,0:T(8,128)(2,1)S(1)}, u32[]{:S(2)}, u32[]{:S(2)}) collective-permute-start(bf16[32,1408]{1,0:T(8,128)(2,1)S(1)} %get-tuple-element.12.refs_0_), channel_id=1, source_target_pairs={{0,2},{1,3},{2,0},{3,1},{4,6},{5,7},{6,4},{7,5},{8,10},{9,11},{10,... | collective-permute-start | bytes 270344 | tf_op jit(solution)/shard_map/ppermute | solution.py:20
  7.2 6.4 %copy-start = (bf16[1024,1024]{1,0:T(8,128)(2,1)S(1)}, bf16[1024,1024]{1,0:T(8,128)(2,1)}, u32[]{:S(2)}) copy-start(bf16[1024,1024]{1,0:T(8,128)(2,1)} %leaf_ref.1) | copy-start | bytes 6291460
  7.2 6.4 %copy-start.1 = (bf16[1024,128]{1,0:T(8,128)(2,1)S(1)}, bf16[1024,128]{1,0:T(8,128)(2,1)}, u32[]{:S(2)}) copy-start(bf16[1024,128]{1,0:T(8,128)(2,1)} %shift_ref.1) | copy-start | bytes 786436
  7.2 6.4 %copy-start.2 = (bf16[1024,128]{1,0:T(8,128)(2,1)S(1)}, bf16[1024,128]{1,0:T(8,128)(2,1)}, u32[]{:S(2)}) copy-start(bf16[1024,128]{1,0:T(8,128)(2,1)} %noise_ref.1) | copy-start | bytes 786436
  7.2 6.4 %copy-start.3 = (bf16[3,32]{1,0:T(4,128)(2,1)S(1)}, bf16[3,32]{1,0:T(4,128)(2,1)}, u32[]{:S(2)}) copy-start(bf16[3,32]{1,0:T(4,128)(2,1)} %sep_dev_ref.1) | copy-start | bytes 580
  7.3 11.1 %collective-permute-start.10 = (bf16[64,1280]{1,0:T(8,128)(2,1)S(1)}, bf16[64,1280]{1,0:T(8,128)(2,1)S(1)}, u32[]{:S(2)}, u32[]{:S(2)}) collective-permute-start(bf16[64,1280]{1,0:T(8,128)(2,1)S(1)} %join.8.refs_0_), channel_id=1, source_target_pairs={{0,6},{1,5},{2,4},{3,7},{4,2},{5,1},{6,0},{7,3},{8,14},{9,13},{10,... | collective-permute-start | bytes 491528 | tf_op jit(solution)/shard_map/ppermute | solution.py:20
  10.2 8.8 %collective-permute-start.7 = (bf16[64,1280]{1,0:T(8,128)(2,1)S(1)}, bf16[64,1280]{1,0:T(8,128)(2,1)S(1)}, u32[]{:S(2)}, u32[]{:S(2)}) collective-permute-start(bf16[64,1280]{1,0:T(8,128)(2,1)S(1)} %join.8.refs_0_), channel_id=1, source_target_pairs={{0,12},{1,15},{2,14},{3,13},{4,8},{5,11},{6,10},{7,9},{8,4},{9,7},... | collective-permute-start | bytes 491528 | tf_op jit(solution)/shard_map/ppermute | solution.py:20
  11.7 7.4 %collective-permute-start.6 = (bf16[64,1280]{1,0:T(8,128)(2,1)S(1)}, bf16[64,1280]{1,0:T(8,128)(2,1)S(1)}, u32[]{:S(2)}, u32[]{:S(2)}) collective-permute-start(bf16[64,1280]{1,0:T(8,128)(2,1)S(1)} %join.8.refs_0_), channel_id=1, source_target_pairs={{0,8},{1,11},{2,10},{3,9},{4,12},{5,15},{6,14},{7,13},{8,0},{9,3},... | collective-permute-start | bytes 491528 | tf_op jit(solution)/shard_map/ppermute | solution.py:20
  12.2 6.8 %collective-permute-start.8 = (bf16[32,1280]{1,0:T(8,128)(2,1)S(1)}, bf16[32,1280]{1,0:T(8,128)(2,1)S(1)}, u32[]{:S(2)}, u32[]{:S(2)}) collective-permute-start(bf16[32,1280]{1,0:T(8,128)(2,1)S(1)} %join.9), channel_id=1, source_target_pairs={{0,2},{1,3},{2,0},{3,1},{4,6},{5,7},{6,4},{7,5},{8,10},{9,11},{10,... | collective-permute-start | bytes 245768 | tf_op jit(solution)/shard_map/ppermute | solution.py:20
  13.5 1.8 %collective-permute-start.3 = (bf16[128,1408]{1,0:T(8,128)(2,1)S(1)}, bf16[128,1408]{1,0:T(8,128)(2,1)S(1)}, u32[]{:S(2)}, u32[]{:S(2)}) collective-permute-start(bf16[128,1408]{1,0:T(8,128)(2,1)S(1)} %join.6.refs_0_), channel_id=1, source_target_pairs={{0,1},{1,0},{2,3},{3,2},{4,5},{5,4},{6,7},{7,6},{8,9},{9,8},{10,11... | collective-permute-start | bytes 1081352 | tf_op jit(solution)/shard_map/ppermute | solution.py:389
  16.1 4.5 %collective-permute-start.4 = (bf16[256,128]{1,0:T(8,128)(2,1)S(1)}, bf16[256,128]{1,0:T(8,128)(2,1)S(1)}, u32[]{:S(2)}, u32[]{:S(2)}) collective-permute-start(bf16[256,128]{1,0:T(8,128)(2,1)S(1)} %get-tuple-element.16.refs_0_.refs_8_), channel_id=1, source_target_pairs={{0,8},{1,9},{2,10},{3,11},{4,12},{5,13},{6,14},{7,15},{8,0},{9,1},... | collective-permute-start | bytes 196616 | tf_op jit(solution)/shard_map/ppermute | solution.py:20
  18.5 2.2 %collective-permute-start.11 = (bf16[64,1280]{1,0:T(8,128)(2,1)S(1)}, bf16[64,1280]{1,0:T(8,128)(2,1)S(1)}, u32[]{:S(2)}, u32[]{:S(2)}) collective-permute-start(bf16[64,1280]{1,0:T(8,128)(2,1)S(1)} %join.11.refs_13_), channel_id=1, source_target_pairs={{0,1},{1,0},{2,3},{3,2},{4,5},{5,4},{6,7},{7,6},{8,9},{9,8},{10,11... | collective-permute-start | bytes 491528 | tf_op jit(solution)/shard_map/ppermute | solution.py:389
  19.1 1.8 %collective-permute-start.9 = (bf16[160,1280]{1,0:T(8,128)(2,1)S(1)}, bf16[160,1280]{1,0:T(8,128)(2,1)S(1)}, u32[]{:S(2)}, u32[]{:S(2)}) collective-permute-start(bf16[160,1280]{1,0:T(8,128)(2,1)S(1)} %join.10.refs_11_), channel_id=1, source_target_pairs={{0,1},{1,0},{2,3},{3,2},{4,5},{5,4},{6,7},{7,6},{8,9},{9,8},{10,11... | collective-permute-start | bytes 1228808 | tf_op jit(solution)/shard_map/ppermute | solution.py:389

commit v8 on v7

--- a/solution.py
+++ b/solution.py
@@ -96,7 +96,7 @@
     piece_refs, (whole_ref, *solved_refs) = refs[: -levels - 1], refs[-levels:]
     row_count = unit // 2
     place(pieces, piece_refs, whole_ref, row_count, 2 ** (levels - 1))
-    samples = solved_refs[0].shape[1]
+    samples = solved_refs[-1].shape[0]
     total = whole_ref.shape[0]
     below_ref, at = whole_ref, samples
     for height in range(1, levels):
@@ -104,7 +104,11 @@
         for group in range(total // span):
             rows = slice(group * span, (group + 1) * span)
             children = below_ref[rows, 0:samples]
-            solved_refs[height - 1][rows, :] = solve_forward(whole_ref, rows, at, span, samples, children)
+            solved = solve_forward(whole_ref, rows, at, span, samples, children)
+            if height < levels - 1:
+                solved_refs[height - 1][rows, :] = solved
+            else:
+                solved_refs[height - 1][:, rows] = solved.astype(jnp.float32).T.astype(jnp.bfloat16)
         below_ref = solved_refs[height - 1]
         at += 2 * span + 2 * samples
 
@@ -152,19 +156,17 @@
 def top_kernel(levels, unit, pieces, *refs):
     low_ref, sep_scale_ref, partner_ref, base_ref, edge_ref, inner_ref, scale_ref = refs[:7]
     solved_refs = refs[7 : 7 + levels - 1]
-    out_ref, sample_ref, whole_ref, child_ref, x_ref, sum_ref = refs[-6:]
-    piece_refs = refs[7 + levels - 1 : -6]
-    samples = partner_ref.shape[1]
+    out_ref, sample_ref, whole_ref, x_ref, sum_ref = refs[-5:]
+    piece_refs = refs[7 + levels - 1 : -5]
+    samples = partner_ref.shape[0]
     row_count = unit // 2
     leaf, section = lax.axis_index("leaf"), lax.axis_index("sec")
     place(pieces, piece_refs, whole_ref, row_count, 2**levels)
-    half = partner_ref.shape[0]
     upper = leaf >> (levels - 1) & 1
-    child_ref[pl.ds(pl.multiple_of(upper * half, half), half), :] = solved_refs[-1][...]
-    child_ref[pl.ds(pl.multiple_of((1 - upper) * half, half), half), :] = partner_ref[...]
+    mine, theirs = solved_refs[-1][...], partner_ref[...]
+    children = jnp.concatenate([jnp.where(upper == 1, theirs, mine), jnp.where(upper == 1, mine, theirs)], axis=1)
     top_span = 2**levels * unit
     across = (((1,), (1,)), ((), ()))
-    children = child_ref[...].astype(jnp.float32).T.astype(jnp.bfloat16)
     rhs = whole_ref[:, 2 * top_span : 2 * top_span + samples].astype(jnp.float32).T
     reduced = rhs - lax.dot_general(
         children, whole_ref[:, 0:top_span], across, preferred_element_type=jnp.float32
@@ -185,9 +187,9 @@
             low_at -= 2 * span + 2 * samples
             first = ((leaf & (2 ** (levels - 1) - 1)) >> height) * span
             source, at, rows = low_ref, low_at, pl.ds(pl.multiple_of(first, span), span)
-            own = solved_refs[height - 1][rows, :]
+            own = solved_refs[height - 1][...] if height == levels - 1 else solved_refs[height - 1][rows, :]
         noise = source[rows, at + 2 * span + samples : at + 2 * span + 2 * samples]
-        if height == levels:
+        if height >= levels - 1:
             summed = own.astype(jnp.float32) + noise.astype(jnp.float32).T
         else:
             summed = (own.astype(jnp.float32) + noise.astype(jnp.float32)).T
@@ -440,7 +442,8 @@
     low_whole, *solved = pl.pallas_call(
         functools.partial(low_kernel, levels, unit, places),
         out_shape=[jax.ShapeDtypeStruct((quad * unit, low_columns), jnp.bfloat16)]
-        + [jax.ShapeDtypeStruct((quad * unit, samples), jnp.bfloat16)] * (levels - 1),
+        + [jax.ShapeDtypeStruct((quad * unit, samples), jnp.bfloat16)] * (levels - 2)
+        + [jax.ShapeDtypeStruct((samples, quad * unit), jnp.bfloat16)],
         in_specs=[vmem] * len(arrays) + [pl.BlockSpec(memory_space=pl.ANY)],
         out_specs=[vmem] * levels,
         compiler_params=params(8),
@@ -474,7 +477,6 @@
         out_specs=(vmem, vmem),
         scratch_shapes=[
             pltpu.VMEM((span, top_columns), jnp.bfloat16),
-            pltpu.VMEM((span, samples), jnp.bfloat16),
             pltpu.VMEM((span, samples), jnp.float32),
             pltpu.VMEM((unit * 2, samples), jnp.float32),
         ],

time: 23.6 us -> 23.6 us (level)
  no operation moved by 1% of the time
where the time goes in v8:
time: 23.6 us; the launch traced here: 23.4 us
  starting transfers between devices  13.1 us (56%)
  Pallas kernels  6.29 us (27%)
  waiting for transfers between devices  2.54 us (11%)
  between operations  1.44 us (6%)
    ppermute x8, starting transfers between devices, to_chips(): return lax.ppermute(block, AXES, route)  12 us
    pallas_call x1, Pallas kernels, on_device(): pl.pallas_call(functools.partial(top_kernel, levels, unit, places), out_s...  2.45 us
    ppermute x8, waiting for transfers between devices, to_chips(): return lax.ppermute(block, AXES, route)  2.33 us
    pallas_call x1, Pallas kernels, on_device(): pl.pallas_call(functools.partial(leaf_kernel, row_count), out_shape=(jax....  1.71 us
    pallas_call x1, Pallas kernels, on_device(): pl.pallas_call(functools.partial(pack_kernel, levels), out_shape=(jax.Sha...  1.22 us
    ppermute x4, starting transfers between devices, swap(): return lax.ppermute(block, 'sec', [(0, 1), (1, 0)])  1.12 us
    pallas_call x1, Pallas kernels, on_device(): pl.pallas_call(functools.partial(low_kernel, levels, unit, places), out_s...  0.82 us
  transfers between devices with their start and end apart: 12, of which 5 were waited for; matrix products, arithmetic and copies ran while one was open for 0% of the time, Pallas kernels for 11%

profile of v8, /device:TPU:0, one launch (start us, length us, event | category | flops | bytes accessed | tf_op | source)
XLA Modules:
  0.0 23.4 jit_solution(15425839452025315465)
XLA Ops:
  0.6 0.0 copy-start.4
  1.3 1.2 %pack.1 = (bf16[32,1408]{1,0:T(8,128)(2,1)S(1)}, bf16[32,1280]{1,0:T(8,128)(2,1)S(1)}) custom-call(s32[1,1]{1,0:T(1,128)S(6)} %copy.12.blocks_ref, bf16[1024,1024]{1,0:T(8,128)(2,1)} %leaf_ref.1, bf16[1024,128]{1,0:T(8,128)(2,1)} %shift_ref.1, bf16[32,896]{1,0:T(8,128)(2,1)} %refs_2_.1, bf16[32,896]{1,0:T(8,128)(2,1)} %refs_3_.1, ...), custom_call_target="tpu_custom_call" | custom-call | tf_op jit(solution)/shard_map/pack/pallas_call | solution.py:369
  2.5 0.5 %collective-permute-start.5 = (bf16[32,1280]{1,0:T(8,128)(2,1)S(1)}, bf16[32,1280]{1,0:T(8,128)(2,1)S(1)}, u32[]{:S(2)}, u32[]{:S(2)}) collective-permute-start(bf16[32,1280]{1,0:T(8,128)(2,1)S(1)} %get-tuple-element.21.refs_0_.refs_1_.refs_9_), channel_id=1, source_target_pairs={{0,1},{1,0},{2,3},{3,2},{4,5},{5,4},{6,7},{7,6},{8,9},{9,8},{10,11... | collective-permute-start | bytes 245768 | tf_op jit(solution)/shard_map/ppermute | solution.py:391
  3.0 3.5 %collective-permute-start.2 = (bf16[32,1408]{1,0:T(8,128)(2,1)S(1)}, bf16[32,1408]{1,0:T(8,128)(2,1)S(1)}, u32[]{:S(2)}, u32[]{:S(2)}) collective-permute-start(bf16[32,1408]{1,0:T(8,128)(2,1)S(1)} %get-tuple-element.12.refs_0_), channel_id=1, source_target_pairs={{0,6},{1,7},{2,4},{3,5},{4,2},{5,3},{6,0},{7,1},{8,14},{9,15},{10,... | collective-permute-start | bytes 270344 | tf_op jit(solution)/shard_map/ppermute | solution.py:20
  6.6 0.5 %collective-permute-start.1 = (bf16[32,1408]{1,0:T(8,128)(2,1)S(1)}, bf16[32,1408]{1,0:T(8,128)(2,1)S(1)}, u32[]{:S(2)}, u32[]{:S(2)}) collective-permute-start(bf16[32,1408]{1,0:T(8,128)(2,1)S(1)} %get-tuple-element.12.refs_0_), channel_id=1, source_target_pairs={{0,4},{1,5},{2,6},{3,7},{4,0},{5,1},{6,2},{7,3},{8,12},{9,13},{10,... | collective-permute-start | bytes 270344 | tf_op jit(solution)/shard_map/ppermute | solution.py:20
  7.1 0.1 collective-permute-start
  7.2 0.0 copy-done.4
  7.2 0.0 copy-start
  7.2 0.0 copy-start.1
  7.2 0.0 copy-start.2
  7.2 0.0 copy-start.3
  7.3 0.0 collective-permute-done.5.refs_1_.refs_10_
  7.3 2.9 %collective-permute-start.10 = (bf16[64,1280]{1,0:T(8,128)(2,1)S(1)}, bf16[64,1280]{1,0:T(8,128)(2,1)S(1)}, u32[]{:S(2)}, u32[]{:S(2)}) collective-permute-start(bf16[64,1280]{1,0:T(8,128)(2,1)S(1)} %join.8.refs_0_), channel_id=1, source_target_pairs={{0,6},{1,5},{2,4},{3,7},{4,2},{5,1},{6,0},{7,3},{8,14},{9,13},{10,... | collective-permute-start | bytes 491528 | tf_op jit(solution)/shard_map/ppermute | solution.py:20
  10.2 1.5 %collective-permute-start.7 = (bf16[64,1280]{1,0:T(8,128)(2,1)S(1)}, bf16[64,1280]{1,0:T(8,128)(2,1)S(1)}, u32[]{:S(2)}, u32[]{:S(2)}) collective-permute-start(bf16[64,1280]{1,0:T(8,128)(2,1)S(1)} %join.8.refs_0_), channel_id=1, source_target_pairs={{0,12},{1,15},{2,14},{3,13},{4,8},{5,11},{6,10},{7,9},{8,4},{9,7},... | collective-permute-start | bytes 491528 | tf_op jit(solution)/shard_map/ppermute | solution.py:20
  11.7 0.0 collective-permute-done.2.refs_3_
  11.7 0.4 %collective-permute-start.6 = (bf16[64,1280]{1,0:T(8,128)(2,1)S(1)}, bf16[64,1280]{1,0:T(8,128)(2,1)S(1)}, u32[]{:S(2)}, u32[]{:S(2)}) collective-permute-start(bf16[64,1280]{1,0:T(8,128)(2,1)S(1)} %join.8.refs_0_), channel_id=1, source_target_pairs={{0,8},{1,11},{2,10},{3,9},{4,12},{5,15},{6,14},{7,13},{8,0},{9,3},... | collective-permute-start | bytes 491528 | tf_op jit(solution)/shard_map/ppermute | solution.py:20
  12.2 0.0 collective-permute-done.1.refs_2_
  12.2 1.3 %collective-permute-start.8 = (bf16[32,1280]{1,0:T(8,128)(2,1)S(1)}, bf16[32,1280]{1,0:T(8,128)(2,1)S(1)}, u32[]{:S(2)}, u32[]{:S(2)}) collective-permute-start(bf16[32,1280]{1,0:T(8,128)(2,1)S(1)} %join.9), channel_id=1, source_target_pairs={{0,2},{1,3},{2,0},{3,1},{4,6},{5,7},{6,4},{7,5},{8,10},{9,11},{10,... | collective-permute-start | bytes 245768 | tf_op jit(solution)/shard_map/ppermute | solution.py:20
  13.5 0.0 collective-permute-done.refs_1_
  13.5 0.1 collective-permute-start.3
  13.6 0.0 copy-done
  13.6 0.0 copy-done.1
  13.6 0.0 copy-done.2
  13.6 0.0 copy-done.3
  13.6 1.7 %leaf.1 = (f32[1024,128]{1,0:T(8,128)S(1)}, f32[32,128]{1,0:T(8,128)S(1)}, bf16[1024,32]{1,0:T(8,128)(2,1)S(1)}, f32[1024,128]{1,0:T(8,128)S(1)}, f32[3,32,128]{2,1,0:T(8,128)S(1)}) custom-call(s32[1,1]{1,0:T(1,128)S(6)} %copy.12.blocks_ref, bf16[1024,1024]{1,0:T(8,128)(2,1)S(1)} %copy-done, bf16[1024,128]{1,0:T(8,128)(2,1)S(1)} %copy-done.1, ...), custom_call_target="tpu_custom_call" | custom-call | flops 10000000000 | bytes 1 | tf_op jit(solution)/shard_map/leaf/pallas_call | solution.py:425
  15.4 0.0 collective-permute-done.3.refs_1_
  15.4 0.8 %low.1 = (bf16[256,1408]{1,0:T(8,128)(2,1)S(1)}, bf16[256,128]{1,0:T(8,128)(2,1)S(1)}, bf16[128,256]{1,0:T(8,128)(2,1)S(1)}) custom-call(bf16[128,1408]{1,0:T(8,128)(2,1)S(1)} %join.6.refs_0_, bf16[128,1408]{1,0:T(8,128)(2,1)S(1)} %collective-permute-done.3.refs_1_, f32[32,128]{1,0:T(8,128)S(1)} %get-tuple-element.13.refs_2_.refs_1_), custom_call_target="tpu_custom_call" | custom-call | tf_op jit(solution)/shard_map/low/pallas_call | solution.py:442
  16.2 1.6 %collective-permute-start.4 = (bf16[128,256]{1,0:T(8,128)(2,1)S(1)}, bf16[128,256]{1,0:T(8,128)(2,1)S(1)}, u32[]{:S(2)}, u32[]{:S(2)}) collective-permute-start(bf16[128,256]{1,0:T(8,128)(2,1)S(1)} %get-tuple-element.16.refs_0_.refs_8_), channel_id=1, source_target_pairs={{0,8},{1,9},{2,10},{3,11},{4,12},{5,13},{6,14},{7,15},{8,0},{9,1},... | collective-permute-start | bytes 196616 | tf_op jit(solution)/shard_map/ppermute | solution.py:20
  17.8 0.6 %collective-permute-done.10.refs_1_ = bf16[64,1280]{1,0:T(8,128)(2,1)S(1)} collective-permute-done((bf16[64,1280]{1,0:T(8,128)(2,1)S(1)}, bf16[64,1280]{1,0:T(8,128)(2,1)S(1)}, u32[]{:S(2)}, u32[]{:S(2)}) %collective-permute-start.10) | collective-permute-done | bytes 163872 | tf_op jit(solution)/shard_map/ppermute | solution.py:20
  18.5 0.5 %collective-permute-start.11 = (bf16[64,1280]{1,0:T(8,128)(2,1)S(1)}, bf16[64,1280]{1,0:T(8,128)(2,1)S(1)}, u32[]{:S(2)}, u32[]{:S(2)}) collective-permute-start(bf16[64,1280]{1,0:T(8,128)(2,1)S(1)} %join.11.refs_13_), channel_id=1, source_target_pairs={{0,1},{1,0},{2,3},{3,2},{4,5},{5,4},{6,7},{7,6},{8,9},{9,8},{10,11... | collective-permute-start | bytes 491528 | tf_op jit(solution)/shard_map/ppermute | solution.py:391
  18.9 0.1 collective-permute-done.8.refs_3_
  19.0 0.0 collective-permute-done.7.refs_2_
  19.0 0.1 collective-permute-done.6.refs_1_
  19.1 0.1 collective-permute-start.9
  19.2 1.5 %collective-permute-done.4.refs_0_.refs_2_ = bf16[128,256]{1,0:T(8,128)(2,1)S(1)} collective-permute-done((bf16[128,256]{1,0:T(8,128)(2,1)S(1)}, bf16[128,256]{1,0:T(8,128)(2,1)S(1)}, u32[]{:S(2)}, u32[]{:S(2)}) %collective-permute-start.4) | collective-permute-done | bytes 65568 | tf_op jit(solution)/shard_map/ppermute | solution.py:20
  20.7 0.0 collective-permute-done.11.refs_14_
  20.7 0.2 collective-permute-done.9.refs_12_
  20.9 2.4 %top.1 = (bf16[1024,128]{1,0:T(8,128)(2,1)}, bf16[3,32,128]{2,1,0:T(8,128)(2,1)}) custom-call(bf16[256,1408]{1,0:T(8,128)(2,1)S(1)} %get-tuple-element.14.refs_0_, f32[3,32,128]{2,1,0:T(8,128)S(1)} %get-tuple-element.15.refs_1_, bf16[128,256]{1,0:T(8,128)(2,1)S(1)} %collective-permute-done.4.refs_0_.refs_2_, f32[1024,128]{1,0:T(8,128)S(1)} %get-tuple-element.17.refs_3_, ...), custom_call_target="tpu_custom_call" | custom-call | tf_op jit(solution)/shard_map/top/pallas_call | solution.py:470
  (7 shorter events, 0.1 us)
Async XLA Ops:
  0.6 6.6 %copy-start.4 = (bf16[1024]{0:T(1024)(128)(2,1)S(1)}, bf16[1024]{0:T(1024)(128)(2,1)}, u32[]{:S(2)}) copy-start(bf16[1024]{0:T(1024)(128)(2,1)} %param.14) | copy-start | bytes 6148
  2.5 4.7 %collective-permute-start.5 = (bf16[32,1280]{1,0:T(8,128)(2,1)S(1)}, bf16[32,1280]{1,0:T(8,128)(2,1)S(1)}, u32[]{:S(2)}, u32[]{:S(2)}) collective-permute-start(bf16[32,1280]{1,0:T(8,128)(2,1)S(1)} %get-tuple-element.21.refs_0_.refs_1_.refs_9_), channel_id=1, source_target_pairs={{0,1},{1,0},{2,3},{3,2},{4,5},{5,4},{6,7},{7,6},{8,9},{9,8},{10,11... | collective-permute-start | bytes 245768 | tf_op jit(solution)/shard_map/ppermute | solution.py:391
  3.0 8.7 %collective-permute-start.2 = (bf16[32,1408]{1,0:T(8,128)(2,1)S(1)}, bf16[32,1408]{1,0:T(8,128)(2,1)S(1)}, u32[]{:S(2)}, u32[]{:S(2)}) collective-permute-start(bf16[32,1408]{1,0:T(8,128)(2,1)S(1)} %get-tuple-element.12.refs_0_), channel_id=1, source_target_pairs={{0,6},{1,7},{2,4},{3,5},{4,2},{5,3},{6,0},{7,1},{8,14},{9,15},{10,... | collective-permute-start | bytes 270344 | tf_op jit(solution)/shard_map/ppermute | solution.py:20
  6.6 5.6 %collective-permute-start.1 = (bf16[32,1408]{1,0:T(8,128)(2,1)S(1)}, bf16[32,1408]{1,0:T(8,128)(2,1)S(1)}, u32[]{:S(2)}, u32[]{:S(2)}) collective-permute-start(bf16[32,1408]{1,0:T(8,128)(2,1)S(1)} %get-tuple-element.12.refs_0_), channel_id=1, source_target_pairs={{0,4},{1,5},{2,6},{3,7},{4,0},{5,1},{6,2},{7,3},{8,12},{9,13},{10,... | collective-permute-start | bytes 270344 | tf_op jit(solution)/shard_map/ppermute | solution.py:20
  7.1 6.4 %collective-permute-start = (bf16[32,1408]{1,0:T(8,128)(2,1)S(1)}, bf16[32,1408]{1,0:T(8,128)(2,1)S(1)}, u32[]{:S(2)}, u32[]{:S(2)}) collective-permute-start(bf16[32,1408]{1,0:T(8,128)(2,1)S(1)} %get-tuple-element.12.refs_0_), channel_id=1, source_target_pairs={{0,2},{1,3},{2,0},{3,1},{4,6},{5,7},{6,4},{7,5},{8,10},{9,11},{10,... | collective-permute-start | bytes 270344 | tf_op jit(solution)/shard_map/ppermute | solution.py:20
  7.2 6.4 %copy-start = (bf16[1024,1024]{1,0:T(8,128)(2,1)S(1)}, bf16[1024,1024]{1,0:T(8,128)(2,1)}, u32[]{:S(2)}) copy-start(bf16[1024,1024]{1,0:T(8,128)(2,1)} %leaf_ref.1) | copy-start | bytes 6291460
  7.2 6.4 %copy-start.1 = (bf16[1024,128]{1,0:T(8,128)(2,1)S(1)}, bf16[1024,128]{1,0:T(8,128)(2,1)}, u32[]{:S(2)}) copy-start(bf16[1024,128]{1,0:T(8,128)(2,1)} %shift_ref.1) | copy-start | bytes 786436
  7.2 6.4 %copy-start.2 = (bf16[1024,128]{1,0:T(8,128)(2,1)S(1)}, bf16[1024,128]{1,0:T(8,128)(2,1)}, u32[]{:S(2)}) copy-start(bf16[1024,128]{1,0:T(8,128)(2,1)} %noise_ref.1) | copy-start | bytes 786436
  7.2 6.4 %copy-start.3 = (bf16[3,32]{1,0:T(4,128)(2,1)S(1)}, bf16[3,32]{1,0:T(4,128)(2,1)}, u32[]{:S(2)}) copy-start(bf16[3,32]{1,0:T(4,128)(2,1)} %sep_dev_ref.1) | copy-start | bytes 580
  7.3 11.1 %collective-permute-start.10 = (bf16[64,1280]{1,0:T(8,128)(2,1)S(1)}, bf16[64,1280]{1,0:T(8,128)(2,1)S(1)}, u32[]{:S(2)}, u32[]{:S(2)}) collective-permute-start(bf16[64,1280]{1,0:T(8,128)(2,1)S(1)} %join.8.refs_0_), channel_id=1, source_target_pairs={{0,6},{1,5},{2,4},{3,7},{4,2},{5,1},{6,0},{7,3},{8,14},{9,13},{10,... | collective-permute-start | bytes 491528 | tf_op jit(solution)/shard_map/ppermute | solution.py:20
  10.2 8.8 %collective-permute-start.7 = (bf16[64,1280]{1,0:T(8,128)(2,1)S(1)}, bf16[64,1280]{1,0:T(8,128)(2,1)S(1)}, u32[]{:S(2)}, u32[]{:S(2)}) collective-permute-start(bf16[64,1280]{1,0:T(8,128)(2,1)S(1)} %join.8.refs_0_), channel_id=1, source_target_pairs={{0,12},{1,15},{2,14},{3,13},{4,8},{5,11},{6,10},{7,9},{8,4},{9,7},... | collective-permute-start | bytes 491528 | tf_op jit(solution)/shard_map/ppermute | solution.py:20
  11.7 7.4 %collective-permute-start.6 = (bf16[64,1280]{1,0:T(8,128)(2,1)S(1)}, bf16[64,1280]{1,0:T(8,128)(2,1)S(1)}, u32[]{:S(2)}, u32[]{:S(2)}) collective-permute-start(bf16[64,1280]{1,0:T(8,128)(2,1)S(1)} %join.8.refs_0_), channel_id=1, source_target_pairs={{0,8},{1,11},{2,10},{3,9},{4,12},{5,15},{6,14},{7,13},{8,0},{9,3},... | collective-permute-start | bytes 491528 | tf_op jit(solution)/shard_map/ppermute | solution.py:20
  12.2 6.8 %collective-permute-start.8 = (bf16[32,1280]{1,0:T(8,128)(2,1)S(1)}, bf16[32,1280]{1,0:T(8,128)(2,1)S(1)}, u32[]{:S(2)}, u32[]{:S(2)}) collective-permute-start(bf16[32,1280]{1,0:T(8,128)(2,1)S(1)} %join.9), channel_id=1, source_target_pairs={{0,2},{1,3},{2,0},{3,1},{4,6},{5,7},{6,4},{7,5},{8,10},{9,11},{10,... | collective-permute-start | bytes 245768 | tf_op jit(solution)/shard_map/ppermute | solution.py:20
  13.5 1.8 %collective-permute-start.3 = (bf16[128,1408]{1,0:T(8,128)(2,1)S(1)}, bf16[128,1408]{1,0:T(8,128)(2,1)S(1)}, u32[]{:S(2)}, u32[]{:S(2)}) collective-permute-start(bf16[128,1408]{1,0:T(8,128)(2,1)S(1)} %join.6.refs_0_), channel_id=1, source_target_pairs={{0,1},{1,0},{2,3},{3,2},{4,5},{5,4},{6,7},{7,6},{8,9},{9,8},{10,11... | collective-permute-start | bytes 1081352 | tf_op jit(solution)/shard_map/ppermute | solution.py:391
  16.2 4.5 %collective-permute-start.4 = (bf16[128,256]{1,0:T(8,128)(2,1)S(1)}, bf16[128,256]{1,0:T(8,128)(2,1)S(1)}, u32[]{:S(2)}, u32[]{:S(2)}) collective-permute-start(bf16[128,256]{1,0:T(8,128)(2,1)S(1)} %get-tuple-element.16.refs_0_.refs_8_), channel_id=1, source_target_pairs={{0,8},{1,9},{2,10},{3,11},{4,12},{5,13},{6,14},{7,15},{8,0},{9,1},... | collective-permute-start | bytes 196616 | tf_op jit(solution)/shard_map/ppermute | solution.py:20
  18.5 2.3 %collective-permute-start.11 = (bf16[64,1280]{1,0:T(8,128)(2,1)S(1)}, bf16[64,1280]{1,0:T(8,128)(2,1)S(1)}, u32[]{:S(2)}, u32[]{:S(2)}) collective-permute-start(bf16[64,1280]{1,0:T(8,128)(2,1)S(1)} %join.11.refs_13_), channel_id=1, source_target_pairs={{0,1},{1,0},{2,3},{3,2},{4,5},{5,4},{6,7},{7,6},{8,9},{9,8},{10,11... | collective-permute-start | bytes 491528 | tf_op jit(solution)/shard_map/ppermute | solution.py:391
  19.1 1.8 %collective-permute-start.9 = (bf16[160,1280]{1,0:T(8,128)(2,1)S(1)}, bf16[160,1280]{1,0:T(8,128)(2,1)S(1)}, u32[]{:S(2)}, u32[]{:S(2)}) collective-permute-start(bf16[160,1280]{1,0:T(8,128)(2,1)S(1)} %join.10.refs_11_), channel_id=1, source_target_pairs={{0,1},{1,0},{2,3},{3,2},{4,5},{5,4},{6,7},{7,6},{8,9},{9,8},{10,11... | collective-permute-start | bytes 1228808 | tf_op jit(solution)/shard_map/ppermute | solution.py:391
